TPU v7x, 32 devices: a whole 2x2x4 slice. The times are simulated.
32 devices in a mesh: gx: 4 (over y, x), gy: 4 (over z), gz: 2 (over core).
Axes of the slice: x: 2, y: 2, z: 4, core: 2. Of those that a mesh axis runs over, the one named last changes fastest.
Arguments:
- point_feats: bfloat16 [32, 262144], P(None, ('gx', 'gy', 'gz')), may hold values from -40 to 40
- voxel_ids: int32 [262144], P(('gx', 'gy', 'gz')), may hold values from 0 to 4095
- send_counts: int32 [32, 32], P(('gx', 'gy', 'gz')), may hold values from 0 to 256, as said below
- active: int32 [16, 16, 512], P('gx', 'gy', 'gz'), may hold values from 0 to 1
- w_sub: bfloat16 [64, 864], replicated, may hold values from -0.21875 to 0.21875
- w_down: bfloat16 [64, 512], replicated, may hold values from -0.25 to 0.25
- bn_gain: float32 [64], replicated, may hold values from 0.4 to 1.6
- bn_shift: float32 [64], replicated, may hold values from -2.5 to 2.5
- cotangent: bfloat16 [64, 8, 8, 256], P(None, 'gx', 'gy', 'gz'), may hold values from -6 to 6
Outputs:
- coarse_out: bfloat16 [64, 8, 8, 256], P(None, 'gx', 'gy', 'gz')
- grad_points: bfloat16 [32, 262144], P(None, ('gx', 'gy', 'gz'))
- grad_sub: float32 [64, 864], replicated
- grad_down: float32 [64, 512], replicated
- grad_gain: float32 [64], replicated
- grad_shift: float32 [64], replicated
Inputs may be any that keep to these rules, and one draw needn't show every extreme that they name: The slots for destination d are the 256 slots from d * 256 on; the first send_counts[src, d] of them hold points. Some destination device gets 256 points from every source device.
All inputs are finite; a program needn't handle non-finite values.
Results may differ from a plain program's by a relative error of at most 0.009.
Values may be sent and summed in bfloat16 or wider, within the bound.
No kernel may reach another device: no remote copies, remote signals or barrier semaphores. Data moves between devices by JAX's collectives and lax.ppermute only.
A program may use at most 192 MiB of HBM per device.

v0:
```python
import jax
import jax.numpy as jnp
from jax import lax
from jax.sharding import PartitionSpec as P

EPS = 1e-05


def padded_2(cells, sides, width):
    for axis, dim in sides:
        count = lax.axis_size(axis)
        ends = count - 1
        head = lax.slice_in_dim(cells, 0, width, axis=dim)
        tail = lax.slice_in_dim(cells, cells.shape[dim] - width, cells.shape[dim], axis=dim)
        cells = jnp.concatenate(
            [
                lax.ppermute(tail, axis, [(i, (i + 1) % count) for i in range(ends)]),
                cells,
                lax.ppermute(head, axis, [((i + 1) % count, i) for i in range(ends)]),
            ],
            axis=dim,
        )
    return cells


def columns(padded, start_x, start_y, size_x, size_y, size_z, starts_z):
    pieces = [
        padded[
            :, start_x : start_x + size_x, start_y : start_y + size_y, start_z : start_z + size_z
        ]
        for start_z in starts_z
    ]
    joined = jnp.concatenate(pieces, axis=0)
    return joined.reshape(joined.shape[0], size_x * size_y * size_z)


def on_device(
    point_feats, voxel_ids, send_counts, active, w_sub, w_down, bn_gain, bn_shift, cotangent
):
    in_chan, slot_total = point_feats.shape
    devices = send_counts.shape[1]
    slot_cap = slot_total // devices
    size_x, size_y, size_z = active.shape
    volume = size_x * size_y * size_z
    out_chan = w_sub.shape[0]
    slot_rank = jnp.arange(slot_cap, dtype=jnp.int32)
    usable = (slot_rank[None, :] < send_counts[0][:, None]).reshape(1, slot_total)
    outgoing = jnp.where(usable, point_feats, jnp.zeros_like(point_feats))
    voxel_tags = jnp.where(usable, voxel_ids.reshape(1, slot_total), -1)
    arriving, arrived_tags = (
        lax.all_to_all(outgoing, ("gx", "gy", "gz"), split_axis=1, concat_axis=1, tiled=True),
        lax.all_to_all(voxel_tags, ("gx", "gy", "gz"), split_axis=1, concat_axis=1, tiled=True),
    )
    landed = arrived_tags[0] >= 0
    target = jnp.where(landed, arrived_tags[0], 0)
    summed = jax.ops.segment_sum(arriving.T.astype(jnp.float32), target, num_segments=volume)
    activity = active.reshape(1, volume).astype(jnp.float32)
    grid_in = (summed.T * activity).astype(jnp.bfloat16).reshape(in_chan, size_x, size_y, size_z)
    padded = padded_2(grid_in, (("gx", 1), ("gy", 2), ("gz", 3)), 1)
    conv_sum = jnp.zeros((out_chan, volume), jnp.float32)
    for start_x in range(3):
        for start_y in range(3):
            first = (start_x * 3 + start_y) * 3 * in_chan
            stacked = columns(padded, start_x, start_y, size_x, size_y, size_z, (0, 1, 2))
            conv_sum = conv_sum + jnp.dot(
                w_sub[:, first : first + 3 * in_chan], stacked, preferred_element_type=jnp.float32
            )
    hidden = conv_sum * activity
    totals, active_count = lax.psum(
        (jnp.sum(hidden, axis=1), jnp.sum(activity)), ("gx", "gy", "gz")
    )
    average = totals / active_count
    centred = (hidden - average[:, None]) * activity
    spread = lax.psum(jnp.sum(centred * centred, axis=1), ("gx", "gy", "gz"))
    variance = spread / active_count
    inverse = lax.rsqrt(variance + EPS)
    normed = (hidden - average[:, None]) * inverse[:, None]
    pre_act = bn_gain[:, None] * normed + bn_shift[:, None]
    gelu_val, gelu_back = jax.vjp(jax.nn.gelu, pre_act)
    fine_out = (gelu_val * activity).astype(jnp.bfloat16)
    half_x, half_y, half_z = (size_x // 2, size_y // 2, size_z // 2)
    coarse_active = (
        active.reshape(half_x, 2, half_y, 2, half_z, 2).max(axis=(1, 3, 5)).reshape(1, -1)
    )
    fine_stack = (
        fine_out.reshape(out_chan, half_x, 2, half_y, 2, half_z, 2)
        .transpose(2, 4, 6, 0, 1, 3, 5)
        .reshape(8 * out_chan, -1)
    )
    coarse_sum = jnp.dot(
        w_down, fine_stack, preferred_element_type=jnp.float32
    ) * coarse_active.astype(jnp.float32)
    coarse_out = coarse_sum.astype(jnp.bfloat16).reshape(out_chan, half_x, half_y, half_z)
    grad_c = cotangent.reshape(out_chan, -1) * coarse_active.astype(jnp.bfloat16)
    local_down = lax.dot_general(
        grad_c, fine_stack, (((1,), (1,)), ((), ())), preferred_element_type=jnp.float32
    )
    grad_stack = jnp.dot(w_down.T, grad_c, preferred_element_type=jnp.float32)
    grad_fine = (
        grad_stack.reshape(2, 2, 2, out_chan, half_x, half_y, half_z)
        .transpose(3, 4, 0, 5, 1, 6, 2)
        .reshape(out_chan, volume)
    )
    grad_pre = gelu_back(grad_fine * activity)[0]
    raw_shift, raw_gain = lax.psum(
        (jnp.sum(grad_pre, axis=1), jnp.sum(grad_pre * normed, axis=1)), ("gx", "gy", "gz")
    )
    grad_hidden = (
        activity
        * (bn_gain * inverse)[:, None]
        * (grad_pre - (raw_shift[:, None] + normed * raw_gain[:, None]) / active_count)
    )
    grad_hidden = grad_hidden.astype(jnp.bfloat16)
    w_blocks = w_sub.reshape(out_chan, 27, in_chan)
    sub_parts = []
    tap_groups = []
    for start_x in range(3):
        for start_y in range(3):
            stacked = columns(padded, start_x, start_y, size_x, size_y, size_z, (0, 1, 2))
            sub_parts.append(
                lax.dot_general(
                    grad_hidden,
                    stacked,
                    (((1,), (1,)), ((), ())),
                    preferred_element_type=jnp.float32,
                )
            )
            group = (start_x * 3 + start_y) * 3
            tap_groups.append(
                w_blocks[:, group : group + 3, :].transpose(2, 1, 0).reshape(in_chan, 3 * out_chan)
            )
    local_sub = jnp.concatenate(sub_parts, axis=1)
    grad_cube = grad_hidden.reshape(out_chan, size_x, size_y, size_z)
    grad_padded = padded_2(grad_cube, (("gx", 1), ("gy", 2), ("gz", 3)), 1)
    back_sum = jnp.zeros((in_chan, volume), jnp.float32)
    for start_x in range(3):
        for start_y in range(3):
            shifted = columns(
                grad_padded, 2 - start_x, 2 - start_y, size_x, size_y, size_z, (2, 1, 0)
            )
            back_sum = back_sum + jnp.dot(
                tap_groups[start_x * 3 + start_y], shifted, preferred_element_type=jnp.float32
            )
    grad_grid = (back_sum * activity).astype(jnp.bfloat16)
    grad_slots = jnp.where(landed[None, :], grad_grid[:, target], jnp.zeros((), jnp.bfloat16))
    returned = lax.all_to_all(
        grad_slots, ("gx", "gy", "gz"), split_axis=1, concat_axis=1, tiled=True
    )
    raw_sub, raw_down = lax.psum((local_sub, local_down), ("gx", "gy", "gz"))
    grad_scale = lax.rsqrt(active_count)
    return (
        coarse_out,
        returned,
        raw_sub * grad_scale,
        raw_down * grad_scale,
        raw_gain * grad_scale,
        raw_shift * grad_scale,
    )


def solution(mesh):
    in_specs = (
        P(None, ("gx", "gy", "gz")),
        P(("gx", "gy", "gz")),
        P(("gx", "gy", "gz"), None),
        P("gx", "gy", "gz"),
        P(),
        P(),
        P(),
        P(),
        P(None, "gx", "gy", "gz"),
    )
    out_specs = (P(None, "gx", "gy", "gz"), P(None, ("gx", "gy", "gz")), P(), P(), P(), P())
    return jax.shard_map(
        on_device, mesh=mesh, in_specs=in_specs, out_specs=out_specs, check_vma=False
    )
```

profile of v0, /device:TPU:0, one launch (start us, length us, event | category | flops | bytes accessed | tf_op | source)
XLA Modules:
  0.0 630.0 jit_solution(11880198223628366143)
XLA Ops:
  9.4 7.3 %all-to-all-start = ((s32[1,32,256]{2,0,1:T(1,128)}), s32[1,32,256]{2,0,1:T(1,128)S(1)}, u32[]{:S(2)}, u32[]{:S(2)}) async-start(s32[1,32,256]{2,0,1:T(1,128)} %bitcast.1), calls=%async_computation | async-start | bytes 65536 | tf_op jit(solution)/shard_map/all_to_all | solution.py:52
  35.0 5.8 all-to-all-start.1
  40.9 16.3 %all-to-all-done.1 = bf16[32,32,256]{2,0,1:T(8,128)(2,1)S(1)} async-done(((bf16[32,32,256]{2,0,1:T(8,128)(2,1)}), bf16[32,32,256]{2,0,1:T(8,128)(2,1)S(1)}, u32[]{:S(2)}, u32[]{:S(2)}) %all-to-all-start.1) | async-done | bytes 524320 | tf_op jit(solution)/shard_map/all_to_all | solution.py:51
  57.4 2.7 copy.104
  60.2 53.4 %scatter_custom_fusion = f32[4096,32]{1,0:T(8,128)S(1)} fusion(s32[8192]{0:T(1024)S(1)} %bitcast.145, f32[8192,32]{1,0:T(8,128)} %copy.104, f32[]{:T(128)} %constant.13.clone.1), kind=kCustom, calls=%fused_computation.76 | custom fusion | flops 262144 | bytes 524800 | tf_op jit(solution)/shard_map/scatter-add | solution.py:56
  118.2 5.0 collective-permute-done.1
  123.5 3.0 collective-permute-start.2
  129.6 4.4 collective-permute-done.3
  142.4 3.9 fusion.74
  172.3 10.6 %reshape.256 = bf16[96,4096]{1,0:T(8,128)(2,1)} reshape(bf16[96,4,4,256]{3,2,1,0:T(4,128)(2,1)} %get-tuple-element.87) | data formatting | bytes 1572864 | tf_op jit(solution)/shard_map/reshape | solution.py:34
  189.7 39.4 %all-reduce.1 = (f32[64]{0:T(128)S(1)}, f32[]{:T(128)}) all-reduce(f32[64]{0:T(128)S(1)} %get-tuple-element.103, f32[]{:T(128)} %convert_reduce_fusion), channel_id=1, replica_groups=mesh['gx'=4,'gy'=4,'gz'=2] {'gx','gy','gz'}, use_global_device_ids=true, to_apply=%region_2.3 | all-reduce | flops 65 | bytes 520 | tf_op jit(solution)/shard_map/psum | solution.py:69
  230.1 40.8 %psum.51 = f32[64]{0:T(128)S(1)} all-reduce(f32[64]{0:T(128)S(1)} %multiply_reduce_fusion), channel_id=1, replica_groups=mesh['gx'=4,'gy'=4,'gz'=2] {'gx','gy','gz'}, use_global_device_ids=true, to_apply=%region_6.7 | all-reduce | flops 64 | bytes 512 | tf_op jit(solution)/shard_map/psum | solution.py:74
  271.5 3.6 fusion.68
  275.2 39.4 %all-reduce = (f32[64]{0:T(128)S(1)}, f32[64]{0:T(128)S(1)}) all-reduce(f32[64]{0:T(128)S(1)} %get-tuple-element.7, f32[64]{0:T(128)S(1)} %get-tuple-element.6), channel_id=1, replica_groups=mesh['gx'=4,'gy'=4,'gz'=2] {'gx','gy','gz'}, use_global_device_ids=true, to_apply=%region_11.12 | all-reduce | flops 128 | bytes 1024 | tf_op jit(solution)/shard_map/psum | solution.py:105
  327.7 4.8 collective-permute-start.6
  336.2 3.6 collective-permute-start.8
  342.9 4.4 collective-permute-done.9
  357.0 2.6 pad_maximum_fusion
  359.6 3.5 fusion.71
  373.3 2.9 reshape.287
  379.7 3.9 reshape.281
  390.7 3.9 reshape.278
  398.2 4.1 reshape.276
  405.9 3.9 reshape.271
  414.7 3.8 reshape.285
  418.5 3.8 copy.123
  422.4 3.8 reshape.274
  426.2 3.8 copy.134
  430.0 3.8 reshape.283
  445.6 29.2 %gather_fusion = bf16[8192,32]{1,0:T(8,128)(2,1)} fusion(bf16[32,4096]{0,1:T(8,128)(2,1)S(1)} %copy.141, s32[8192]{0:T(1024)S(1)} %copy-done.60), kind=kCustom, calls=%fused_computation | custom fusion | bytes 1081344 | tf_op jit(solution)/shard_map/gather | solution.py:145
  477.7 6.0 all-to-all-start.2
  487.5 131.1 %all-reduce.5.cloned.1.call-done = (f32[64,864]{1,0:T(8,128)}, f32[64,512]{1,0:T(8,128)}) async-done(((f32[64,864]{1,0:T(8,128)}, f32[64,512]{1,0:T(8,128)}), (f32[64,864]{1,0:T(8,128)}, f32[64,512]{1,0:T(8,128)})) %all-reduce.5.cloned.1.call-update) | async-done | bytes 352272 | tf_op jit(solution)/shard_map/psum | solution.py:149
  (342 shorter events, 154.9 us)
Async XLA Ops:
  7.2 22.8 %copy-start = (bf16[64,512]{1,0:T(8,128)(2,1)S(1)}, bf16[64,512]{1,0:T(8,128)(2,1)}, u32[]{:S(2)}) copy-start(bf16[64,512]{1,0:T(8,128)(2,1)} %param.14) | copy-start | bytes 196612
  8.0 19.6 %copy-start.49 = (bf16[32,8192]{1,0:T(8,128)(2,1)S(1)}, bf16[32,8192]{1,0:T(8,128)(2,1)}, u32[]{:S(2)}) copy-start(bf16[32,8192]{1,0:T(8,128)(2,1)} %param.9) | copy-start | bytes 1572868
  9.4 25.6 %all-to-all-start = ((s32[1,32,256]{2,0,1:T(1,128)}), s32[1,32,256]{2,0,1:T(1,128)S(1)}, u32[]{:S(2)}, u32[]{:S(2)}) async-start(s32[1,32,256]{2,0,1:T(1,128)} %bitcast.1), calls=%async_computation | async-start | bytes 65536 | tf_op jit(solution)/shard_map/all_to_all | solution.py:52
  35.0 22.2 %all-to-all-start.1 = ((bf16[32,32,256]{2,0,1:T(8,128)(2,1)}), bf16[32,32,256]{2,0,1:T(8,128)(2,1)S(1)}, u32[]{:S(2)}, u32[]{:S(2)}) async-start(bf16[32,32,256]{2,0,1:T(8,128)(2,1)} %bitcast.127), calls=%async_computation.1 | async-start | bytes 1048576 | tf_op jit(solution)/shard_map/all_to_all | solution.py:51
  114.2 15.5 %copy-start.21 = (bf16[32,4096]{1,0:T(8,128)(2,1)}, bf16[32,4096]{1,0:T(8,128)(2,1)S(1)}, u32[]{:S(2)}) copy-start(bf16[32,4096]{1,0:T(8,128)(2,1)S(1)} %fusion.47) | copy-start | bytes 786436
  114.4 3.6 collective-permute-start
  116.4 6.8 %collective-permute-start.1 = (bf16[32,1,4,256]{3,2,1,0:T(4,128)(2,1)S(1)}, bf16[32,1,4,256]{3,2,1,0:T(4,128)(2,1)S(1)}, u32[]{:S(2)}, u32[]{:S(2)}) collective-permute-start(bf16[32,1,4,256]{3,2,1,0:T(4,128)(2,1)S(1)} %get-tuple-element.88), channel_id=1, source_target_pairs={{8,0},{16,8},{24,16},{9,1},{17,9},{25,17},{10,2},{18,10},{26,18},{... | collective-permute-start | bytes 196616 | tf_op jit(solution)/shard_map/ppermute | solution.py:19
  118.0 11.6 %copy-start.53 = (bf16[32,1,4,256]{3,2,1,0:T(4,128)(2,1)}, bf16[32,1,4,256]{3,2,1,0:T(4,128)(2,1)S(1)}, u32[]{:S(2)}) copy-start(bf16[32,1,4,256]{3,2,1,0:T(4,128)(2,1)S(1)} %collective-permute-done) | copy-start | bytes 196612
  123.5 6.1 collective-permute-start.2
  126.5 7.6 %collective-permute-start.3 = (bf16[32,6,1,256]{3,2,1,0:T(2,128)(2,1)S(1)}, bf16[32,6,1,256]{3,2,1,0:T(2,128)(2,1)S(1)}, u32[]{:S(2)}, u32[]{:S(2)}) collective-permute-start(bf16[32,6,1,256]{3,2,1,0:T(2,128)(2,1)S(1)} %get-tuple-element.85), channel_id=1, source_target_pairs={{2,0},{4,2},{6,4},{3,1},{5,3},{7,5},{10,8},{12,10},{14,12},{11,9},... | collective-permute-start | bytes 294920 | tf_op jit(solution)/shard_map/ppermute | solution.py:19
  134.9 4.8 collective-permute-start.4
  136.2 3.6 collective-permute-start.5
  152.6 34.1 %copy-start.2 = (bf16[96,4096]{1,0:T(8,128)(2,1)}, bf16[96,4096]{1,0:T(8,128)(2,1)S(1)}, u32[]{:S(2)}) copy-start(bf16[96,4096]{1,0:T(8,128)(2,1)S(1)} %reshape.259) | copy-start | bytes 2359300
  155.1 30.1 %copy-start.4 = (bf16[96,4096]{1,0:T(8,128)(2,1)}, bf16[96,4096]{1,0:T(8,128)(2,1)S(1)}, u32[]{:S(2)}) copy-start(bf16[96,4096]{1,0:T(8,128)(2,1)S(1)} %reshape.258) | copy-start | bytes 2359300
  169.7 13.2 %copy-start.44 = (bf16[64,864]{1,0:T(8,128)(2,1)S(1)}, bf16[64,864]{1,0:T(8,128)(2,1)}, u32[]{:S(2)}) copy-start(bf16[64,864]{1,0:T(8,128)(2,1)} %param.13) | copy-start | bytes 331780
  189.3 81.6 %copy-start.80 = (f32[64]{0:T(128)S(1)}, f32[64]{0:T(128)}, u32[]{:S(2)}) copy-start(f32[64]{0:T(128)} %param.15) | copy-start | bytes 772
  189.3 82.2 %copy-start.85 = (f32[64]{0:T(128)S(1)}, f32[64]{0:T(128)}, u32[]{:S(2)}) copy-start(f32[64]{0:T(128)} %param.16) | copy-start | bytes 772
  326.4 9.1 %collective-permute-start.7 = (bf16[64,1,4,256]{3,0,2,1:T(8,128)(2,1)}, bf16[64,1,4,256]{3,0,2,1:T(8,128)(2,1)S(1)}, u32[]{:S(2)}, u32[]{:S(2)}) collective-permute-start(bf16[64,1,4,256]{3,0,2,1:T(8,128)(2,1)} %get-tuple-element.78), channel_id=1, source_target_pairs={{8,0},{16,8},{24,16},{9,1},{17,9},{25,17},{10,2},{18,10},{26,18},{... | collective-permute-start | bytes 393224 | tf_op jit(solution)/shard_map/ppermute | solution.py:19
  327.7 7.6 %collective-permute-start.6 = (bf16[64,1,4,256]{3,0,2,1:T(8,128)(2,1)}, bf16[64,1,4,256]{3,0,2,1:T(8,128)(2,1)S(1)}, u32[]{:S(2)}, u32[]{:S(2)}) collective-permute-start(bf16[64,1,4,256]{3,0,2,1:T(8,128)(2,1)} %get-tuple-element.79), channel_id=1, source_target_pairs={{0,8},{8,16},{16,24},{1,9},{9,17},{17,25},{2,10},{10,18},{18,26},{... | collective-permute-start | bytes 393224 | tf_op jit(solution)/shard_map/ppermute | solution.py:17
  336.2 6.7 %collective-permute-start.8 = (bf16[64,6,1,256]{3,0,2,1:T(8,128)(2,1)S(1)}, bf16[64,6,1,256]{3,0,2,1:T(8,128)(2,1)S(1)}, u32[]{:S(2)}, u32[]{:S(2)}) collective-permute-start(bf16[64,6,1,256]{3,0,2,1:T(8,128)(2,1)S(1)} %get-tuple-element.66), channel_id=1, source_target_pairs={{0,2},{2,4},{4,6},{1,3},{3,5},{5,7},{8,10},{10,12},{12,14},{9,11},... | collective-permute-start | bytes 589832 | tf_op jit(solution)/shard_map/ppermute | solution.py:17
  339.7 7.6 %collective-permute-start.9 = (bf16[64,6,1,256]{3,0,2,1:T(8,128)(2,1)S(1)}, bf16[64,6,1,256]{3,0,2,1:T(8,128)(2,1)S(1)}, u32[]{:S(2)}, u32[]{:S(2)}) collective-permute-start(bf16[64,6,1,256]{3,0,2,1:T(8,128)(2,1)S(1)} %get-tuple-element.67), channel_id=1, source_target_pairs={{2,0},{4,2},{6,4},{3,1},{5,3},{7,5},{10,8},{12,10},{14,12},{11,9},... | collective-permute-start | bytes 589832 | tf_op jit(solution)/shard_map/ppermute | solution.py:19
  350.4 5.5 collective-permute-start.11
  351.6 3.1 collective-permute-start.10
  477.6 7.9 %copy-start.61 = (f32[64,96]{1,0:T(8,128)S(1)}, f32[64,96]{1,0:T(8,128)}, u32[]{:S(2)}) copy-start(f32[64,96]{1,0:T(8,128)} %fusion.90) | copy-start | bytes 73732
  477.6 7.9 %copy-start.62 = (f32[64,96]{1,0:T(8,128)S(1)}, f32[64,96]{1,0:T(8,128)}, u32[]{:S(2)}) copy-start(f32[64,96]{1,0:T(8,128)} %fusion.89) | copy-start | bytes 73732
  477.6 7.9 %copy-start.63 = (f32[64,96]{1,0:T(8,128)S(1)}, f32[64,96]{1,0:T(8,128)}, u32[]{:S(2)}) copy-start(f32[64,96]{1,0:T(8,128)} %fusion.88) | copy-start | bytes 73732
  477.6 7.9 %copy-start.64 = (f32[64,96]{1,0:T(8,128)S(1)}, f32[64,96]{1,0:T(8,128)}, u32[]{:S(2)}) copy-start(f32[64,96]{1,0:T(8,128)} %fusion.87) | copy-start | bytes 73732
  477.6 7.9 %copy-start.65 = (f32[64,96]{1,0:T(8,128)S(1)}, f32[64,96]{1,0:T(8,128)}, u32[]{:S(2)}) copy-start(f32[64,96]{1,0:T(8,128)} %fusion.86) | copy-start | bytes 73732
  477.7 7.9 %copy-start.66 = (f32[64,96]{1,0:T(8,128)S(1)}, f32[64,96]{1,0:T(8,128)}, u32[]{:S(2)}) copy-start(f32[64,96]{1,0:T(8,128)} %fusion.85) | copy-start | bytes 73732
  477.7 144.2 %all-to-all-start.2 = ((bf16[32,32,256]{2,0,1:T(8,128)(2,1)}), bf16[32,32,256]{2,0,1:T(8,128)(2,1)S(1)}, u32[]{:S(2)}, u32[]{:S(2)}) async-start(bf16[32,32,256]{2,0,1:T(8,128)(2,1)} %broadcast_select_fusion), calls=%async_computation.2 | async-start | bytes 1048576 | tf_op jit(solution)/shard_map/all_to_all | solution.py:146
  483.7 134.9 %all-reduce.5.cloned.1.call-start = ((), (), s32[]{:S(2)}) async-start(), calls=%async_computation.3 | async-start | bytes 720896 | tf_op jit(solution)/shard_map/psum | solution.py:149
  483.8 138.9 %copy-start.1 = (bf16[64,512]{1,0:T(8,128)(2,1)S(1)}, bf16[64,512]{1,0:T(8,128)(2,1)}, u32[]{:S(2)}) copy-start(bf16[64,512]{1,0:T(8,128)(2,1)} %param.14) | copy-start | bytes 196612
  (70 other events, 208.2 us)
Sparse Core Ops, SparseCore 0:
  490.5 128.0 all-reduce.4
where the time goes:
time: 639 us; the launch traced here: 630 us
  waiting for transfers between devices  165 us (26%)
  local copies, waits for them, and re-layouts  162 us (25%)
  blocking collectives  120 us (19%)
  other arithmetic  103 us (16%)
  starting transfers between devices  42.4 us (7%)
  matrix products  22.1 us (3%)
  between operations  16.3 us (3%)
    psum x1, waiting for transfers between devices, on_device(): raw_sub, raw_down = lax.psum((local_sub, local_down), ('gx', 'gy', 'gz'))  131 us
    scatter-add x1, other arithmetic, on_device(): jax.ops.segment_sum(arriving.T.astype(jnp.float32), target, num_segments=...  53.4 us
    reshape x16, local copies, waits for them, and re-layouts, columns(): return joined.reshape(joined.shape[0], size_x * size_y * size_z)  51 us
    psum x1, blocking collectives, on_device(): spread = lax.psum(jnp.sum(centred * centred, axis=1), ('gx', 'gy', 'gz'))  40.8 us
    psum x1, blocking collectives, on_device(): lax.psum((jnp.sum(grad_pre, axis=1), jnp.sum(grad_pre * normed, axis=1)),...  39.4 us
    psum x1, blocking collectives, on_device(): lax.psum((jnp.sum(hidden, axis=1), jnp.sum(activity)), ('gx', 'gy', 'gz'))  39.4 us
    gather x2, local copies, waits for them, and re-layouts, on_device(): grad_grid[:, target]  31.1 us
    concatenate x12, local copies, waits for them, and re-layouts, columns(): joined = jnp.concatenate(pieces, axis=0)  28.2 us
  transfers between devices with their start and end apart: 16, of which 11 were waited for; matrix products, arithmetic and copies ran while one was open for 5% of the time, Pallas kernels for 0%

commit v1 on v0

v1 whole, which is shorter than its diff:
```python
import functools

import jax
import jax.numpy as jnp
from jax import lax
from jax.experimental import pallas as pl
from jax.experimental.pallas import tpu as pltpu
from jax.sharding import PartitionSpec as P

EPS = 1e-05
AXES = ("gx", "gy", "gz")
LANES = 128
GELU_SCALE = 0.7978845608028654
GELU_CUBE = 0.044715
F32 = jnp.float32
BF16 = jnp.bfloat16
NT = (((1,), (1,)), ((), ()))


def local_call(kernel, outs, *args, scratch=(), smem=(), limit=40, flops=0, moved=0):
    vmem = pl.BlockSpec(memory_space=pltpu.VMEM)
    scalar = pl.BlockSpec(memory_space=pltpu.SMEM)
    return pl.pallas_call(
        kernel,
        out_shape=[jax.ShapeDtypeStruct(shape, kind) for shape, kind in outs],
        in_specs=[scalar if i in smem else vmem for i in range(len(args))],
        out_specs=[vmem] * len(outs),
        scratch_shapes=[pltpu.VMEM(shape, kind) for shape, kind in scratch],
        compiler_params=pltpu.CompilerParams(vmem_limit_bytes=limit * 1024 * 1024),
        cost_estimate=pl.CostEstimate(
            flops=int(flops), bytes_accessed=int(moved), transcendentals=0
        ),
    )(*args)


def neighbours(axis, step):
    count = lax.axis_size(axis)
    return [(i, i + step) for i in range(count) if 0 <= i + step < count]


def exchange(low, high, axis):
    return (
        lax.ppermute(high, axis, neighbours(axis, 1)),
        lax.ppermute(low, axis, neighbours(axis, -1)),
    )


def z_exchange(low, high, swap):
    if lax.axis_size("gz") != 2:
        return exchange(low, high, "gz")
    got = lax.ppermute(swap, "gz", [(0, 1), (1, 0)])
    return got, got


def everyone(block):
    return lax.all_to_all(block, AXES, split_axis=0, concat_axis=0, tiled=True)


def pack_kernel(halves, groups, depth, counts_ref, feats_ref, ids_ref, out_ref):
    devices = out_ref.shape[0]
    chan = feats_ref.shape[0]
    rank = lax.broadcasted_iota(jnp.int32, (halves, LANES), 0) * LANES + lax.broadcasted_iota(
        jnp.int32, (halves, LANES), 1
    )
    blank = jnp.zeros((8 - 2 * halves, LANES), F32)
    for d in range(devices):
        for h in range(halves):
            first = (d * halves + h) * LANES
            out_ref[d, h * chan : (h + 1) * chan, :] = feats_ref[:, first : first + LANES]
        ids = ids_ref[d * halves : (d + 1) * halves, :]
        usable = rank < counts_ref[0, d]
        group = jnp.where(usable, ids // depth, groups).astype(F32)
        place = (ids % depth).astype(F32)
        tags = jnp.concatenate([group, place, blank], axis=0)
        out_ref[d, halves * chan :, :] = tags.astype(BF16)


def pack_plain(feats, ids, counts, groups, depth):
    chan, total = feats.shape
    devices = counts.shape[1]
    cap = total // devices
    ids = ids.reshape(devices, 1, cap)
    rank = jnp.arange(cap, dtype=jnp.int32)[None, None, :]
    group = jnp.where(rank < counts.reshape(devices, 1, 1), ids // depth, groups)
    tags = jnp.concatenate([group, ids % depth], axis=1).astype(BF16)
    rows = feats.reshape(chan, devices, cap).transpose(1, 0, 2)
    return jnp.concatenate([rows, jnp.pad(tags, ((0, 0), (0, 6), (0, 0)))], axis=1)


def scatter_kernel(halves, chan, size_y, recv_ref, act_ref, low_ref, high_ref, acc, masked, hot):
    chunks = recv_ref.shape[0]
    groups, depth = act_ref.shape
    per_step = masked.shape[1] // (halves * LANES)
    steps = chunks // per_step
    place = lax.broadcasted_iota(jnp.int32, (depth, LANES), 0).astype(F32)

    def step(s, carry):
        for j in range(per_step):
            block = recv_ref[s * per_step + j]
            tags = block[halves * chan :, :].astype(F32)
            for h in range(halves):
                feats = block[h * chan : (h + 1) * chan, :]
                col = (j * halves + h) * LANES
                group = jnp.broadcast_to(tags[h : h + 1, :], (chan, LANES)).astype(BF16)
                for k in range(groups):
                    masked[k * chan : (k + 1) * chan, col : col + LANES] = jnp.where(
                        group == k, feats, jnp.zeros_like(feats)
                    )
                low = tags[halves + h : halves + h + 1, :]
                hot[:, col : col + LANES] = jnp.where(place == low, 1.0, 0.0).astype(BF16)
        part = lax.dot_general(masked[...], hot[...], NT, preferred_element_type=F32)

        @pl.when(s == 0)
        def _():
            acc[...] = part

        @pl.when(s > 0)
        def _():
            acc[...] += part

        return carry

    lax.fori_loop(0, steps, step, 0)
    half = size_y // 2
    for k in range(groups):
        p, q = k // size_y, k % size_y
        out_ref = low_ref if p < 2 else high_ref
        row = ((q // half) * 4 + (p % 2) * 2 + q % half) * chan
        out_ref[row : row + chan, :] = (
            acc[k * chan : (k + 1) * chan, :] * act_ref[k : k + 1, :]
        ).astype(BF16)


def coarse_kernel(act_ref, cot_ref, low_ref, high_ref, grad_ref, mask_ref):
    depth = act_ref.shape[1]
    chan = cot_ref.shape[2]
    fine = lax.broadcasted_iota(jnp.int32, (depth, LANES), 0) // 2
    pair = (fine == lax.broadcasted_iota(jnp.int32, (depth, LANES), 1)).astype(BF16)
    acts = act_ref[...]
    sums = jnp.dot(acts.astype(BF16), pair, preferred_element_type=F32)
    masks = []
    for x in range(2):
        for y in range(2):
            rows = [sums[(2 * x + a) * 4 + 2 * y + b] for a in range(2) for b in range(2)]
            any_row = (rows[0] + rows[1] + rows[2] + rows[3])[None, :]
            mask = jnp.where(any_row > 0.5, 1.0, 0.0)
            masks.append(mask)
            grad = (cot_ref[x, y].astype(F32) * mask).astype(BF16)
            first = (x * 2 + y) * chan
            grad_ref[first : first + chan, :] = grad
            out_ref = low_ref if x == 0 else high_ref
            out_ref[y * chan : (y + 1) * chan, :] = grad
    mask_ref[...] = jnp.concatenate(masks + [jnp.zeros((4, LANES), F32)], axis=0)
    blank = jnp.zeros((8, LANES), F32)
    for out_ref, p in ((low_ref, 0), (high_ref, 3)):
        rows = acts[4 * p : 4 * p + 4]
        tail = jnp.concatenate([rows[:, :LANES], rows[:, LANES:], blank], axis=0)
        out_ref[2 * chan :, :] = tail.astype(BF16)


def coarse_rows_kernel(act_ref, grad_ref, before_ref, after_ref, low_ref, high_ref):
    chan = grad_ref.shape[0] // 4
    for out_ref, y, q in ((low_ref, 0, 0), (high_ref, 1, 3)):
        out_ref[0:chan, :] = before_ref[y * chan : (y + 1) * chan, :]
        out_ref[chan : 2 * chan, :] = grad_ref[y * chan : (y + 1) * chan, :]
        out_ref[2 * chan : 3 * chan, :] = grad_ref[(2 + y) * chan : (3 + y) * chan, :]
        out_ref[3 * chan : 4 * chan, :] = after_ref[y * chan : (y + 1) * chan, :]
        before = before_ref[2 * chan :, :].astype(F32)
        after = after_ref[2 * chan :, :].astype(F32)
        acts = act_ref[...]
        rows = [before[q : q + 1], before[4 + q : 5 + q]]
        for p in range(4):
            rows += [acts[4 * p + q : 4 * p + q + 1, :LANES], acts[4 * p + q : 4 * p + q + 1, LANES:]]
        rows += [after[q : q + 1], after[4 + q : 5 + q], jnp.zeros((4, LANES), F32)]
        out_ref[4 * chan :, :] = jnp.concatenate(rows, axis=0).astype(BF16)


def fine_grad_kernel(
    act_ref, grad_ref, xb_ref, xa_ref, yb_ref, ya_ref, down_ref, fine_ref, acts_ref, up
):
    chan = grad_ref.shape[0] // 4
    depth = act_ref.shape[1]
    acts = act_ref[...]
    xb = xb_ref[2 * chan :, :].astype(F32)
    xa = xa_ref[2 * chan :, :].astype(F32)
    yb = yb_ref[4 * chan :, :].astype(F32)
    ya = ya_ref[4 * chan :, :].astype(F32)
    rows = []
    for p in range(6):
        rows.append(jnp.concatenate([yb[2 * p : 2 * p + 1], yb[2 * p + 1 : 2 * p + 2]], axis=1))
        for q in range(4):
            if p in (0, 5):
                got = xb if p == 0 else xa
                rows.append(jnp.concatenate([got[q : q + 1], got[4 + q : 5 + q]], axis=1))
            else:
                rows.append(acts[4 * (p - 1) + q : 4 * (p - 1) + q + 1])
        rows.append(jnp.concatenate([ya[2 * p : 2 * p + 1], ya[2 * p + 1 : 2 * p + 2]], axis=1))
    rows.append(jnp.zeros((4, depth), F32))
    acts_ref[...] = jnp.concatenate(rows, axis=0)
    coarse = lax.broadcasted_iota(jnp.int32, (LANES, depth), 0)
    fine = lax.broadcasted_iota(jnp.int32, (LANES, depth), 1)
    spread = [(2 * coarse + c == fine).astype(BF16) for c in range(2)]
    for x in range(4):
        for y in range(4):
            if y in (0, 3):
                got = yb_ref if y == 0 else ya_ref
                block = got[x * chan : (x + 1) * chan, :]
            elif x in (0, 3):
                got = xb_ref if x == 0 else xa_ref
                block = got[(y - 1) * chan : y * chan, :]
            else:
                first = ((x - 1) * 2 + y - 1) * chan
                block = grad_ref[first : first + chan, :]
            for c in range(2):
                up[c * chan : (c + 1) * chan, :] = jnp.dot(
                    block, spread[c], preferred_element_type=F32
                ).astype(BF16)
            for a in range(2):
                p = 2 * x + a - 1
                for b in range(2):
                    q = 2 * y + b - 1
                    if 0 <= p < 6 and 0 <= q < 6:
                        first = (a * 2 + b) * chan
                        row = (p * 6 + q) * chan
                        fine_ref[row : row + chan, :] = jnp.dot(
                            down_ref[first : first + chan, :], up[...], preferred_element_type=F32
                        )


def bands_kernel(front_ref, back_ref, bands_ref, back_bands_ref):
    rows, width = front_ref.shape[0], front_ref.shape[1] // 9
    back_rows, back_width = back_ref.shape[0], back_ref.shape[1] // 9
    for t in range(9):
        block = front_ref[:, t * width : (t + 1) * width].astype(F32)
        for q in range(6):
            moved = pltpu.roll(block, q * back_rows, 1) if q else block
            bands_ref[q * rows : (q + 1) * rows, t * width : (t + 1) * width] = moved.astype(BF16)
        block = back_ref[:, t * back_width : (t + 1) * back_width].astype(F32)
        for q in range(4):
            moved = pltpu.roll(block, q * rows, 1) if q else block
            back_bands_ref[
                q * back_rows : (q + 1) * back_rows, t * back_width : (t + 1) * back_width
            ] = moved.astype(BF16)


def band_inputs(w_sub, in_chan):
    out_chan = w_sub.shape[0]
    taps = w_sub.reshape(out_chan, 3, 3, 3, in_chan)
    front = taps.transpose(0, 1, 3, 2, 4).reshape(out_chan, 9, 3 * in_chan)
    front = jnp.pad(front, ((0, 0), (0, 0), (0, 5 * in_chan)))
    back = taps[:, ::-1, ::-1].transpose(4, 1, 3, 2, 0).reshape(in_chan, 9, 3 * out_chan)
    back = jnp.pad(back, ((0, 0), (0, 0), (0, 3 * out_chan)))
    return front.reshape(out_chan, -1), back.reshape(in_chan, -1)


def rows_kernel(b_ref, low_ref, high_ref, a_ref, out_low_ref, out_high_ref):
    half = b_ref.shape[0] // 2
    for n, ref in enumerate((b_ref, low_ref, high_ref, a_ref)):
        out_low_ref[n * half : (n + 1) * half, :] = ref[:half, :]
        out_high_ref[n * half : (n + 1) * half, :] = ref[half:, :]


def columns_kernel(
    chan, place_ref, b_ref, low_ref, high_ref, a_ref, yb_ref, ya_ref, front_ref, rear_ref, swap_ref
):
    for n, ref in enumerate((b_ref, low_ref, high_ref, a_ref)):
        for p in range(2):
            for y in range(8):
                if y in (0, 1, 6, 7):
                    got = yb_ref if y < 2 else ya_ref
                    row = (n * 4 + p * 2 + y % 2) * chan
                else:
                    got = ref
                    row = (((y - 2) // 2) * 4 + p * 2 + y % 2) * chan
                block = got[row : row + chan, :]
                to = ((n * 2 + p) * 8 + y) * chan
                front_ref[to : to + chan, :] = block[:, :LANES]
                rear_ref[to : to + chan, :] = block[:, LANES:]

    @pl.when(place_ref[0] == 0)
    def _():
        swap_ref[...] = rear_ref[...]

    @pl.when(place_ref[0] != 0)
    def _():
        swap_ref[...] = front_ref[...]


def shifted(low, high, before, after, step):
    lane = lax.broadcasted_iota(jnp.int32, low.shape, 1)
    if step > 0:
        turned = [pltpu.roll(tile.astype(F32), LANES - 1, 1) for tile in (low, high, after)]
        edge = lane == LANES - 1
        tiles = [jnp.where(edge, turned[1], turned[0]), jnp.where(edge, turned[2], turned[1])]
    else:
        turned = [pltpu.roll(tile.astype(F32), 1, 1) for tile in (before, low, high)]
        edge = lane == 0
        tiles = [jnp.where(edge, turned[0], turned[1]), jnp.where(edge, turned[1], turned[2])]
    return tiles[0].astype(BF16), tiles[1].astype(BF16)


def keep(tile, wanted):
    return jnp.where(wanted, tile, jnp.zeros_like(tile))


def to_rows(columns):
    lane = lax.broadcasted_iota(jnp.int32, (LANES, LANES), 1)
    wide = jnp.zeros((LANES, LANES), F32)
    for n, column in enumerate(columns):
        tall = jnp.concatenate([column, jnp.zeros((LANES - column.shape[0], 1), F32)], axis=0)
        wide = jnp.where(lane == n, tall, wide)
    return wide.T[:8, :]


def to_columns(rows, chan):
    wide = jnp.concatenate(rows + [jnp.zeros((LANES - len(rows), LANES), F32)], axis=0).T
    return [wide[:chan, n : n + 1] for n in range(len(rows))]


def conv_kernel(
    only_two, place_ref, low_ref, high_ref, before_ref, after_ref, bands_ref, acts_ref,
    hidden_ref, stack_ref, stats_ref,
):
    rows = low_ref.shape[0] // 8
    depth = acts_ref.shape[1]
    wide = bands_ref.shape[0]
    chan = wide // 6
    has_before = place_ref[0] != 0 if only_two else True
    has_after = place_ref[0] == 0 if only_two else True
    for x in range(8):
        own = slice(x * rows, (x + 1) * rows)
        low, high = low_ref[own, :], high_ref[own, :]
        before, after = before_ref[own, :], after_ref[own, :]
        if only_two:
            before, after = keep(before, has_before), keep(after, has_after)
        for n, step in enumerate((-1, 0, 1)):
            tiles = (low, high) if step == 0 else shifted(low, high, before, after, step)
            to = slice((x * 3 + n) * rows, (x * 3 + n + 1) * rows)
            stack_ref[to, :LANES] = tiles[0]
            stack_ref[to, LANES:] = tiles[1]
    total = jnp.zeros((chan, depth), F32)
    for p in range(6):
        first = p * 3 * rows
        out = jnp.dot(
            bands_ref[...], stack_ref[first : first + 9 * rows, :], preferred_element_type=F32
        )
        for q in range(6):
            block = out[q * chan : (q + 1) * chan] * acts_ref[p * 6 + q : p * 6 + q + 1, :]
            hidden_ref[p * wide + q * chan : p * wide + (q + 1) * chan, :] = block
            if 1 <= p <= 4 and 1 <= q <= 4:
                total = total + block
    count = jnp.zeros((1, depth), F32)
    for p in range(1, 5):
        for q in range(1, 5):
            count = count + acts_ref[p * 6 + q : p * 6 + q + 1, :]
    count = jnp.sum(count, axis=1, keepdims=True)
    total = jnp.sum(total, axis=1, keepdims=True)
    mean = total / jnp.maximum(count, 1.0)
    squares = jnp.zeros((chan, depth), F32)
    for p in range(1, 5):
        for q in range(1, 5):
            row = p * wide + q * chan
            centred = (hidden_ref[row : row + chan, :] - mean) * acts_ref[
                p * 6 + q : p * 6 + q + 1, :
            ]
            squares = squares + centred * centred
    squares = jnp.sum(squares, axis=1, keepdims=True)
    packed = to_rows([total, squares, jnp.broadcast_to(count, (chan, 1))])
    for d in range(stats_ref.shape[0]):
        stats_ref[d] = packed


def merged_stats(stats_ref):
    totals, squares, counts = stats_ref[:, 0, :], stats_ref[:, 1, :], stats_ref[:, 2, :]
    count = jnp.sum(counts, axis=0, keepdims=True)
    average = jnp.sum(totals, axis=0, keepdims=True) / count
    off = totals / jnp.maximum(counts, 1.0) - average
    spread = jnp.sum(squares + counts * off * off, axis=0, keepdims=True)
    return count, average, lax.rsqrt(spread / count + EPS)


def norm_kernel(
    stats_ref, gain_ref, shift_ref, hidden_ref, fine_ref, acts_ref, pre_ref, out_ref, sums_ref
):
    chan = gain_ref.shape[0]
    depth = acts_ref.shape[1]
    count, average, inverse = merged_stats(stats_ref)
    average, inverse = to_columns([average, inverse], chan)
    full = (chan, LANES)
    average, inverse = jnp.broadcast_to(average, full), jnp.broadcast_to(inverse, full)
    gain, shift = jnp.broadcast_to(gain_ref[...], full), jnp.broadcast_to(shift_ref[...], full)
    sum_shift = jnp.zeros((chan, LANES), F32)
    sum_gain = jnp.zeros((chan, LANES), F32)
    for p in range(6):
        for q in range(6):
            row = (p * 6 + q) * chan
            for half in range(depth // LANES):
                lanes = slice(half * LANES, (half + 1) * LANES)
                act = acts_ref[p * 6 + q : p * 6 + q + 1, lanes]
                normed = (hidden_ref[row : row + chan, lanes] - average) * inverse
                x = gain * normed + shift
                square = x * x
                bent = jnp.tanh(GELU_SCALE * (x + GELU_CUBE * (square * x)))
                cdf = 0.5 + 0.5 * bent
                slope = cdf + (0.5 * x) * (1.0 - bent * bent) * (
                    GELU_SCALE + (3.0 * GELU_CUBE * GELU_SCALE) * square
                )
                grad = (act * slope) * fine_ref[row : row + chan, lanes]
                pre_ref[row : row + chan, lanes] = grad
                if 1 <= p <= 4 and 1 <= q <= 4:
                    sum_shift = sum_shift + grad
                    sum_gain = sum_gain + grad * normed
                    to = ((p - 1) * 4 + q - 1) * chan
                    out_ref[to : to + chan, lanes] = (x * cdf * act).astype(BF16)
    sums = to_rows(
        [jnp.sum(sum_shift, axis=1, keepdims=True), jnp.sum(sum_gain, axis=1, keepdims=True)]
    )
    for d in range(sums_ref.shape[0]):
        sums_ref[d] = sums


def down_kernel(out_ref, grad_ref, mask_ref, down_ref, coarse_ref, raw_ref, stack):
    depth = out_ref.shape[1]
    chan = grad_ref.shape[0] // 4
    source = lax.broadcasted_iota(jnp.int32, (depth, depth), 0)
    target = lax.broadcasted_iota(jnp.int32, (depth, depth), 1)
    wanted = jnp.where(target < LANES, 2 * target, 2 * (target - LANES) + 1)
    sort = (source == wanted).astype(BF16)
    for x in range(2):
        for y in range(2):
            for a in range(2):
                for b in range(2):
                    row = ((2 * x + a) * 4 + 2 * y + b) * chan
                    parted = jnp.dot(
                        out_ref[row : row + chan, :], sort, preferred_element_type=F32
                    ).astype(BF16)
                    lanes = slice((x * 2 + y) * LANES, (x * 2 + y + 1) * LANES)
                    to = (a * 4 + b * 2) * chan
                    stack[to : to + chan, lanes] = parted[:, :LANES]
                    stack[to + chan : to + 2 * chan, lanes] = parted[:, LANES:]
    sums = jnp.dot(down_ref[...], stack[...], preferred_element_type=F32)
    for n in range(4):
        coarse_ref[n] = (sums[:, n * LANES : (n + 1) * LANES] * mask_ref[n : n + 1, :]).astype(
            BF16
        )
    grads = jnp.concatenate([grad_ref[n * chan : (n + 1) * chan, :] for n in range(4)], axis=1)
    raw = lax.dot_general(grads, stack[...], NT, preferred_element_type=F32)
    for n in range(4):
        raw_ref[n * chan : (n + 1) * chan, :] = raw[:, n * LANES : (n + 1) * LANES]


def hidden_grad_kernel(
    place_ref, stats_ref, sums_ref, gain_ref, hidden_ref, pre_ref, acts_ref,
    front_ref, rear_ref, swap_ref, small_ref,
):
    chan = gain_ref.shape[0]
    count, average, inverse = merged_stats(stats_ref)
    raw_shift = jnp.sum(sums_ref[:, 0, :], axis=0, keepdims=True)
    raw_gain = jnp.sum(sums_ref[:, 1, :], axis=0, keepdims=True)
    scale = lax.rsqrt(count)
    small_ref[...] = jnp.concatenate(
        [raw_shift * scale, raw_gain * scale, scale, jnp.zeros((5, LANES), F32)], axis=0
    )
    columns = to_columns([average, inverse, raw_shift / count, raw_gain / count], chan)
    average, inverse, mean_shift, mean_gain = [
        jnp.broadcast_to(column, (chan, LANES)) for column in columns
    ]
    weight = jnp.broadcast_to(gain_ref[...], (chan, LANES)) * inverse
    for n in range(36):
        row = n * chan
        for half, out_ref in enumerate((front_ref, rear_ref)):
            lanes = slice(half * LANES, (half + 1) * LANES)
            act = acts_ref[n : n + 1, lanes]
            normed = (hidden_ref[row : row + chan, lanes] - average) * inverse
            grad = pre_ref[row : row + chan, lanes] - (mean_shift + normed * mean_gain)
            out_ref[row : row + chan, :] = ((act * weight) * grad).astype(BF16)

    @pl.when(place_ref[0] == 0)
    def _():
        swap_ref[...] = rear_ref[...]

    @pl.when(place_ref[0] != 0)
    def _():
        swap_ref[...] = front_ref[...]


def weight_grad_kernel(in_chan, stack_ref, front_ref, rear_ref, raw_ref, out_ref, acc):
    chan = front_ref.shape[0] // 36
    rows = stack_ref.shape[0] // 8
    band = rows // 3
    for p in range(4):
        own = slice(((p + 1) * 6 + 1) * chan, ((p + 1) * 6 + 5) * chan)
        grads = jnp.concatenate([front_ref[own, :], rear_ref[own, :]], axis=1)
        for dx in range(3):
            first = (p + 1 + dx) * rows
            part = lax.dot_general(
                stack_ref[first : first + rows, :], grads, NT, preferred_element_type=F32
            )
            if p == 0:
                acc[dx] = part
            else:
                acc[dx] += part
    low = lax.broadcasted_iota(jnp.int32, (in_chan, LANES), 1) < chan
    for dx in range(3):
        for dy in range(3):
            for dz in range(3):
                blocks = []
                for q in range(4):
                    row = dz * band + (q + 1 + dy) * in_chan
                    lanes = slice((q // 2) * LANES, (q // 2 + 1) * LANES)
                    blocks.append(acc[dx, row : row + in_chan, lanes])
                both = jnp.where(low, blocks[0] + blocks[2], blocks[1] + blocks[3])
                folded = both + pltpu.roll(both, chan, 1)
                tap = (dx * 3 + dy) * 3 + dz
                if tap < 16:
                    out_ref[tap * in_chan : (tap + 1) * in_chan, :chan] = folded[:, :chan]
                else:
                    to = (tap - 16) * in_chan
                    out_ref[to : to + in_chan, chan:] = folded[:, chan:]
    out_ref[11 * in_chan : 16 * in_chan, chan:] = jnp.zeros((5 * in_chan, LANES - chan), F32)
    tail = 16 * in_chan
    out_ref[tail : tail + 4 * chan, :] = raw_ref[...]
    if tail + 4 * chan < out_ref.shape[0]:
        out_ref[tail + 4 * chan :, :] = jnp.zeros(
            (out_ref.shape[0] - tail - 4 * chan, LANES), F32
        )


def point_grad_kernel(
    only_two, halves, chan, place_ref, front_ref, rear_ref, before_ref, after_ref, bands_ref, act_ref,
    recv_ref, out_ref, stack, cells,
):
    rows = front_ref.shape[0] // 6
    groups, depth = act_ref.shape
    has_before = place_ref[0] != 0 if only_two else True
    has_after = place_ref[0] == 0 if only_two else True
    for x in range(6):
        own = slice(x * rows, (x + 1) * rows)
        low, high = front_ref[own, :], rear_ref[own, :]
        before, after = before_ref[own, :], after_ref[own, :]
        if only_two:
            before, after = keep(before, has_before), keep(after, has_after)
        for n, step in enumerate((1, 0, -1)):
            tiles = (low, high) if step == 0 else shifted(low, high, before, after, step)
            to = slice((x * 3 + n) * rows, (x * 3 + n + 1) * rows)
            stack[to, :LANES] = tiles[0]
            stack[to, LANES:] = tiles[1]
    for p in range(4):
        first = p * 3 * rows
        grid = jnp.dot(
            bands_ref[...], stack[first : first + 9 * rows, :], preferred_element_type=F32
        )
        for q in range(4):
            k = p * 4 + q
            cells[k * chan : (k + 1) * chan, :] = (
                grid[q * chan : (q + 1) * chan] * act_ref[k : k + 1, :]
            ).astype(BF16)
    place = lax.broadcasted_iota(jnp.int32, (depth, LANES), 0).astype(F32)

    def step(d, carry):
        tags = recv_ref[d][halves * chan :, :].astype(F32)
        for h in range(halves):
            group = jnp.broadcast_to(tags[h : h + 1, :], (chan, LANES))
            low = tags[halves + h : halves + h + 1, :]
            hot = jnp.where(place == low, 1.0, 0.0).astype(BF16)
            found = jnp.dot(cells[...], hot, preferred_element_type=F32)
            out = jnp.zeros((chan, LANES), F32)
            for k in range(groups):
                out = jnp.where(group == k, found[k * chan : (k + 1) * chan], out)
            out_ref[d, h * chan : (h + 1) * chan, :] = out.astype(BF16)
        return carry

    lax.fori_loop(0, recv_ref.shape[0], step, 0)


def piece_kernel(parts_ref, points_ref, out_ref):
    rows = points_ref.shape[1]
    piece = jnp.sum(parts_ref[...], axis=0).astype(BF16)
    for d in range(out_ref.shape[0]):
        out_ref[d, :rows, :] = points_ref[d]
        out_ref[d, rows:, :] = piece


def sum_kernel(parts_ref, out_ref):
    piece = jnp.sum(parts_ref[...], axis=0).astype(BF16)
    for d in range(out_ref.shape[0]):
        out_ref[d] = piece


def weights_out(rows, small_ref, in_chan, sub_ref, down_ref):
    chan = down_ref.shape[0]
    scale = small_ref[2:3, 0:1]
    for n in range(4):
        turned = rows(n).T * scale
        sub_ref[:, n * LANES : (n + 1) * LANES] = turned[:chan]
        left = sub_ref.shape[1] - 16 * in_chan - n * LANES
        if left > 0:
            width = min(left, LANES)
            first = 16 * in_chan + n * LANES
            sub_ref[:, first : first + width] = turned[chan:, :width]
    for n in range(2):
        both = rows(4 + n) * scale
        down_ref[:, 2 * n * LANES : (2 * n + 1) * LANES] = both[:chan]
        down_ref[:, (2 * n + 1) * LANES : (2 * n + 2) * LANES] = both[chan:]


def last_kernel(halves, chan, got_ref, small_ref, points_ref, sub_ref, down_ref, flat):
    devices = got_ref.shape[0]
    piece = got_ref.shape[1] - halves * chan
    for d in range(devices):
        block = got_ref[d]
        for h in range(halves):
            first = (d * halves + h) * LANES
            points_ref[:, first : first + LANES] = block[h * chan : (h + 1) * chan, :]
        flat[d * piece : (d + 1) * piece, :] = block[halves * chan :, :].astype(F32)
    weights_out(lambda n: flat[n * LANES : (n + 1) * LANES, :], small_ref, chan, sub_ref, down_ref)


def weights_kernel(chan, got_ref, small_ref, sub_ref, down_ref, flat):
    piece = got_ref.shape[1]
    for d in range(got_ref.shape[0]):
        flat[d * piece : (d + 1) * piece, :] = got_ref[d].astype(F32)
    weights_out(lambda n: flat[n * LANES : (n + 1) * LANES, :], small_ref, chan, sub_ref, down_ref)


def on_device(
    point_feats, voxel_ids, send_counts, active, w_sub, w_down, bn_gain, bn_shift, cotangent
):
    in_chan, slot_total = point_feats.shape
    devices = send_counts.shape[1]
    slot_cap = slot_total // devices
    size_x, size_y, size_z = active.shape
    groups = size_x * size_y
    out_chan = w_sub.shape[0]
    only_two = lax.axis_size("gz") == 2
    place = lax.axis_index("gz").astype(jnp.int32).reshape(1)
    aligned = slot_cap % LANES == 0
    halves = slot_cap // LANES if aligned else 1

    if aligned:
        payload = local_call(
            functools.partial(pack_kernel, halves, groups, size_z),
            [((devices, halves * in_chan + 8, LANES), BF16)],
            send_counts, point_feats, voxel_ids.reshape(-1, LANES),
            smem=(0,), moved=2e6,
        )[0]
        recv = everyone(payload)
    else:
        payload = pack_plain(point_feats, voxel_ids, send_counts, groups, size_z)
        together = LANES // slot_cap
        recv = everyone(payload)
        recv = recv.reshape(devices // together, together, in_chan + 8, slot_cap)
        recv = recv.transpose(0, 2, 1, 3).reshape(devices // together, in_chan + 8, LANES)
    chunks = recv.shape[0]

    acts = active.reshape(groups, size_z).astype(F32)
    front, back = band_inputs(w_sub, in_chan)
    wide, back_wide = 6 * out_chan, 4 * in_chan
    bands, back_bands = local_call(
        bands_kernel,
        [((wide, 9 * 8 * in_chan), BF16), ((back_wide, 9 * 6 * out_chan), BF16)],
        front, back, moved=4e6,
    )
    cot = cotangent.transpose(1, 2, 0, 3)
    cot_low, cot_high, grad_c, coarse_mask = local_call(
        coarse_kernel,
        [((2 * out_chan + 16, LANES), BF16)] * 2
        + [((4 * out_chan, LANES), BF16), ((8, LANES), F32)],
        acts, cot, moved=2e5,
    )
    cot_xb, cot_xa = exchange(cot_low, cot_high, "gx")
    cot_low, cot_high = local_call(
        coarse_rows_kernel,
        [((4 * out_chan + 16, LANES), BF16)] * 2,
        acts, grad_c, cot_xb, cot_xa, moved=2e5,
    )
    cot_yb, cot_ya = exchange(cot_low, cot_high, "gy")
    by_child = (
        w_down.reshape(out_chan, 4, 2, out_chan)
        .transpose(1, 3, 2, 0)
        .reshape(4 * out_chan, 2 * out_chan)
    )
    fine_grad, acts_wide = local_call(
        fine_grad_kernel,
        [((36 * out_chan, size_z), F32), ((40, size_z), F32)],
        acts, grad_c, cot_xb, cot_xa, cot_yb, cot_ya, by_child,
        scratch=[((2 * out_chan, size_z), BF16)], moved=3e6,
    )

    per_step = min(chunks, 16 // halves)
    low, high = local_call(
        functools.partial(scatter_kernel, halves, in_chan, size_y),
        [((groups // 2 * in_chan, size_z), BF16)] * 2,
        recv, acts,
        scratch=[
            ((groups * in_chan, size_z), F32),
            ((groups * in_chan, per_step * halves * LANES), BF16),
            ((size_z, per_step * halves * LANES), BF16),
        ],
        moved=2e7,
    )
    below, above = exchange(low, high, "gx")
    row_low, row_high = local_call(
        rows_kernel,
        [((groups * in_chan, size_z), BF16)] * 2,
        below, low, high, above, moved=1e6,
    )
    left, right = exchange(row_low, row_high, "gy")
    all_rows = 64 * in_chan
    tile_low, tile_high, swap = local_call(
        functools.partial(columns_kernel, in_chan),
        [((all_rows, LANES), BF16)] * 3,
        place, below, low, high, above, left, right, smem=(0,), moved=3e6,
    )
    before, after = z_exchange(tile_low, tile_high, swap)

    hidden, stack, stats = local_call(
        functools.partial(conv_kernel, only_two),
        [((6 * wide, size_z), F32), ((3 * all_rows, size_z), BF16), ((devices, 8, LANES), F32)],
        place, tile_low, tile_high, before, after, bands, acts_wide, smem=(0,), moved=2e7,
    )
    stats = everyone(stats)
    gain, shift = bn_gain.reshape(-1, 1), bn_shift.reshape(-1, 1)
    grad_pre, fine_out, sums = local_call(
        norm_kernel,
        [
            ((6 * wide, size_z), F32),
            ((groups * out_chan, size_z), BF16),
            ((devices, 8, LANES), F32),
        ],
        stats, gain, shift, hidden, fine_grad, acts_wide, moved=1e7,
    )
    sums = everyone(sums)
    coarse, raw_down = local_call(
        down_kernel,
        [((4, out_chan, LANES), BF16), ((4 * out_chan, LANES), F32)],
        fine_out, grad_c, coarse_mask, w_down,
        scratch=[((8 * out_chan, 4 * LANES), BF16)], moved=5e6,
    )
    half_x, half_y, half_z = size_x // 2, size_y // 2, size_z // 2
    coarse_out = coarse.reshape(half_x, half_y, out_chan, half_z).transpose(2, 0, 1, 3)

    grad_low, grad_high, grad_swap, small = local_call(
        hidden_grad_kernel,
        [((6 * wide, LANES), BF16)] * 3 + [((8, LANES), F32)],
        place, stats, sums, gain, hidden, grad_pre, acts_wide, smem=(0,), moved=5e6,
    )
    grad_before, grad_after = z_exchange(grad_low, grad_high, grad_swap)
    piece = -(-(16 * in_chan + 4 * out_chan) // devices)
    piece = -(-piece // 8) * 8
    parts = local_call(
        functools.partial(weight_grad_kernel, in_chan),
        [((devices * piece, LANES), F32)],
        stack, grad_low, grad_high, raw_down,
        scratch=[((3, 24 * in_chan, 4 * out_chan), F32)], moved=1e7,
    )[0]
    parts = everyone(parts.reshape(devices, piece, LANES))

    points = local_call(
        functools.partial(point_grad_kernel, only_two, halves, in_chan),
        [((chunks, halves * in_chan, LANES), BF16)],
        place, grad_low, grad_high, grad_before, grad_after, back_bands, acts, recv,
        scratch=[((18 * wide, size_z), BF16), ((groups * in_chan, size_z), BF16)],
        smem=(0,), moved=2e7,
    )[0]
    shapes = [((out_chan, 27 * in_chan), F32), ((out_chan, 8 * out_chan), F32)]
    flat = [((devices * piece, LANES), F32)]
    if aligned:
        both = local_call(
            piece_kernel,
            [((devices, halves * in_chan + piece, LANES), BF16)],
            parts, points, moved=2e6,
        )[0]
        returned, raw_sub, raw_down = local_call(
            functools.partial(last_kernel, halves, in_chan),
            [((in_chan, slot_total), BF16)] + shapes,
            everyone(both), small, scratch=flat, moved=2e6,
        )
    else:
        points = points.reshape(chunks, in_chan, together, slot_cap).transpose(0, 2, 1, 3)
        returned = everyone(points.reshape(devices, in_chan, slot_cap))
        returned = returned.transpose(1, 0, 2).reshape(in_chan, slot_total)
        whole = local_call(sum_kernel, [((devices, piece, LANES), BF16)], parts)[0]
        raw_sub, raw_down = local_call(
            functools.partial(weights_kernel, in_chan), shapes, everyone(whole), small, scratch=flat
        )
    return (
        coarse_out,
        returned,
        raw_sub,
        raw_down,
        small[1, :out_chan],
        small[0, :out_chan],
    )


def solution(mesh):
    in_specs = (
        P(None, AXES),
        P(AXES),
        P(AXES, None),
        P("gx", "gy", "gz"),
        P(),
        P(),
        P(),
        P(),
        P(None, "gx", "gy", "gz"),
    )
    out_specs = (P(None, "gx", "gy", "gz"), P(None, AXES), P(), P(), P(), P())
    return jax.shard_map(
        on_device, mesh=mesh, in_specs=in_specs, out_specs=out_specs, check_vma=False
    )
```

time: 639 us -> 173 us (0.27); the launches traced: 630 us -> 172 us
  local copies, waits for them, and re-layouts: 162 us -> 30.1 us
  blocking collectives: 120 us -> 0 us
  other arithmetic: 103 us -> 0.72 us
  waiting for transfers between devices: 165 us -> 72.1 us
  Pallas kernels: 0 us -> 32.6 us
  matrix products: 22.1 us -> 0 us
  between operations: 16.3 us -> 1.13 us
  starting transfers between devices: 42.4 us -> 35.6 us
    psum x1 -> x0, waiting for transfers between devices: 131 us -> none  [on_device(): raw_sub, raw_down = lax.psum((local_sub, local_down), ('gx', 'gy', 'gz'))]
    psum x3 -> x0, blocking collectives: 120 us -> none  [the longest x1 40.8 us: on_device(): spread = lax.psum(jnp.sum(centred * centred, axis=1), ('gx', 'gy', 'gz'))]
    reshape x34 -> x7, local copies, waits for them, and re-layouts: 63.7 us -> 2.83 us  [the longest x2 1.5 us: on_device(): gain, shift = (bn_gain.reshape(-1, 1), bn_shift.reshape(-1, 1))]
    scatter-add x1 -> x0, other arithmetic: 53.4 us -> none  [on_device(): jax.ops.segment_sum(arriving.T.astype(jnp.float32), target, num_segments=...]
    pallas_call x0 -> x16, Pallas kernels: none -> 32.6 us  [local_call(): pl.pallas_call(kernel, out_shape=[jax.ShapeDtypeStruct(shape, kind) for s...]
    all_to_all x3 -> x5, waiting for transfers between devices: 16.3 us -> 47.8 us  [everyone(): return lax.all_to_all(block, AXES, split_axis=0, concat_axis=0, tiled=True)]
    gather x2 -> x0, local copies, waits for them, and re-layouts: 31.1 us -> none  [on_device(): grad_grid[:, target]]
    concatenate x18 -> x0, other arithmetic: 30.8 us -> none  [the longest x12 21.5 us: columns(): joined = jnp.concatenate(pieces, axis=0)]
  transfers between devices with their start and end apart: 16 -> 15, of which waited for: 11 -> 11; matrix products, arithmetic and copies ran while one was open for 5% -> 3% of each run, Pallas kernels for 0% -> 9%
where the time goes in v1:
time: 173 us; the launch traced here: 172 us
  waiting for transfers between devices  72.1 us (42%)
  starting transfers between devices  35.6 us (21%)
  Pallas kernels  32.6 us (19%)
  local copies, waits for them, and re-layouts  30.1 us (17%)
    all_to_all x5, waiting for transfers between devices, everyone(): return lax.all_to_all(block, AXES, split_axis=0, concat_axis=0, tiled=True)  47.8 us
    pallas_call x16, Pallas kernels, local_call(): pl.pallas_call(kernel, out_shape=[jax.ShapeDtypeStruct(shape, kind) for s...  32.6 us
    unnamed x89, local copies, waits for them, and re-layouts  26.5 us
    all_to_all x5, starting transfers between devices, everyone(): return lax.all_to_all(block, AXES, split_axis=0, concat_axis=0, tiled=True)  21.1 us
    ppermute x4, waiting for transfers between devices, exchange(): lax.ppermute(low, axis, neighbours(axis, -1))  16 us
    ppermute x4, starting transfers between devices, exchange(): lax.ppermute(high, axis, neighbours(axis, 1))  9.19 us
    ppermute x4, waiting for transfers between devices, exchange(): lax.ppermute(high, axis, neighbours(axis, 1))  6.13 us
    ppermute x4, starting transfers between devices, exchange(): lax.ppermute(low, axis, neighbours(axis, -1))  5.17 us
  transfers between devices with their start and end apart: 15, of which 11 were waited for; matrix products, arithmetic and copies ran while one was open for 3% of the time, Pallas kernels for 9%

profile of v1, /device:TPU:0, one launch (start us, length us, event | category | flops | bytes accessed | tf_op | source)
XLA Modules:
  0.0 172.2 jit_solution(13079844759751031567)
XLA Ops:
  3.1 1.6 shard_map.136
  4.7 7.3 %all-to-all-start = ((bf16[32,72,128]{2,1,0:T(8,128)(2,1)}), bf16[32,72,128]{2,1,0:T(8,128)(2,1)S(1)}, u32[]{:S(2)}, u32[]{:S(2)}) async-start(bf16[32,72,128]{2,1,0:T(8,128)(2,1)} %shard_map.136), calls=%async_computation | async-start | bytes 1179648 | tf_op jit(solution)/shard_map/all_to_all | solution.py:56
  12.7 17.0 %all-to-all-done.recv_ref = bf16[32,72,128]{2,1,0:T(8,128)(2,1)S(1)} async-done(((bf16[32,72,128]{2,1,0:T(8,128)(2,1)}), bf16[32,72,128]{2,1,0:T(8,128)(2,1)S(1)}, u32[]{:S(2)}, u32[]{:S(2)}) %all-to-all-start) | async-done | bytes 589856 | tf_op jit(solution)/shard_map/all_to_all | solution.py:56
  29.7 4.1 %shard_map.137 = (bf16[256,256]{1,0:T(8,128)(2,1)S(1)}, bf16[256,256]{1,0:T(8,128)(2,1)S(1)}) custom-call(bf16[32,72,128]{2,1,0:T(8,128)(2,1)S(1)} %all-to-all-done.recv_ref, f32[16,256]{1,0:T(8,128)S(1)} %convert_element_type.10.act_ref), custom_call_target="tpu_custom_call" | custom-call | bytes 20000000 | tf_op jit(solution)/shard_map/pallas_call | solution.py:23
  33.9 1.5 collective-permute-start
  36.7 2.3 %collective-permute-done.b_ref = bf16[256,256]{1,0:T(8,128)(2,1)S(1)} collective-permute-done((bf16[256,256]{1,0:T(8,128)(2,1)S(1)}, bf16[256,256]{1,0:T(8,128)(2,1)S(1)}, u32[]{:S(2)}, u32[]{:S(2)}) %collective-permute-start) | collective-permute-done | bytes 131104 | tf_op jit(solution)/shard_map/ppermute | solution.py:43
  39.0 5.2 %collective-permute-done.1.a_ref = bf16[256,256]{1,0:T(8,128)(2,1)S(1)} collective-permute-done((bf16[256,256]{1,0:T(8,128)(2,1)S(1)}, bf16[256,256]{1,0:T(8,128)(2,1)S(1)}, u32[]{:S(2)}, u32[]{:S(2)}) %collective-permute-start.1) | collective-permute-done | bytes 131104 | tf_op jit(solution)/shard_map/ppermute | solution.py:44
  44.3 1.7 collective-permute-start.2
  47.3 3.8 %collective-permute-done.2.yb_ref = bf16[512,256]{1,0:T(8,128)(2,1)S(1)} collective-permute-done((bf16[512,256]{1,0:T(8,128)(2,1)S(1)}, bf16[512,256]{1,0:T(8,128)(2,1)S(1)}, u32[]{:S(2)}, u32[]{:S(2)}) %collective-permute-start.2) | collective-permute-done | bytes 262176 | tf_op jit(solution)/shard_map/ppermute | solution.py:43
  51.1 4.1 %collective-permute-done.3.ya_ref = bf16[512,256]{1,0:T(8,128)(2,1)S(1)} collective-permute-done((bf16[512,256]{1,0:T(8,128)(2,1)S(1)}, bf16[512,256]{1,0:T(8,128)(2,1)S(1)}, u32[]{:S(2)}, u32[]{:S(2)}) %collective-permute-start.3) | collective-permute-done | bytes 262176 | tf_op jit(solution)/shard_map/ppermute | solution.py:44
  57.9 3.3 %collective-permute-start.5 = (bf16[144,128]{1,0:T(8,128)(2,1)S(1)}, bf16[144,128]{1,0:T(8,128)(2,1)S(1)}, u32[]{:S(2)}, u32[]{:S(2)}) collective-permute-start(bf16[144,128]{1,0:T(8,128)(2,1)S(1)} %get-tuple-element.47), channel_id=1, source_target_pairs={{0,8},{8,16},{16,24},{1,9},{9,17},{17,25},{2,10},{10,18},{18,26},{... | collective-permute-start | bytes 110600 | tf_op jit(solution)/shard_map/ppermute | solution.py:43
  63.1 3.9 %collective-permute-done.6.after_ref.xa_ref = bf16[144,128]{1,0:T(8,128)(2,1)S(1)} collective-permute-done((bf16[144,128]{1,0:T(8,128)(2,1)S(1)}, bf16[144,128]{1,0:T(8,128)(2,1)S(1)}, u32[]{:S(2)}, u32[]{:S(2)}) %collective-permute-start.6) | collective-permute-done | bytes 36896 | tf_op jit(solution)/shard_map/ppermute | solution.py:44
  67.1 2.6 %collective-permute-start.7 = (bf16[272,128]{1,0:T(8,128)(2,1)S(1)}, bf16[272,128]{1,0:T(8,128)(2,1)S(1)}, u32[]{:S(2)}, u32[]{:S(2)}) collective-permute-start(bf16[272,128]{1,0:T(8,128)(2,1)S(1)} %get-tuple-element.49), channel_id=1, source_target_pairs={{0,2},{2,4},{4,6},{1,3},{3,5},{5,7},{8,10},{10,12},{12,14},{9,11},... | collective-permute-start | bytes 208904 | tf_op jit(solution)/shard_map/ppermute | solution.py:43
  73.2 2.7 %collective-permute-done.8.ya_ref = bf16[272,128]{1,0:T(8,128)(2,1)S(1)} collective-permute-done((bf16[272,128]{1,0:T(8,128)(2,1)S(1)}, bf16[272,128]{1,0:T(8,128)(2,1)S(1)}, u32[]{:S(2)}, u32[]{:S(2)}) %collective-permute-start.8) | collective-permute-done | bytes 69664 | tf_op jit(solution)/shard_map/ppermute | solution.py:44
  75.9 2.9 %shard_map.143 = (f32[2304,256]{1,0:T(8,128)S(1)}, f32[40,256]{1,0:T(8,128)S(1)}) custom-call(f32[16,256]{1,0:T(8,128)S(1)} %convert_element_type.10.act_ref, bf16[256,128]{1,0:T(8,128)(2,1)S(1)} %get-tuple-element.46.grad_ref, bf16[144,128]{1,0:T(8,128)(2,1)S(1)} %collective-permute-done.5.before_ref.xb_ref, ...), custom_call_target="tpu_custom_call" | custom-call | bytes 3000000 | tf_op jit(solution)/shard_map/pallas_call | solution.py:23
  78.8 1.4 copy-done.4
  82.3 3.6 %shard_map.144 = (f32[2304,256]{1,0:T(8,128)S(1)}, bf16[6144,256]{1,0:T(8,128)(2,1)S(1)}, f32[32,8,128]{2,1,0:T(8,128)S(1)}) custom-call(s32[1]{0:T(128)} %bitcast.place_ref, bf16[2048,128]{1,0:T(8,128)(2,1)S(1)} %copy-done.13, bf16[2048,128]{1,0:T(8,128)(2,1)S(1)} %copy-done.15, bf16[2048,128]{1,0:T(8,128)(2,1)S(1)} %collective-permute-done.4.before_ref.after_ref, ...), custom_call_target="tpu_custom_call" | custom-call | bytes 20000000 | tf_op jit(solution)/shard_map/pallas_call | solution.py:23
  86.0 1.6 copy-done
  88.3 2.6 %all-to-all-start.1 = ((f32[32,8,128]{2,1,0:T(8,128)}), f32[32,8,128]{2,1,0:T(8,128)S(1)}, u32[]{:S(2)}, u32[]{:S(2)}) async-start(f32[32,8,128]{2,1,0:T(8,128)} %copy-done.30), calls=%async_computation.1 | async-start | bytes 262144 | tf_op jit(solution)/shard_map/all_to_all | solution.py:56
  92.3 6.7 %all-to-all-done.1.stats_ref = f32[32,8,128]{2,1,0:T(8,128)S(1)} async-done(((f32[32,8,128]{2,1,0:T(8,128)}), f32[32,8,128]{2,1,0:T(8,128)S(1)}, u32[]{:S(2)}, u32[]{:S(2)}) %all-to-all-start.1) | async-done | bytes 131104 | tf_op jit(solution)/shard_map/all_to_all | solution.py:56
  99.0 1.7 copy-done.5
  101.5 2.2 %shard_map.145 = (f32[2304,256]{1,0:T(8,128)S(1)}, bf16[1024,256]{1,0:T(8,128)(2,1)S(1)}, f32[32,8,128]{2,1,0:T(8,128)}) custom-call(f32[32,8,128]{2,1,0:T(8,128)S(1)} %all-to-all-done.1.stats_ref, f32[64,1]{1,0:T(8,128)S(1)} %copy.30.gain_ref, f32[64,1]{1,0:T(8,128)S(1)} %copy.31.shift_ref, f32[2304,256]{1,0:T(8,128)S(1)} %get-tuple-element.53.hidden_ref, ...), custom_call_target="tpu_custom_call" | custom-call | bytes 10000000 | tf_op jit(solution)/shard_map/pallas_call | solution.py:23
  103.8 1.4 copy-done.6
  106.0 2.8 %all-to-all-start.2 = ((f32[32,8,128]{2,1,0:T(8,128)}), f32[32,8,128]{2,1,0:T(8,128)S(1)}, u32[]{:S(2)}, u32[]{:S(2)}) async-start(f32[32,8,128]{2,1,0:T(8,128)} %get-tuple-element.59), calls=%async_computation.2 | async-start | bytes 262144 | tf_op jit(solution)/shard_map/all_to_all | solution.py:56
  111.9 4.8 %all-to-all-done.2.sums_ref = f32[32,8,128]{2,1,0:T(8,128)S(1)} async-done(((f32[32,8,128]{2,1,0:T(8,128)}), f32[32,8,128]{2,1,0:T(8,128)S(1)}, u32[]{:S(2)}, u32[]{:S(2)}) %all-to-all-start.2) | async-done | bytes 131104 | tf_op jit(solution)/shard_map/all_to_all | solution.py:56
  117.4 1.7 copy-done.7
  124.3 2.3 %shard_map.148 = f32[768,128]{1,0:T(8,128)} custom-call(bf16[6144,256]{1,0:T(8,128)(2,1)S(1)} %copy-done.1, bf16[2304,128]{1,0:T(8,128)(2,1)S(1)} %get-tuple-element.61.front_ref, bf16[2304,128]{1,0:T(8,128)(2,1)S(1)} %get-tuple-element.62.rear_ref, f32[256,128]{1,0:T(8,128)S(1)} %copy-done.29), custom_call_target="tpu_custom_call" | custom-call | bytes 10000000 | tf_op jit(solution)/shard_map/pallas_call | solution.py:23
  126.6 2.6 %all-to-all-start.3 = ((f32[32,24,128]{2,1,0:T(8,128)}), f32[32,24,128]{2,1,0:T(8,128)S(1)}, u32[]{:S(2)}, u32[]{:S(2)}) async-start(f32[32,24,128]{2,1,0:T(8,128)} %bitcast.13), calls=%async_computation.3 | async-start | bytes 786432 | tf_op jit(solution)/shard_map/all_to_all | solution.py:56
  129.4 2.1 %collective-permute-done.9.before_ref.after_ref = bf16[2304,128]{1,0:T(8,128)(2,1)S(1)} collective-permute-done((bf16[2304,128]{1,0:T(8,128)(2,1)}, bf16[2304,128]{1,0:T(8,128)(2,1)S(1)}, u32[]{:S(2)}, u32[]{:S(2)}) %collective-permute-start.9) | collective-permute-done | bytes 589856 | tf_op jit(solution)/shard_map/ppermute | solution.py:51
  132.5 11.2 %shard_map.149.points_ref = bf16[32,64,128]{2,1,0:T(8,128)(2,1)S(1)} custom-call(s32[1]{0:T(128)} %bitcast.place_ref, bf16[2304,128]{1,0:T(8,128)(2,1)S(1)} %get-tuple-element.61.front_ref, bf16[2304,128]{1,0:T(8,128)(2,1)S(1)} %copy-done.3, bf16[2304,128]{1,0:T(8,128)(2,1)S(1)} %collective-permute-done.9.before_ref.after_ref, ...), custom_call_target="tpu_custom_call" | custom-call | bytes 20000000 | tf_op jit(solution)/shard_map/pallas_call | solution.py:23
  144.8 5.8 %all-to-all-start.4 = ((bf16[32,88,128]{2,1,0:T(8,128)(2,1)}), bf16[32,88,128]{2,1,0:T(8,128)(2,1)S(1)}, u32[]{:S(2)}, u32[]{:S(2)}) async-start(bf16[32,88,128]{2,1,0:T(8,128)(2,1)} %shard_map.150), calls=%async_computation.4 | async-start | bytes 1441792 | tf_op jit(solution)/shard_map/all_to_all | solution.py:56
  151.8 19.3 %all-to-all-done.4.got_ref = bf16[32,88,128]{2,1,0:T(8,128)(2,1)S(1)} async-done(((bf16[32,88,128]{2,1,0:T(8,128)(2,1)}), bf16[32,88,128]{2,1,0:T(8,128)(2,1)S(1)}, u32[]{:S(2)}, u32[]{:S(2)}) %all-to-all-start.4) | async-done | bytes 720928 | tf_op jit(solution)/shard_map/all_to_all | solution.py:56
  (117 shorter events, 33.0 us)
Async XLA Ops:
  3.1 54.0 %copy-start.41 = (bf16[64,2,2,128]{3,2,1,0:T(2,128)(2,1)S(1)}, bf16[64,2,2,128]{3,2,1,0:T(2,128)(2,1)}, u32[]{:S(2)}) copy-start(bf16[64,2,2,128]{3,2,1,0:T(2,128)(2,1)} %param.17) | copy-start | bytes 196612
  3.1 59.4 %copy-start.26 = (bf16[64,512]{1,0:T(8,128)(2,1)S(1)}, bf16[64,512]{1,0:T(8,128)(2,1)}, u32[]{:S(2)}) copy-start(bf16[64,512]{1,0:T(8,128)(2,1)} %down_ref.1) | copy-start | bytes 196612
  4.7 58.2 %copy-start.40 = (bf16[64,864]{1,0:T(8,128)(2,1)S(1)}, bf16[64,864]{1,0:T(8,128)(2,1)}, u32[]{:S(2)}) copy-start(bf16[64,864]{1,0:T(8,128)(2,1)} %param.13) | copy-start | bytes 331780
  4.7 25.1 %all-to-all-start = ((bf16[32,72,128]{2,1,0:T(8,128)(2,1)}), bf16[32,72,128]{2,1,0:T(8,128)(2,1)S(1)}, u32[]{:S(2)}, u32[]{:S(2)}) async-start(bf16[32,72,128]{2,1,0:T(8,128)(2,1)} %shard_map.136), calls=%async_computation | async-start | bytes 1179648 | tf_op jit(solution)/shard_map/all_to_all | solution.py:56
  33.9 5.2 %collective-permute-start = (bf16[256,256]{1,0:T(8,128)(2,1)S(1)}, bf16[256,256]{1,0:T(8,128)(2,1)S(1)}, u32[]{:S(2)}, u32[]{:S(2)}) collective-permute-start(bf16[256,256]{1,0:T(8,128)(2,1)S(1)} %get-tuple-element.38.high_ref), channel_id=1, source_target_pairs={{0,8},{8,16},{16,24},{1,9},{9,17},{17,25},{2,10},{10,18},{18,26},{... | collective-permute-start | bytes 393224 | tf_op jit(solution)/shard_map/ppermute | solution.py:43
  35.4 8.8 %collective-permute-start.1 = (bf16[256,256]{1,0:T(8,128)(2,1)S(1)}, bf16[256,256]{1,0:T(8,128)(2,1)S(1)}, u32[]{:S(2)}, u32[]{:S(2)}) collective-permute-start(bf16[256,256]{1,0:T(8,128)(2,1)S(1)} %get-tuple-element.39.low_ref), channel_id=1, source_target_pairs={{8,0},{16,8},{24,16},{9,1},{17,9},{25,17},{10,2},{18,10},{26,18},{... | collective-permute-start | bytes 393224 | tf_op jit(solution)/shard_map/ppermute | solution.py:44
  44.3 6.8 %collective-permute-start.2 = (bf16[512,256]{1,0:T(8,128)(2,1)S(1)}, bf16[512,256]{1,0:T(8,128)(2,1)S(1)}, u32[]{:S(2)}, u32[]{:S(2)}) collective-permute-start(bf16[512,256]{1,0:T(8,128)(2,1)S(1)} %get-tuple-element.40), channel_id=1, source_target_pairs={{0,2},{2,4},{4,6},{1,3},{3,5},{5,7},{8,10},{10,12},{12,14},{9,11},... | collective-permute-start | bytes 786440 | tf_op jit(solution)/shard_map/ppermute | solution.py:43
  46.0 9.3 %collective-permute-start.3 = (bf16[512,256]{1,0:T(8,128)(2,1)S(1)}, bf16[512,256]{1,0:T(8,128)(2,1)S(1)}, u32[]{:S(2)}, u32[]{:S(2)}) collective-permute-start(bf16[512,256]{1,0:T(8,128)(2,1)S(1)} %get-tuple-element.41), channel_id=1, source_target_pairs={{2,0},{4,2},{6,4},{3,1},{5,3},{7,5},{10,8},{12,10},{14,12},{11,9},... | collective-permute-start | bytes 786440 | tf_op jit(solution)/shard_map/ppermute | solution.py:44
  57.1 23.2 %collective-permute-start.4 = (bf16[2048,128]{1,0:T(8,128)(2,1)S(1)}, bf16[2048,128]{1,0:T(8,128)(2,1)S(1)}, u32[]{:S(2)}, u32[]{:S(2)}) collective-permute-start(bf16[2048,128]{1,0:T(8,128)(2,1)S(1)} %get-tuple-element.44), channel_id=1, source_target_pairs={{0,1},{1,0},{2,3},{3,2},{4,5},{5,4},{6,7},{7,6},{8,9},{9,8},{10,11... | collective-permute-start | bytes 1572872 | tf_op jit(solution)/shard_map/ppermute | solution.py:51
  57.9 5.3 %collective-permute-start.5 = (bf16[144,128]{1,0:T(8,128)(2,1)S(1)}, bf16[144,128]{1,0:T(8,128)(2,1)S(1)}, u32[]{:S(2)}, u32[]{:S(2)}) collective-permute-start(bf16[144,128]{1,0:T(8,128)(2,1)S(1)} %get-tuple-element.47), channel_id=1, source_target_pairs={{0,8},{8,16},{16,24},{1,9},{9,17},{17,25},{2,10},{10,18},{18,26},{... | collective-permute-start | bytes 110600 | tf_op jit(solution)/shard_map/ppermute | solution.py:43
  61.2 5.9 %collective-permute-start.6 = (bf16[144,128]{1,0:T(8,128)(2,1)S(1)}, bf16[144,128]{1,0:T(8,128)(2,1)S(1)}, u32[]{:S(2)}, u32[]{:S(2)}) collective-permute-start(bf16[144,128]{1,0:T(8,128)(2,1)S(1)} %get-tuple-element.48), channel_id=1, source_target_pairs={{8,0},{16,8},{24,16},{9,1},{17,9},{25,17},{10,2},{18,10},{26,18},{... | collective-permute-start | bytes 110600 | tf_op jit(solution)/shard_map/ppermute | solution.py:44
  67.1 6.2 %collective-permute-start.7 = (bf16[272,128]{1,0:T(8,128)(2,1)S(1)}, bf16[272,128]{1,0:T(8,128)(2,1)S(1)}, u32[]{:S(2)}, u32[]{:S(2)}) collective-permute-start(bf16[272,128]{1,0:T(8,128)(2,1)S(1)} %get-tuple-element.49), channel_id=1, source_target_pairs={{0,2},{2,4},{4,6},{1,3},{3,5},{5,7},{8,10},{10,12},{12,14},{9,11},... | collective-permute-start | bytes 208904 | tf_op jit(solution)/shard_map/ppermute | solution.py:43
  69.7 6.2 %collective-permute-start.8 = (bf16[272,128]{1,0:T(8,128)(2,1)S(1)}, bf16[272,128]{1,0:T(8,128)(2,1)S(1)}, u32[]{:S(2)}, u32[]{:S(2)}) collective-permute-start(bf16[272,128]{1,0:T(8,128)(2,1)S(1)} %get-tuple-element.50), channel_id=1, source_target_pairs={{2,0},{4,2},{6,4},{3,1},{5,3},{7,5},{10,8},{12,10},{14,12},{11,9},... | collective-permute-start | bytes 208904 | tf_op jit(solution)/shard_map/ppermute | solution.py:44
  80.2 5.7 %copy-start.21 = (f32[40,256]{1,0:T(8,128)}, f32[40,256]{1,0:T(8,128)S(1)}, u32[]{:S(2)}) copy-start(f32[40,256]{1,0:T(8,128)S(1)} %get-tuple-element.51.acts_ref) | copy-start | bytes 122884
  88.3 10.8 %all-to-all-start.1 = ((f32[32,8,128]{2,1,0:T(8,128)}), f32[32,8,128]{2,1,0:T(8,128)S(1)}, u32[]{:S(2)}, u32[]{:S(2)}) async-start(f32[32,8,128]{2,1,0:T(8,128)} %copy-done.30), calls=%async_computation.1 | async-start | bytes 262144 | tf_op jit(solution)/shard_map/all_to_all | solution.py:56
  91.6 12.1 %copy-start.24 = (f32[64,1]{1,0:T(8,128)}, f32[64,1]{1,0:T(8,128)S(1)}, u32[]{:S(2)}) copy-start(f32[64,1]{1,0:T(8,128)S(1)} %copy.30.gain_ref) | copy-start | bytes 772
  99.0 4.7 %copy-start.8 = (f32[32,8,128]{2,1,0:T(8,128)}, f32[32,8,128]{2,1,0:T(8,128)S(1)}, u32[]{:S(2)}) copy-start(f32[32,8,128]{2,1,0:T(8,128)S(1)} %all-to-all-done.1.stats_ref) | copy-start | bytes 393220
  99.0 1.7 copy-start.5
  101.5 7.2 %copy-start.27 = (bf16[64,512]{1,0:T(8,128)(2,1)S(1)}, bf16[64,512]{1,0:T(8,128)(2,1)}, u32[]{:S(2)}) copy-start(bf16[64,512]{1,0:T(8,128)(2,1)} %down_ref.1) | copy-start | bytes 196612
  101.5 7.3 %copy-start.37 = (f32[8,128]{1,0:T(8,128)S(1)}, f32[8,128]{1,0:T(8,128)}, u32[]{:S(2)}) copy-start(f32[8,128]{1,0:T(8,128)} %copy-done.36) | copy-start | bytes 12292
  106.0 10.8 %all-to-all-start.2 = ((f32[32,8,128]{2,1,0:T(8,128)}), f32[32,8,128]{2,1,0:T(8,128)S(1)}, u32[]{:S(2)}, u32[]{:S(2)}) async-start(f32[32,8,128]{2,1,0:T(8,128)} %get-tuple-element.59), calls=%async_computation.2 | async-start | bytes 262144 | tf_op jit(solution)/shard_map/all_to_all | solution.py:56
  122.4 1.9 %copy-start.1 = (bf16[6144,256]{1,0:T(8,128)(2,1)S(1)}, bf16[6144,256]{1,0:T(8,128)(2,1)}, u32[]{:S(2)}) copy-start(bf16[6144,256]{1,0:T(8,128)(2,1)} %copy-done) | copy-start | bytes 9437188
  122.4 1.9 %copy-start.29 = (f32[256,128]{1,0:T(8,128)S(1)}, f32[256,128]{1,0:T(8,128)}, u32[]{:S(2)}) copy-start(f32[256,128]{1,0:T(8,128)} %copy-done.28) | copy-start | bytes 393220
  123.6 3.0 %copy-start.2 = (bf16[2304,128]{1,0:T(8,128)(2,1)}, bf16[2304,128]{1,0:T(8,128)(2,1)S(1)}, u32[]{:S(2)}) copy-start(bf16[2304,128]{1,0:T(8,128)(2,1)S(1)} %get-tuple-element.62.rear_ref) | copy-start | bytes 1769476
  123.6 3.0 %copy-start.34 = (f32[8,128]{1,0:T(8,128)}, f32[8,128]{1,0:T(8,128)S(1)}, u32[]{:S(2)}) copy-start(f32[8,128]{1,0:T(8,128)S(1)} %get-tuple-element.66.small_ref) | copy-start | bytes 12292
  123.6 2.9 %copy-start.39 = (bf16[2304,128]{1,0:T(8,128)(2,1)}, bf16[2304,128]{1,0:T(8,128)(2,1)S(1)}, u32[]{:S(2)}) copy-start(bf16[2304,128]{1,0:T(8,128)(2,1)S(1)} %get-tuple-element.64) | copy-start | bytes 1769476
  124.3 7.2 %copy-start.11 = (bf16[128,3456]{1,0:T(8,128)(2,1)S(1)}, bf16[128,3456]{1,0:T(8,128)(2,1)}, u32[]{:S(2)}) copy-start(bf16[128,3456]{1,0:T(8,128)(2,1)} %copy-done.10) | copy-start | bytes 2654212
  126.6 17.2 %all-to-all-start.3 = ((f32[32,24,128]{2,1,0:T(8,128)}), f32[32,24,128]{2,1,0:T(8,128)S(1)}, u32[]{:S(2)}, u32[]{:S(2)}) async-start(f32[32,24,128]{2,1,0:T(8,128)} %bitcast.13), calls=%async_computation.3 | async-start | bytes 786432 | tf_op jit(solution)/shard_map/all_to_all | solution.py:56
  129.2 2.3 %collective-permute-start.9 = (bf16[2304,128]{1,0:T(8,128)(2,1)}, bf16[2304,128]{1,0:T(8,128)(2,1)S(1)}, u32[]{:S(2)}, u32[]{:S(2)}) collective-permute-start(bf16[2304,128]{1,0:T(8,128)(2,1)} %copy-done.39), channel_id=1, source_target_pairs={{0,1},{1,0},{2,3},{3,2},{4,5},{5,4},{6,7},{7,6},{8,9},{9,8},{10,11... | collective-permute-start | bytes 1769480 | tf_op jit(solution)/shard_map/ppermute | solution.py:51
  143.8 6.8 %copy-start.32 = (bf16[4,64,128]{2,1,0:T(8,128)(2,1)S(1)}, bf16[4,64,128]{2,1,0:T(8,128)(2,1)}, u32[]{:S(2)}) copy-start(bf16[4,64,128]{2,1,0:T(8,128)(2,1)} %copy-done.31) | copy-start | bytes 196612
  143.8 7.5 %copy-start.35 = (f32[8,128]{1,0:T(8,128)S(1)}, f32[8,128]{1,0:T(8,128)}, u32[]{:S(2)}) copy-start(f32[8,128]{1,0:T(8,128)} %copy-done.34) | copy-start | bytes 12292
  144.8 26.4 %all-to-all-start.4 = ((bf16[32,88,128]{2,1,0:T(8,128)(2,1)}), bf16[32,88,128]{2,1,0:T(8,128)(2,1)S(1)}, u32[]{:S(2)}, u32[]{:S(2)}) async-start(bf16[32,88,128]{2,1,0:T(8,128)(2,1)} %shard_map.150), calls=%async_computation.4 | async-start | bytes 1441792 | tf_op jit(solution)/shard_map/all_to_all | solution.py:56
  (25 other events, 23.5 us)

commit v2 on v1

v2 whole, which is shorter than its diff:
```python
import functools
import math

import jax
import jax.numpy as jnp
from jax import lax
from jax.experimental import pallas as pl
from jax.experimental.pallas import tpu as pltpu
from jax.sharding import PartitionSpec as P

EPS = 1e-05
AXES = ("gx", "gy", "gz")
LANES = 128
GELU_SCALE = 0.7978845608028654
GELU_CUBE = 0.044715
F32 = jnp.float32
BF16 = jnp.bfloat16
NT = (((1,), (1,)), ((), ()))


def local_call(kernel, outs, *args, scratch=(), smem=(), hbm=(), hbm_outs=(), copies=0, moved=0):
    held = sum(math.prod(shape) * jnp.dtype(kind).itemsize for shape, kind in scratch)
    limit = held // 2**20 + 6
    vmem = pl.BlockSpec(memory_space=pltpu.VMEM)
    scalar = pl.BlockSpec(memory_space=pltpu.SMEM)
    far = pl.BlockSpec(memory_space=pltpu.HBM)
    args = [
        pltpu.with_memory_space_constraint(arg, pltpu.HBM) if i in hbm else arg
        for i, arg in enumerate(args)
    ]
    held = [pltpu.VMEM(shape, kind) for shape, kind in scratch]
    if copies:
        held.append(pltpu.SemaphoreType.DMA((copies,)))
    return pl.pallas_call(
        kernel,
        out_shape=[
            pltpu.HBM(shape, kind) if i in hbm_outs else jax.ShapeDtypeStruct(shape, kind)
            for i, (shape, kind) in enumerate(outs)
        ],
        in_specs=[
            scalar if i in smem else far if i in hbm else vmem for i in range(len(args))
        ],
        out_specs=[far if i in hbm_outs else vmem for i in range(len(outs))],
        scratch_shapes=held,
        compiler_params=pltpu.CompilerParams(vmem_limit_bytes=limit * 1024 * 1024),
        cost_estimate=pl.CostEstimate(flops=0, bytes_accessed=int(moved), transcendentals=0),
    )(*args)


def started(source, target, semaphore):
    copy = pltpu.make_async_copy(source, target, semaphore)
    copy.start()
    return copy


def rows_of(n, count):
    return pl.ds(n * count, count)


def neighbours(axis, step):
    count = lax.axis_size(axis)
    return [(i, i + step) for i in range(count) if 0 <= i + step < count]


def swaps(first, second, axis):
    count = lax.axis_size(axis)
    got = []
    for block, begin in ((first, 0), (second, 1)):
        pairs = [(i, i + 1) for i in range(begin, count - 1, 2)]
        got.append(lax.ppermute(block, axis, pairs + [(j, i) for i, j in pairs]))
    return got


def sided(odd, first, second):
    return jnp.where(odd, first, second), jnp.where(odd, second, first)


def z_exchange(low, high, swap):
    if lax.axis_size("gz") != 2:
        return (
            lax.ppermute(high, "gz", neighbours("gz", 1)),
            lax.ppermute(low, "gz", neighbours("gz", -1)),
        )
    got = lax.ppermute(swap, "gz", [(0, 1), (1, 0)])
    return got, got


def everyone(block):
    return lax.all_to_all(block, AXES, split_axis=0, concat_axis=0, tiled=True)


def pack_kernel(
    halves, groups, depth, counts_ref, feats_ref, ids_ref, out_ref, feats, ids, sems
):
    devices = out_ref.shape[0]
    chan = feats_ref.shape[0]
    parts = 4
    width = feats.shape[1] // parts
    got_ids = started(ids_ref, ids, sems.at[parts])
    got = []
    for n in range(parts):
        lanes = pl.ds(n * width, width)
        got.append(started(feats_ref.at[:, lanes], feats.at[:, lanes], sems.at[n]))
    got_ids.wait()
    rank = lax.broadcasted_iota(jnp.int32, (halves, LANES), 0) * LANES + lax.broadcasted_iota(
        jnp.int32, (halves, LANES), 1
    )
    blank = jnp.zeros((8 - 2 * halves, LANES), F32)
    for d in range(devices):
        those = ids[d * halves : (d + 1) * halves, :]
        usable = rank < counts_ref[0, d]
        group = jnp.where(usable, those // depth, groups).astype(F32)
        place = (those % depth).astype(F32)
        tags = jnp.concatenate([group, place, blank], axis=0)
        out_ref[d, halves * chan :, :] = tags.astype(BF16)
    for d in range(devices):
        if d * parts % devices == 0:
            got[d * parts // devices].wait()
        for h in range(halves):
            first = (d * halves + h) * LANES
            out_ref[d, h * chan : (h + 1) * chan, :] = feats[:, first : first + LANES]


def pack_plain(feats, ids, counts, groups, depth):
    chan, total = feats.shape
    devices = counts.shape[1]
    cap = total // devices
    ids = ids.reshape(devices, 1, cap)
    rank = jnp.arange(cap, dtype=jnp.int32)[None, None, :]
    group = jnp.where(rank < counts.reshape(devices, 1, 1), ids // depth, groups)
    tags = jnp.concatenate([group, ids % depth], axis=1).astype(BF16)
    rows = feats.reshape(chan, devices, cap).transpose(1, 0, 2)
    return jnp.concatenate([rows, jnp.pad(tags, ((0, 0), (0, 6), (0, 0)))], axis=1)


def scatter_kernel(
    halves, chan, size_y, sides_ref, recv_ref, act_ref, first_ref, second_ref, tags_ref,
    acc, masked, hot, tags_held, sems,
):
    chunks = recv_ref.shape[0]
    groups, depth = act_ref.shape
    per_step = masked.shape[1] // (halves * LANES)
    steps = chunks // per_step
    place = lax.broadcasted_iota(jnp.int32, (depth, LANES), 0).astype(F32)
    tags_held[...] = recv_ref[:, halves * chan :, :].astype(F32)
    kept = started(tags_held, tags_ref, sems.at[0])

    def step(s, carry):
        for j in range(per_step):
            block = recv_ref[s * per_step + j]
            tags = tags_held[s * per_step + j]
            for h in range(halves):
                feats = block[h * chan : (h + 1) * chan, :]
                col = (j * halves + h) * LANES
                group = jnp.broadcast_to(tags[h : h + 1, :], (chan, LANES)).astype(BF16)
                for k in range(groups):
                    masked[k * chan : (k + 1) * chan, col : col + LANES] = jnp.where(
                        group == k, feats, jnp.zeros_like(feats)
                    )
                low = tags[halves + h : halves + h + 1, :]
                hot[:, col : col + LANES] = jnp.where(place == low, 1.0, 0.0).astype(BF16)
        part = lax.dot_general(masked[...], hot[...], NT, preferred_element_type=F32)

        @pl.when(s == 0)
        def _():
            acc[...] = part

        @pl.when(s > 0)
        def _():
            acc[...] += part

        return carry

    lax.fori_loop(0, steps, step, 0)
    odd = sides_ref[0] != 0
    half = size_y // 2
    for k in range(groups // 2):
        p, q = k // size_y, k % size_y
        row = ((q // half) * 4 + p * 2 + q % half) * chan
        blocks = []
        for n in (k, k + groups // 2):
            block = acc[n * chan : (n + 1) * chan, :] * act_ref[n : n + 1, :]
            blocks.append(block.astype(BF16))
        first_ref[row : row + chan, :], second_ref[row : row + chan, :] = sided(odd, *blocks)
    kept.wait()


def coarse_kernel(sides_ref, act_ref, cot_ref, first_ref, second_ref, grad_ref, mask_ref):
    depth = act_ref.shape[1]
    chan = cot_ref.shape[2]
    odd = sides_ref[0] != 0
    fine = lax.broadcasted_iota(jnp.int32, (depth, LANES), 0) // 2
    pair = (fine == lax.broadcasted_iota(jnp.int32, (depth, LANES), 1)).astype(BF16)
    acts = act_ref[...]
    sums = jnp.dot(acts.astype(BF16), pair, preferred_element_type=F32)
    masks, grads = [], []
    for x in range(2):
        for y in range(2):
            rows = [sums[(2 * x + a) * 4 + 2 * y + b] for a in range(2) for b in range(2)]
            any_row = (rows[0] + rows[1] + rows[2] + rows[3])[None, :]
            mask = jnp.where(any_row > 0.5, 1.0, 0.0)
            masks.append(mask)
            grads.append((cot_ref[x, y].astype(F32) * mask).astype(BF16))
    for n, grad in enumerate(grads):
        grad_ref[n * chan : (n + 1) * chan, :] = grad
    for y in range(2):
        own = slice(y * chan, (y + 1) * chan)
        first_ref[own, :], second_ref[own, :] = sided(odd, grads[y], grads[2 + y])
    mask_ref[...] = jnp.concatenate(masks + [jnp.zeros((4, LANES), F32)], axis=0)
    blank = jnp.zeros((8, LANES), F32)
    tails = []
    for p in (0, 3):
        rows = acts[4 * p : 4 * p + 4]
        tails.append(jnp.concatenate([rows[:, :LANES], rows[:, LANES:], blank], axis=0))
    tails = sided(odd, *tails)
    for out_ref, tail in zip((first_ref, second_ref), tails):
        out_ref[2 * chan :, :] = tail.astype(BF16)


def coarse_rows_kernel(sides_ref, act_ref, grad_ref, xf_ref, xs_ref, first_ref, second_ref):
    chan = grad_ref.shape[0] // 4
    odd_x, odd_y = sides_ref[0] != 0, sides_ref[1] != 0
    before, after = sided(odd_x, xf_ref[...], xs_ref[...])
    acts = act_ref[...]
    before_acts = before[2 * chan :, :].astype(F32)
    after_acts = after[2 * chan :, :].astype(F32)
    ends = []
    for y, q in ((0, 0), (1, 3)):
        own = slice(y * chan, (y + 1) * chan)
        columns = [before[own], grad_ref[own, :]]
        columns += [grad_ref[(2 + y) * chan : (3 + y) * chan, :], after[own]]
        rows = [before_acts[q : q + 1], before_acts[4 + q : 5 + q]]
        for p in range(4):
            row = acts[4 * p + q : 4 * p + q + 1]
            rows += [row[:, :LANES], row[:, LANES:]]
        rows += [after_acts[q : q + 1], after_acts[4 + q : 5 + q], jnp.zeros((4, LANES), F32)]
        ends.append(columns + [jnp.concatenate(rows, axis=0).astype(BF16)])
    row = 0
    for low, high in zip(*ends):
        own = slice(row, row + low.shape[0])
        first_ref[own, :], second_ref[own, :] = sided(odd_y, low, high)
        row += low.shape[0]


def wide_kernel(
    sides_ref, act_ref, grad_ref, xf_ref, xs_ref, yf_ref, ys_ref, wide_ref, acts_ref
):
    chan = grad_ref.shape[0] // 4
    depth = act_ref.shape[1]
    acts = act_ref[...]
    x_ends = sided(sides_ref[0] != 0, xf_ref[...], xs_ref[...])
    y_ends = sided(sides_ref[1] != 0, yf_ref[...], ys_ref[...])
    xb, xa = [end[2 * chan :, :].astype(F32) for end in x_ends]
    yb, ya = [end[4 * chan :, :].astype(F32) for end in y_ends]
    rows = []
    for p in range(6):
        rows.append(jnp.concatenate([yb[2 * p : 2 * p + 1], yb[2 * p + 1 : 2 * p + 2]], axis=1))
        for q in range(4):
            if p in (0, 5):
                got = xb if p == 0 else xa
                rows.append(jnp.concatenate([got[q : q + 1], got[4 + q : 5 + q]], axis=1))
            else:
                rows.append(acts[4 * (p - 1) + q : 4 * (p - 1) + q + 1])
        rows.append(jnp.concatenate([ya[2 * p : 2 * p + 1], ya[2 * p + 1 : 2 * p + 2]], axis=1))
    rows.append(jnp.zeros((4, depth), F32))
    acts_ref[...] = jnp.concatenate(rows, axis=0)
    for x in range(4):
        for y in range(4):
            if y in (0, 3):
                block = y_ends[y // 3][x * chan : (x + 1) * chan, :]
            elif x in (0, 3):
                block = x_ends[x // 3][(y - 1) * chan : y * chan, :]
            else:
                first = ((x - 1) * 2 + y - 1) * chan
                block = grad_ref[first : first + chan, :]
            wide_ref[(x * 4 + y) * chan : (x * 4 + y + 1) * chan, :] = block


def bands_kernel(front_ref, back_ref, bands_ref, back_bands_ref):
    rows, width = front_ref.shape[0], front_ref.shape[1] // 9
    back_rows, back_width = back_ref.shape[0], back_ref.shape[1] // 9
    for t in range(9):
        block = front_ref[:, t * width : (t + 1) * width].astype(F32)
        for q in range(6):
            moved = pltpu.roll(block, q * back_rows, 1) if q else block
            bands_ref[q * rows : (q + 1) * rows, t * width : (t + 1) * width] = moved.astype(BF16)
        block = back_ref[:, t * back_width : (t + 1) * back_width].astype(F32)
        for q in range(4):
            moved = pltpu.roll(block, q * rows, 1) if q else block
            back_bands_ref[
                q * back_rows : (q + 1) * back_rows, t * back_width : (t + 1) * back_width
            ] = moved.astype(BF16)


def band_inputs(w_sub, in_chan):
    out_chan = w_sub.shape[0]
    taps = w_sub.reshape(out_chan, 3, 3, 3, in_chan)
    front = taps.transpose(0, 1, 3, 2, 4).reshape(out_chan, 9, 3 * in_chan)
    front = jnp.pad(front, ((0, 0), (0, 0), (0, 5 * in_chan)))
    back = taps[:, ::-1, ::-1].transpose(4, 1, 3, 2, 0).reshape(in_chan, 9, 3 * out_chan)
    back = jnp.pad(back, ((0, 0), (0, 0), (0, 3 * out_chan)))
    return front.reshape(out_chan, -1), back.reshape(in_chan, -1)


def rows_kernel(sides_ref, first_ref, second_ref, gf_ref, gs_ref, out_first_ref, out_second_ref):
    odd_x, odd_y = sides_ref[0] != 0, sides_ref[1] != 0
    half = first_ref.shape[0] // 2
    low, high = sided(odd_x, first_ref[...], second_ref[...])
    below, above = sided(odd_x, gf_ref[...], gs_ref[...])
    for n, block in enumerate((below, low, high, above)):
        own = slice(n * half, (n + 1) * half)
        out_first_ref[own, :], out_second_ref[own, :] = sided(odd_y, block[:half], block[half:])


def columns_kernel(
    chan, sides_ref, first_ref, second_ref, gf_ref, gs_ref, yf_ref, ys_ref, front_ref, rear_ref, swap_ref
):
    odd_x, odd_y, place = sides_ref[0] != 0, sides_ref[1] != 0, sides_ref[2]
    low, high = sided(odd_x, first_ref[...], second_ref[...])
    below, above = sided(odd_x, gf_ref[...], gs_ref[...])
    left, right = sided(odd_y, yf_ref[...], ys_ref[...])
    for n, own in enumerate((below, low, high, above)):
        for p in range(2):
            for y in range(8):
                if y in (0, 1, 6, 7):
                    got = left if y < 2 else right
                    row = (n * 4 + p * 2 + y % 2) * chan
                else:
                    got = own
                    row = (((y - 2) // 2) * 4 + p * 2 + y % 2) * chan
                block = got[row : row + chan]
                to = ((n * 2 + p) * 8 + y) * chan
                front_ref[to : to + chan, :] = block[:, :LANES]
                rear_ref[to : to + chan, :] = block[:, LANES:]
                swap_ref[to : to + chan, :] = jnp.where(
                    place == 0, block[:, LANES:], block[:, :LANES]
                )


def shifted(low, high, before, after, step):
    lane = lax.broadcasted_iota(jnp.int32, low.shape, 1)
    if step > 0:
        turned = [pltpu.roll(tile.astype(F32), LANES - 1, 1) for tile in (low, high, after)]
        edge = lane == LANES - 1
        tiles = [jnp.where(edge, turned[1], turned[0]), jnp.where(edge, turned[2], turned[1])]
    else:
        turned = [pltpu.roll(tile.astype(F32), 1, 1) for tile in (before, low, high)]
        edge = lane == 0
        tiles = [jnp.where(edge, turned[0], turned[1]), jnp.where(edge, turned[1], turned[2])]
    return tiles[0].astype(BF16), tiles[1].astype(BF16)


def keep(tile, wanted):
    return jnp.where(wanted, tile, jnp.zeros_like(tile))


def to_rows(columns):
    lane = lax.broadcasted_iota(jnp.int32, (LANES, LANES), 1)
    wide = jnp.zeros((LANES, LANES), F32)
    for n, column in enumerate(columns):
        tall = jnp.concatenate([column, jnp.zeros((LANES - column.shape[0], 1), F32)], axis=0)
        wide = jnp.where(lane == n, tall, wide)
    return wide.T[:8, :]


def to_columns(rows, chan):
    wide = jnp.concatenate(rows + [jnp.zeros((LANES - len(rows), LANES), F32)], axis=0).T
    return [wide[:chan, n : n + 1] for n in range(len(rows))]


def conv_kernel(
    only_two, sides_ref, low_ref, high_ref, before_ref, after_ref, bands_ref, acts_ref,
    hidden_ref, stack_ref, stats_ref, hidden, stack, sems,
):
    rows = low_ref.shape[0] // 8
    depth = acts_ref.shape[1]
    wide = bands_ref.shape[0]
    chan = wide // 6
    place = sides_ref[2]
    kept = []
    for x in range(8):
        own = slice(x * rows, (x + 1) * rows)
        low, high = low_ref[own, :], high_ref[own, :]
        before, after = before_ref[own, :], after_ref[own, :]
        if only_two:
            before, after = keep(before, place != 0), keep(after, place == 0)
        for n, step in enumerate((-1, 0, 1)):
            tiles = (low, high) if step == 0 else shifted(low, high, before, after, step)
            to = slice((x * 3 + n) * rows, (x * 3 + n + 1) * rows)
            stack[to, :LANES] = tiles[0]
            stack[to, LANES:] = tiles[1]
        if 1 <= x <= 6:
            kept.append(
                started(
                    stack.at[rows_of(x, 3 * rows), :],
                    stack_ref.at[rows_of(x - 1, 3 * rows), :],
                    sems.at[x - 1],
                )
            )
    total = jnp.zeros((chan, depth), F32)
    for p in range(6):
        first = p * 3 * rows
        out = jnp.dot(
            bands_ref[...], stack[first : first + 9 * rows, :], preferred_element_type=F32
        )
        for q in range(6):
            block = out[q * chan : (q + 1) * chan] * acts_ref[p * 6 + q : p * 6 + q + 1, :]
            hidden[p * wide + q * chan : p * wide + (q + 1) * chan, :] = block
            if 1 <= p <= 4 and 1 <= q <= 4:
                total = total + block
        own = rows_of(p, wide)
        kept.append(started(hidden.at[own, :], hidden_ref.at[own, :], sems.at[6 + p]))
    count = jnp.zeros((1, depth), F32)
    for p in range(1, 5):
        for q in range(1, 5):
            count = count + acts_ref[p * 6 + q : p * 6 + q + 1, :]
    count = jnp.sum(count, axis=1, keepdims=True)
    total = jnp.sum(total, axis=1, keepdims=True)
    mean = total / jnp.maximum(count, 1.0)
    squares = jnp.zeros((chan, depth), F32)
    for p in range(1, 5):
        for q in range(1, 5):
            row = p * wide + q * chan
            centred = (hidden[row : row + chan, :] - mean) * acts_ref[p * 6 + q : p * 6 + q + 1, :]
            squares = squares + centred * centred
    squares = jnp.sum(squares, axis=1, keepdims=True)
    packed = to_rows([total, squares, jnp.broadcast_to(count, (chan, 1))])
    for d in range(stats_ref.shape[0]):
        stats_ref[d] = packed
    for copy in kept:
        copy.wait()


def merged_stats(stats_ref):
    totals, squares, counts = stats_ref[:, 0, :], stats_ref[:, 1, :], stats_ref[:, 2, :]
    count = jnp.sum(counts, axis=0, keepdims=True)
    average = jnp.sum(totals, axis=0, keepdims=True) / count
    off = totals / jnp.maximum(counts, 1.0) - average
    spread = jnp.sum(squares + counts * off * off, axis=0, keepdims=True)
    return count, average, lax.rsqrt(spread / count + EPS)


def norm_kernel(
    stats_ref, params_ref, hidden_ref, wide_ref, acts_ref, down_ref, pre_ref, out_ref, sums_ref,
    hidden, wide, acts, up, fine, pre, outs, sems,
):
    chan = hidden.shape[0] // 36
    depth = acts.shape[1]
    got_acts = started(acts_ref, acts, sems.at[0])
    got_wide = started(wide_ref, wide, sems.at[1])
    got = []
    for p in range(6):
        own = rows_of(p, 6 * chan)
        got.append(started(hidden_ref.at[own, :], hidden.at[own, :], sems.at[2 + p]))
    coarse_z = lax.broadcasted_iota(jnp.int32, (LANES, 2 * depth), 0)
    fine_z = lax.broadcasted_iota(jnp.int32, (LANES, 2 * depth), 1)
    child = jnp.where(fine_z < depth, 0, 1)
    spread = (2 * coarse_z + child == fine_z - child * depth).astype(BF16)
    got_wide.wait()
    up[...] = jnp.dot(wide[...], spread, preferred_element_type=F32).astype(BF16)
    for x in range(4):
        for y in range(4):
            own = slice((x * 4 + y) * chan, (x * 4 + y + 1) * chan)
            both = jnp.concatenate([up[own, :depth], up[own, depth:]], axis=0)
            for a in range(2):
                p = 2 * x + a - 1
                if not 0 <= p < 6:
                    continue
                cols = [b for b in range(2) if 0 <= 2 * y + b - 1 < 6]
                first = (a * 2 + cols[0]) * chan
                grads = jnp.dot(
                    down_ref[first : first + len(cols) * chan, :], both, preferred_element_type=F32
                )
                row = (p * 6 + 2 * y + cols[0] - 1) * chan
                fine[row : row + len(cols) * chan, :] = grads
    count, average, inverse = merged_stats(stats_ref)
    full = (chan, LANES)
    average, inverse, gain, shift = [
        jnp.broadcast_to(column, full)
        for column in to_columns([average, inverse, params_ref[0:1, :], params_ref[1:2, :]], chan)
    ]
    sum_shift = jnp.zeros((chan, LANES), F32)
    sum_gain = jnp.zeros((chan, LANES), F32)
    kept = []
    got_acts.wait()
    for p in range(6):
        got[p].wait()
        for q in range(6):
            row = (p * 6 + q) * chan
            for half in range(depth // LANES):
                lanes = slice(half * LANES, (half + 1) * LANES)
                act = acts[p * 6 + q : p * 6 + q + 1, lanes]
                normed = (hidden[row : row + chan, lanes] - average) * inverse
                x = gain * normed + shift
                square = x * x
                bent = jnp.tanh(GELU_SCALE * (x + GELU_CUBE * (square * x)))
                cdf = 0.5 + 0.5 * bent
                slope = cdf + (0.5 * x) * (1.0 - bent * bent) * (
                    GELU_SCALE + (3.0 * GELU_CUBE * GELU_SCALE) * square
                )
                grad = (act * slope) * fine[row : row + chan, lanes]
                pre[row : row + chan, lanes] = grad
                if 1 <= p <= 4 and 1 <= q <= 4:
                    sum_shift = sum_shift + grad
                    sum_gain = sum_gain + grad * normed
                    to = ((p - 1) * 4 + q - 1) * chan
                    outs[to : to + chan, lanes] = (x * cdf * act).astype(BF16)
        own = rows_of(p, 6 * chan)
        kept.append(started(pre.at[own, :], pre_ref.at[own, :], sems.at[8 + p]))
    kept.append(started(outs, out_ref, sems.at[14]))
    sums = to_rows(
        [jnp.sum(sum_shift, axis=1, keepdims=True), jnp.sum(sum_gain, axis=1, keepdims=True)]
    )
    for d in range(sums_ref.shape[0]):
        sums_ref[d] = sums
    for copy in kept:
        copy.wait()


def down_kernel(out_ref, grad_ref, mask_ref, down_ref, coarse_ref, raw_ref, stack):
    depth = out_ref.shape[1]
    chan = grad_ref.shape[0] // 4
    source = lax.broadcasted_iota(jnp.int32, (depth, depth), 0)
    target = lax.broadcasted_iota(jnp.int32, (depth, depth), 1)
    wanted = jnp.where(target < LANES, 2 * target, 2 * (target - LANES) + 1)
    sort = (source == wanted).astype(BF16)
    for x in range(2):
        for y in range(2):
            for a in range(2):
                for b in range(2):
                    row = ((2 * x + a) * 4 + 2 * y + b) * chan
                    parted = jnp.dot(
                        out_ref[row : row + chan, :], sort, preferred_element_type=F32
                    ).astype(BF16)
                    lanes = slice((x * 2 + y) * LANES, (x * 2 + y + 1) * LANES)
                    to = (a * 4 + b * 2) * chan
                    stack[to : to + chan, lanes] = parted[:, :LANES]
                    stack[to + chan : to + 2 * chan, lanes] = parted[:, LANES:]
    sums = jnp.dot(down_ref[...], stack[...], preferred_element_type=F32)
    for n in range(4):
        coarse_ref[n] = (sums[:, n * LANES : (n + 1) * LANES] * mask_ref[n : n + 1, :]).astype(
            BF16
        )
    grads = jnp.concatenate([grad_ref[n * chan : (n + 1) * chan, :] for n in range(4)], axis=1)
    raw = lax.dot_general(grads, stack[...], NT, preferred_element_type=F32)
    for n in range(4):
        raw_ref[n * chan : (n + 1) * chan, :] = raw[:, n * LANES : (n + 1) * LANES]


def hidden_grad_kernel(
    in_chan, sides_ref, stats_ref, sums_ref, params_ref, hidden_ref, pre_ref, acts_ref, stack_ref,
    raw_ref, front_ref, rear_ref, swap_ref, small_ref, out_ref,
    stats, hidden, pre, acts, stack, raw, front, rear, acc, sems,
):
    chan = hidden.shape[0] // 36
    place = sides_ref[2]
    got_stats = started(stats_ref, stats, sems.at[0])
    got_acts = started(acts_ref, acts, sems.at[1])
    got = []
    for p in range(6):
        own = rows_of(p, 6 * chan)
        got.append(
            (
                started(hidden_ref.at[own, :], hidden.at[own, :], sems.at[4 + p]),
                started(pre_ref.at[own, :], pre.at[own, :], sems.at[10 + p]),
            )
        )
    got_stack = started(stack_ref, stack, sems.at[2])
    got_raw = started(raw_ref, raw, sems.at[3])
    raw_shift = jnp.sum(sums_ref[:, 0, :], axis=0, keepdims=True)
    raw_gain = jnp.sum(sums_ref[:, 1, :], axis=0, keepdims=True)
    got_stats.wait()
    count, average, inverse = merged_stats(stats)
    scale = lax.rsqrt(count)
    small_ref[...] = jnp.concatenate(
        [raw_shift * scale, raw_gain * scale, scale, jnp.zeros((5, LANES), F32)], axis=0
    )
    columns = [average, inverse, raw_shift / count, raw_gain / count, params_ref[0:1, :]]
    average, inverse, mean_shift, mean_gain, gain = [
        jnp.broadcast_to(column, (chan, LANES)) for column in to_columns(columns, chan)
    ]
    weight = gain * inverse
    got_acts.wait()
    kept = []
    for p in range(6):
        for copy in got[p]:
            copy.wait()
        for n in range(6 * p, 6 * p + 6):
            row = n * chan
            tiles = []
            for half, held in enumerate((front, rear)):
                lanes = slice(half * LANES, (half + 1) * LANES)
                act = acts[n : n + 1, lanes]
                normed = (hidden[row : row + chan, lanes] - average) * inverse
                grad = pre[row : row + chan, lanes] - (mean_shift + normed * mean_gain)
                tiles.append(((act * weight) * grad).astype(BF16))
                held[row : row + chan, :] = tiles[-1]
            swap_ref[row : row + chan, :] = jnp.where(place == 0, tiles[1], tiles[0])
        own = rows_of(p, 6 * chan)
        kept.append(started(front.at[own, :], front_ref.at[own, :], sems.at[16 + p]))
        kept.append(started(rear.at[own, :], rear_ref.at[own, :], sems.at[22 + p]))
    got_stack.wait()
    got_raw.wait()
    rows = stack.shape[0] // 6
    band = rows // 3
    for p in range(4):
        own = slice(((p + 1) * 6 + 1) * chan, ((p + 1) * 6 + 5) * chan)
        grads = jnp.concatenate([front[own, :], rear[own, :]], axis=1)
        for dx in range(3):
            first = (p + dx) * rows
            part = lax.dot_general(
                stack[first : first + rows, :], grads, NT, preferred_element_type=F32
            )
            if p == 0:
                acc[dx] = part
            else:
                acc[dx] += part
    low = lax.broadcasted_iota(jnp.int32, (in_chan, LANES), 1) < chan
    for dx in range(3):
        for dy in range(3):
            for dz in range(3):
                blocks = []
                for q in range(4):
                    row = dz * band + (q + 1 + dy) * in_chan
                    lanes = slice((q // 2) * LANES, (q // 2 + 1) * LANES)
                    blocks.append(acc[dx, row : row + in_chan, lanes])
                both = jnp.where(low, blocks[0] + blocks[2], blocks[1] + blocks[3])
                folded = (both + pltpu.roll(both, chan, 1)).astype(out_ref.dtype)
                tap = (dx * 3 + dy) * 3 + dz
                if tap < 16:
                    out_ref[tap * in_chan : (tap + 1) * in_chan, :chan] = folded[:, :chan]
                else:
                    to = (tap - 16) * in_chan
                    out_ref[to : to + in_chan, chan:] = folded[:, chan:]
    out_ref[11 * in_chan : 16 * in_chan, chan:] = jnp.zeros(
        (5 * in_chan, LANES - chan), out_ref.dtype
    )
    tail = 16 * in_chan
    out_ref[tail : tail + 4 * chan, :] = raw[...].astype(out_ref.dtype)
    left = out_ref.shape[0] - tail - 4 * chan
    if left:
        out_ref[tail + 4 * chan :, :] = jnp.zeros((left, LANES), out_ref.dtype)
    for copy in kept:
        copy.wait()


def point_grad_kernel(
    only_two, halves, chan, sides_ref, front_ref, rear_ref, before_ref, after_ref, bands_ref, act_ref,
    tags_ref, out_ref, front, rear, bands, acts, tags_held, stack, cells, sems,
):
    rows = front.shape[0] // 6
    groups, depth = acts.shape
    place_z = sides_ref[2]
    got = []
    for x in range(6):
        own = rows_of(x, rows)
        got.append(
            (
                started(front_ref.at[own, :], front.at[own, :], sems.at[3 + x]),
                started(rear_ref.at[own, :], rear.at[own, :], sems.at[9 + x]),
            )
        )
    late = [
        started(bands_ref, bands, sems.at[0]),
        started(act_ref, acts, sems.at[1]),
        started(tags_ref, tags_held, sems.at[2]),
    ]
    for x in range(6):
        for copy in got[x]:
            copy.wait()
        own = slice(x * rows, (x + 1) * rows)
        low, high = front[own, :], rear[own, :]
        before, after = before_ref[own, :], after_ref[own, :]
        if only_two:
            before, after = keep(before, place_z != 0), keep(after, place_z == 0)
        for n, step in enumerate((1, 0, -1)):
            tiles = (low, high) if step == 0 else shifted(low, high, before, after, step)
            to = slice((x * 3 + n) * rows, (x * 3 + n + 1) * rows)
            stack[to, :LANES] = tiles[0]
            stack[to, LANES:] = tiles[1]
    for copy in late:
        copy.wait()
    for p in range(4):
        first = p * 3 * rows
        grid = jnp.dot(
            bands[...], stack[first : first + 9 * rows, :], preferred_element_type=F32
        )
        for q in range(4):
            k = p * 4 + q
            cells[k * chan : (k + 1) * chan, :] = (
                grid[q * chan : (q + 1) * chan] * acts[k : k + 1, :]
            ).astype(BF16)
    place = lax.broadcasted_iota(jnp.int32, (depth, LANES), 0).astype(F32)

    def from_cells(d):
        tags = tags_held[d]
        lows = [tags[halves + h : halves + h + 1, :] for h in range(halves)]
        hot = [jnp.where(place == low, 1.0, 0.0).astype(BF16) for low in lows]
        hot = jnp.concatenate(hot, axis=1)
        found = jnp.dot(cells[...], hot, preferred_element_type=F32)
        for h in range(halves):
            group = jnp.broadcast_to(tags[h : h + 1, :], (chan, LANES))
            lanes = slice(h * LANES, (h + 1) * LANES)
            out = jnp.zeros((chan, LANES), F32)
            for k in range(groups):
                out = jnp.where(group == k, found[k * chan : (k + 1) * chan, lanes], out)
            out_ref[d, h * chan : (h + 1) * chan, :] = out.astype(BF16)

    def step(s, carry):
        for j in range(4):
            from_cells(4 * s + j)
        return carry

    lax.fori_loop(0, tags_held.shape[0] // 4, step, 0)


def piece_kernel(parts_ref, out_ref):
    out_ref[...] = jnp.sum(parts_ref[...].astype(F32), axis=0).astype(BF16)


def gathered(piece, names, sizes):
    for name, size in zip(names, sizes):
        pairs = [[(i, i ^ k) for i in range(size)] for k in range(1, size)]
        parts = [piece] + [lax.ppermute(piece, name, pair) for pair in pairs]
        piece = jnp.concatenate(parts, axis=0)
    return piece


def weights_out(rows, small_ref, in_chan, sub_ref, down_ref):
    chan = down_ref.shape[0]
    scale = small_ref[2:3, 0:1]
    for n in range(4):
        turned = rows(n).T * scale
        sub_ref[:, n * LANES : (n + 1) * LANES] = turned[:chan]
        left = sub_ref.shape[1] - 16 * in_chan - n * LANES
        if left > 0:
            width = min(left, LANES)
            first = 16 * in_chan + n * LANES
            sub_ref[:, first : first + width] = turned[chan:, :width]
    for n in range(2):
        both = rows(4 + n) * scale
        down_ref[:, 2 * n * LANES : (2 * n + 1) * LANES] = both[:chan]
        down_ref[:, (2 * n + 1) * LANES : (2 * n + 2) * LANES] = both[chan:]


def points_kernel(halves, chan, got_ref, points_ref):
    for d in range(got_ref.shape[0]):
        block = got_ref[d]
        for h in range(halves):
            first = (d * halves + h) * LANES
            points_ref[:, first : first + LANES] = block[h * chan : (h + 1) * chan, :]


def weights_kernel(chan, sizes, at_ref, got_ref, small_ref, sub_ref, down_ref, flat):
    nz, nx, ny = sizes
    piece = got_ref.shape[0] // (nx * ny * nz)
    for y in range(ny):
        for x in range(nx):
            for z in range(nz):
                n = (y * nx + x) * nz + z
                device = ((at_ref[1] ^ x) * ny + (at_ref[2] ^ y)) * nz + (at_ref[0] ^ z)
                own = pl.ds(pl.multiple_of(device * piece, 8), piece)
                flat[own, :] = got_ref[n * piece : (n + 1) * piece, :].astype(F32)
    weights_out(lambda n: flat[n * LANES : (n + 1) * LANES, :], small_ref, chan, sub_ref, down_ref)


def on_device(
    point_feats, voxel_ids, send_counts, active, w_sub, w_down, bn_gain, bn_shift, cotangent
):
    in_chan, slot_total = point_feats.shape
    devices = send_counts.shape[1]
    slot_cap = slot_total // devices
    size_x, size_y, size_z = active.shape
    groups = size_x * size_y
    out_chan = w_sub.shape[0]
    only_two = lax.axis_size("gz") == 2
    sides = jnp.stack(
        [lax.axis_index("gx") % 2, lax.axis_index("gy") % 2, lax.axis_index("gz")]
    ).astype(jnp.int32)
    aligned = slot_cap % LANES == 0
    halves = slot_cap // LANES if aligned else 1
    rows_x, rows_6, rows_64 = groups // 2 * in_chan, 36 * out_chan, 64 * in_chan
    wide, back_wide = 6 * out_chan, 4 * in_chan

    if aligned:
        payload = local_call(
            functools.partial(pack_kernel, halves, groups, size_z),
            [((devices, halves * in_chan + 8, LANES), BF16)],
            send_counts, point_feats, voxel_ids.reshape(-1, LANES),
            scratch=[((in_chan, slot_total), BF16), ((devices * halves, LANES), jnp.int32)],
            smem=(0,), hbm=(1, 2), copies=5, moved=2e6,
        )[0]
        recv = everyone(payload)
    else:
        payload = pack_plain(point_feats, voxel_ids, send_counts, groups, size_z)
        together = LANES // slot_cap
        recv = everyone(payload)
        recv = recv.reshape(devices // together, together, in_chan + 8, slot_cap)
        recv = recv.transpose(0, 2, 1, 3).reshape(devices // together, in_chan + 8, LANES)
    chunks = recv.shape[0]

    acts = active.reshape(groups, size_z).astype(F32)
    params = jnp.pad(jnp.stack([bn_gain, bn_shift]), ((0, 6), (0, LANES - out_chan)))
    front, back = band_inputs(w_sub, in_chan)
    cot = cotangent.transpose(1, 2, 0, 3)
    *ends, grad_c, coarse_mask = local_call(
        coarse_kernel,
        [((2 * out_chan + 16, LANES), BF16)] * 2
        + [((4 * out_chan, LANES), BF16), ((8, LANES), F32)],
        sides, acts, cot, smem=(0,), moved=2e5,
    )
    cot_x = swaps(*ends, "gx")
    ends = local_call(
        coarse_rows_kernel,
        [((4 * out_chan + 16, LANES), BF16)] * 2,
        sides, acts, grad_c, *cot_x, smem=(0,), moved=2e5,
    )
    cot_y = swaps(*ends, "gy")
    by_child = (
        w_down.reshape(out_chan, 4, 2, out_chan)
        .transpose(1, 3, 2, 0)
        .reshape(4 * out_chan, 2 * out_chan)
    )
    recv, acts, grad_c, cot_x, cot_y, by_child, front, back, params = lax.optimization_barrier(
        (recv, acts, grad_c, cot_x, cot_y, by_child, front, back, params)
    )

    per_step = min(chunks, 16 // halves)
    *mine, tags = local_call(
        functools.partial(scatter_kernel, halves, in_chan, size_y),
        [((rows_x, size_z), BF16)] * 2 + [((chunks, 8, LANES), F32)],
        sides, recv, acts,
        scratch=[
            ((groups * in_chan, size_z), F32),
            ((groups * in_chan, per_step * halves * LANES), BF16),
            ((size_z, per_step * halves * LANES), BF16),
            ((chunks, 8, LANES), F32),
        ],
        smem=(0,), hbm_outs=(2,), copies=1, moved=2e7,
    )
    got_x = swaps(*mine, "gx")
    grad_wide, acts_wide = local_call(
        wide_kernel,
        [((16 * out_chan, LANES), BF16), ((40, size_z), F32)],
        sides, acts, grad_c, *cot_x, *cot_y,
        smem=(0,), hbm_outs=(), moved=5e5,
    )
    got_x, grad_wide, acts_wide = lax.optimization_barrier((got_x, grad_wide, acts_wide))
    ends = local_call(
        rows_kernel,
        [((2 * rows_x, size_z), BF16)] * 2,
        sides, *mine, *got_x, smem=(0,), moved=1e6,
    )
    got_y = swaps(*ends, "gy")
    bands_shape, back_shape = (wide, 9 * 8 * in_chan), (back_wide, 9 * 6 * out_chan)
    bands, back_bands = local_call(
        bands_kernel,
        [(bands_shape, BF16), (back_shape, BF16)],
        front, back, hbm_outs=(), moved=4e6,
    )
    got_y, bands, back_bands = lax.optimization_barrier((got_y, bands, back_bands))
    tile_low, tile_high, swap = local_call(
        functools.partial(columns_kernel, in_chan),
        [((rows_64, LANES), BF16)] * 3,
        sides, *mine, *got_x, *got_y, smem=(0,), moved=3e6,
    )
    before, after = z_exchange(tile_low, tile_high, swap)

    stats_shape = (devices, 8, LANES)
    stack_shape = (rows_64 // 8 * 6 * 3, size_z)
    hidden, stack, stats = local_call(
        functools.partial(conv_kernel, only_two),
        [((rows_6, size_z), F32), (stack_shape, BF16), (stats_shape, F32)],
        sides, tile_low, tile_high, before, after, bands, acts_wide,
        scratch=[((rows_6, size_z), F32), ((3 * rows_64, size_z), BF16)],
        smem=(0,), hbm_outs=(0, 1), copies=12, moved=2e7,
    )
    stats = everyone(stats)
    grad_pre, fine_out, sums = local_call(
        norm_kernel,
        [((rows_6, size_z), F32), ((groups * out_chan, size_z), BF16), (stats_shape, F32)],
        stats, params, hidden, grad_wide, acts_wide, by_child,
        scratch=[
            ((rows_6, size_z), F32),
            ((16 * out_chan, LANES), BF16),
            ((40, size_z), F32),
            ((16 * out_chan, 2 * size_z), BF16),
            ((rows_6, size_z), F32),
            ((rows_6, size_z), F32),
            ((groups * out_chan, size_z), BF16),
        ],
        hbm=(2, 3, 4), hbm_outs=(0, 1), copies=15, moved=1e7,
    )
    sums = everyone(sums)
    coarse, raw_down = local_call(
        down_kernel,
        [((4, out_chan, LANES), BF16), ((4 * out_chan, LANES), F32)],
        fine_out, grad_c, coarse_mask, w_down,
        scratch=[((8 * out_chan, 4 * LANES), BF16)], moved=5e6,
    )
    half_x, half_y, half_z = size_x // 2, size_y // 2, size_z // 2
    coarse_out = coarse.reshape(half_x, half_y, out_chan, half_z).transpose(2, 0, 1, 3)

    piece = -(-(16 * in_chan + 4 * out_chan) // devices)
    piece = -(-piece // 8) * 8
    grad_low, grad_high, grad_swap, small, parts = local_call(
        functools.partial(hidden_grad_kernel, in_chan),
        [((rows_6, LANES), BF16)] * 3 + [((8, LANES), F32), ((devices * piece, LANES), BF16)],
        sides, stats, sums, params, hidden, grad_pre, acts_wide, stack, raw_down,
        scratch=[
            (stats_shape, F32),
            ((rows_6, size_z), F32),
            ((rows_6, size_z), F32),
            ((40, size_z), F32),
            (stack_shape, BF16),
            ((4 * out_chan, LANES), F32),
            ((rows_6, LANES), BF16),
            ((rows_6, LANES), BF16),
            ((3, 24 * in_chan, 4 * out_chan), F32),
        ],
        smem=(0,), hbm=(1, 4, 5, 6, 7, 8), hbm_outs=(0, 1), copies=28, moved=2e7,
    )
    grad_before, grad_after = z_exchange(grad_low, grad_high, grad_swap)
    parts = everyone(parts.reshape(devices, piece, LANES))

    points = local_call(
        functools.partial(point_grad_kernel, only_two, halves, in_chan),
        [((chunks, halves * in_chan, LANES), BF16)],
        sides, grad_low, grad_high, grad_before, grad_after, back_bands, acts, tags,
        scratch=[
            ((rows_6, LANES), BF16),
            ((rows_6, LANES), BF16),
            (back_shape, BF16),
            ((groups, size_z), F32),
            ((chunks, 8, LANES), F32),
            ((3 * rows_6, size_z), BF16),
            ((groups * in_chan, size_z), BF16),
        ],
        smem=(0,), hbm=(1, 2, 5, 6, 7), copies=15, moved=2e7,
    )[0]
    parts, points = lax.optimization_barrier((parts, points))
    if aligned:
        returned = local_call(
            functools.partial(points_kernel, halves, in_chan),
            [((in_chan, slot_total), BF16)],
            everyone(points), moved=1e6,
        )[0]
    else:
        points = points.reshape(chunks, in_chan, together, slot_cap).transpose(0, 2, 1, 3)
        returned = everyone(points.reshape(devices, in_chan, slot_cap))
        returned = returned.transpose(1, 0, 2).reshape(in_chan, slot_total)

    names = ("gz", "gx", "gy")
    sizes = tuple(lax.axis_size(name) for name in names)
    at = jnp.stack([lax.axis_index(name) for name in names]).astype(jnp.int32)
    summed = local_call(piece_kernel, [((piece, LANES), BF16)], parts, moved=2e5)[0]
    raw_sub, raw_down = local_call(
        functools.partial(weights_kernel, in_chan, sizes),
        [((out_chan, 27 * in_chan), F32), ((out_chan, 8 * out_chan), F32)],
        at, gathered(summed, names, sizes), small,
        scratch=[((devices * piece, LANES), F32)], smem=(0,), moved=5e5,
    )
    return (
        coarse_out,
        returned,
        raw_sub,
        raw_down,
        small[1, :out_chan],
        small[0, :out_chan],
    )


def solution(mesh):
    in_specs = (
        P(None, AXES),
        P(AXES),
        P(AXES, None),
        P("gx", "gy", "gz"),
        P(),
        P(),
        P(),
        P(),
        P(None, "gx", "gy", "gz"),
    )
    out_specs = (P(None, "gx", "gy", "gz"), P(None, AXES), P(), P(), P(), P())
    return jax.shard_map(
        on_device, mesh=mesh, in_specs=in_specs, out_specs=out_specs, check_vma=False
    )
```

time: 173 us -> 135 us (0.78)
  waiting for transfers between devices: 72.1 us -> 36.6 us
  local copies, waits for them, and re-layouts: 30.1 us -> 6.18 us
  blocking collectives: 0 us -> 16.5 us
  Pallas kernels: 32.6 us -> 39.6 us
    all_to_all x5 -> x4, waiting for transfers between devices: 47.8 us -> 10.9 us  [everyone(): return lax.all_to_all(block, AXES, split_axis=0, concat_axis=0, tiled=True)]
    unnamed x89 -> x39, local copies, waits for them, and re-layouts: 26.5 us -> 4.1 us
    all_to_all x0 -> x1, blocking collectives: none -> 16.5 us  [everyone(): return lax.all_to_all(block, AXES, split_axis=0, concat_axis=0, tiled=True)]
    pallas_call x16, Pallas kernels: 32.6 us -> 39.6 us  [local_call(): pl.pallas_call(kernel, out_shape=[pltpu.HBM(shape, kind) if i in hbm_outs...]
    all_to_all x5 -> x4, starting transfers between devices: 21.1 us -> 18.4 us  [everyone(): return lax.all_to_all(block, AXES, split_axis=0, concat_axis=0, tiled=True)]
    ppermute x8 -> x15, waiting for transfers between devices: 22.1 us -> 23.8 us  [the longest x8 13.3 us: swaps(): got.append(lax.ppermute(block, axis, pairs + [(j, i) for i, j in pairs]))]
    ppermute x8 -> x15, starting transfers between devices: 14.4 us -> 15 us  [the longest x7 8.45 us: gathered(): parts = [piece] + [lax.ppermute(piece, name, pair) for pair in pairs]]
  transfers between devices with their start and end apart: 15 -> 21, of which waited for: 11 -> 10; matrix products, arithmetic and copies ran while one was open for 3% -> 2% of each run, Pallas kernels for 9% -> 10%
where the time goes in v2:
time: 135 us; the launch traced here: 134 us
  Pallas kernels  39.6 us (29%)
  waiting for transfers between devices  36.6 us (27%)
  starting transfers between devices  33.9 us (25%)
  blocking collectives  16.5 us (12%)
  local copies, waits for them, and re-layouts  6.18 us (5%)
    pallas_call x16, Pallas kernels, local_call(): pl.pallas_call(kernel, out_shape=[pltpu.HBM(shape, kind) if i in hbm_outs...  39.6 us
    all_to_all x4, starting transfers between devices, everyone(): return lax.all_to_all(block, AXES, split_axis=0, concat_axis=0, tiled=True)  18.4 us
    all_to_all x1, blocking collectives, everyone(): return lax.all_to_all(block, AXES, split_axis=0, concat_axis=0, tiled=True)  16.5 us
    ppermute x8, waiting for transfers between devices, swaps(): got.append(lax.ppermute(block, axis, pairs + [(j, i) for i, j in pairs]))  13.3 us
    all_to_all x4, waiting for transfers between devices, everyone(): return lax.all_to_all(block, AXES, split_axis=0, concat_axis=0, tiled=True)  10.9 us
    ppermute x7, waiting for transfers between devices, gathered(): parts = [piece] + [lax.ppermute(piece, name, pair) for pair in pairs]  10.4 us
    ppermute x7, starting transfers between devices, gathered(): parts = [piece] + [lax.ppermute(piece, name, pair) for pair in pairs]  8.45 us
    ppermute x8, starting transfers between devices, swaps(): got.append(lax.ppermute(block, axis, pairs + [(j, i) for i, j in pairs]))  6.58 us
  transfers between devices with their start and end apart: 21, of which 10 were waited for; matrix products, arithmetic and copies ran while one was open for 2% of the time, Pallas kernels for 10%

profile of v2, /device:TPU:0, one launch (start us, length us, event | category | flops | bytes accessed | tf_op | source)
XLA Modules:
  0.0 134.1 jit_solution(11788132634738947370)
XLA Ops:
  1.3 2.6 %shard_map.136 = bf16[32,72,128]{2,1,0:T(8,128)(2,1)} custom-call(s32[1,32]{1,0:T(1,128)S(1)} %copy-done.8, bf16[32,8192]{1,0:T(8,128)(2,1)} %feats_ref.1, s32[64,128]{1,0:T(8,128)} %bitcast.40), custom_call_target="tpu_custom_call" | custom-call | bytes 2000000 | tf_op jit(solution)/shard_map/pallas_call | solution.py:34
  3.9 7.3 %all-to-all-start = ((bf16[32,72,128]{2,1,0:T(8,128)(2,1)}), bf16[32,72,128]{2,1,0:T(8,128)(2,1)S(1)}, u32[]{:S(2)}, u32[]{:S(2)}) async-start(bf16[32,72,128]{2,1,0:T(8,128)(2,1)} %shard_map.136), calls=%async_computation | async-start | bytes 1179648 | tf_op jit(solution)/shard_map/all_to_all | solution.py:89
  11.4 0.7 shard_map.137
  12.1 1.8 %collective-permute-start = (bf16[144,128]{1,0:T(8,128)(2,1)S(1)}, bf16[144,128]{1,0:T(8,128)(2,1)S(1)}, u32[]{:S(2)}, u32[]{:S(2)}) collective-permute-start(bf16[144,128]{1,0:T(8,128)(2,1)S(1)} %get-tuple-element.61), channel_id=1, source_target_pairs={{0,8},{16,24},{8,0},{24,16},{1,9},{17,25},{9,1},{25,17},{2,10},{18... | collective-permute-start | bytes 110600 | tf_op jit(solution)/shard_map/ppermute | solution.py:70
  16.2 1.5 %collective-permute-done.xf_ref = bf16[144,128]{1,0:T(8,128)(2,1)S(1)} collective-permute-done((bf16[144,128]{1,0:T(8,128)(2,1)S(1)}, bf16[144,128]{1,0:T(8,128)(2,1)S(1)}, u32[]{:S(2)}, u32[]{:S(2)}) %collective-permute-start) | collective-permute-done | bytes 36896 | tf_op jit(solution)/shard_map/ppermute | solution.py:70
  18.2 1.5 %collective-permute-start.2 = (bf16[272,128]{1,0:T(8,128)(2,1)S(1)}, bf16[272,128]{1,0:T(8,128)(2,1)S(1)}, u32[]{:S(2)}, u32[]{:S(2)}) collective-permute-start(bf16[272,128]{1,0:T(8,128)(2,1)S(1)} %get-tuple-element.63), channel_id=1, source_target_pairs={{0,2},{4,6},{2,0},{6,4},{1,3},{5,7},{3,1},{7,5},{8,10},{12,14},{10... | collective-permute-start | bytes 208904 | tf_op jit(solution)/shard_map/ppermute | solution.py:70
  20.5 3.1 %collective-permute-done.2.yf_ref = bf16[272,128]{1,0:T(8,128)(2,1)S(1)} collective-permute-done((bf16[272,128]{1,0:T(8,128)(2,1)S(1)}, bf16[272,128]{1,0:T(8,128)(2,1)S(1)}, u32[]{:S(2)}, u32[]{:S(2)}) %collective-permute-start.2) | collective-permute-done | bytes 69664 | tf_op jit(solution)/shard_map/ppermute | solution.py:70
  23.6 5.4 %all-to-all-done.recv_ref = bf16[32,72,128]{2,1,0:T(8,128)(2,1)S(1)} async-done(((bf16[32,72,128]{2,1,0:T(8,128)(2,1)}), bf16[32,72,128]{2,1,0:T(8,128)(2,1)S(1)}, u32[]{:S(2)}, u32[]{:S(2)}) %all-to-all-start) | async-done | bytes 589856 | tf_op jit(solution)/shard_map/all_to_all | solution.py:89
  29.0 4.7 %shard_map.139 = (bf16[256,256]{1,0:T(8,128)(2,1)S(1)}, bf16[256,256]{1,0:T(8,128)(2,1)S(1)}, f32[32,8,128]{2,1,0:T(8,128)}) custom-call(s32[3]{0:T(128)S(1)} %pad_add_fusion.sides_ref, bf16[32,72,128]{2,1,0:T(8,128)(2,1)S(1)} %all-to-all-done.recv_ref, f32[16,256]{1,0:T(8,128)S(1)} %convert_element_type.12.act_ref), custom_call_target="tpu_custom_call" | custom-call | bytes 20000000 | tf_op jit(solution)/shard_map/pallas_call | solution.py:34
  35.1 4.0 %collective-permute-done.4.gf_ref = bf16[256,256]{1,0:T(8,128)(2,1)S(1)} collective-permute-done((bf16[256,256]{1,0:T(8,128)(2,1)S(1)}, bf16[256,256]{1,0:T(8,128)(2,1)S(1)}, u32[]{:S(2)}, u32[]{:S(2)}) %collective-permute-start.4) | collective-permute-done | bytes 131104 | tf_op jit(solution)/shard_map/ppermute | solution.py:70
  41.2 1.0 copy-done.1
  42.2 4.8 %collective-permute-done.6.yf_ref = bf16[512,256]{1,0:T(8,128)(2,1)S(1)} collective-permute-done((bf16[512,256]{1,0:T(8,128)(2,1)S(1)}, bf16[512,256]{1,0:T(8,128)(2,1)S(1)}, u32[]{:S(2)}, u32[]{:S(2)}) %collective-permute-start.6) | collective-permute-done | bytes 262176 | tf_op jit(solution)/shard_map/ppermute | solution.py:70
  47.0 0.8 shard_map.143
  47.9 1.9 %collective-permute-done.8.before_ref.after_ref = bf16[2048,128]{1,0:T(8,128)(2,1)S(1)} collective-permute-done((bf16[2048,128]{1,0:T(8,128)(2,1)S(1)}, bf16[2048,128]{1,0:T(8,128)(2,1)S(1)}, u32[]{:S(2)}, u32[]{:S(2)}) %collective-permute-start.8) | collective-permute-done | bytes 524320 | tf_op jit(solution)/shard_map/ppermute | solution.py:84
  49.8 4.9 %shard_map.144 = (f32[2304,256]{1,0:T(8,128)}, bf16[4608,256]{1,0:T(8,128)(2,1)}, f32[32,8,128]{2,1,0:T(8,128)S(1)}) custom-call(s32[3]{0:T(128)S(1)} %pad_add_fusion.sides_ref, bf16[2048,128]{1,0:T(8,128)(2,1)S(1)} %get-tuple-element.86.low_ref, bf16[2048,128]{1,0:T(8,128)(2,1)S(1)} %get-tuple-element.87.high_ref, ...), custom_call_target="tpu_custom_call" | custom-call | bytes 20000000 | tf_op jit(solution)/shard_map/pallas_call | solution.py:34
  54.7 16.5 %all_to_all.25.stats_ref = f32[32,8,128]{2,1,0:T(8,128)S(1)} all-to-all(f32[32,8,128]{2,1,0:T(8,128)S(1)} %get-tuple-element.91), channel_id=1, replica_groups=mesh['gx'=4,'gy'=4,'gz'=2] {'gx','gy','gz'}, dimensions={0} | all-to-all | bytes 262144 | tf_op jit(solution)/shard_map/all_to_all | solution.py:89
  71.2 5.6 %shard_map.145 = (f32[2304,256]{1,0:T(8,128)}, bf16[1024,256]{1,0:T(8,128)(2,1)}, f32[32,8,128]{2,1,0:T(8,128)}) custom-call(f32[32,8,128]{2,1,0:T(8,128)S(1)} %all_to_all.25.stats_ref, f32[8,128]{1,0:T(8,128)S(1)} %select_maximum_fusion.params_ref, f32[2304,256]{1,0:T(8,128)} %get-tuple-element.93.hidden_ref, bf16[1024,128]{1,0:T(8,128)(2,1)} %copy-done.6, ...), custom_call_target="tpu_custom_call" | custom-call | bytes 10000000 | tf_op jit(solution)/shard_map/pallas_call | solution.py:34
  76.8 2.8 %all-to-all-start.2 = ((f32[32,8,128]{2,1,0:T(8,128)}), f32[32,8,128]{2,1,0:T(8,128)S(1)}, u32[]{:S(2)}, u32[]{:S(2)}) async-start(f32[32,8,128]{2,1,0:T(8,128)} %get-tuple-element.99), calls=%async_computation.2 | async-start | bytes 262144 | tf_op jit(solution)/shard_map/all_to_all | solution.py:89
  79.6 1.0 copy-done.3
  80.6 0.8 shard_map.146
  82.1 5.5 %all-to-all-done.2.sums_ref = f32[32,8,128]{2,1,0:T(8,128)S(1)} async-done(((f32[32,8,128]{2,1,0:T(8,128)}), f32[32,8,128]{2,1,0:T(8,128)S(1)}, u32[]{:S(2)}, u32[]{:S(2)}) %all-to-all-start.2) | async-done | bytes 131104 | tf_op jit(solution)/shard_map/all_to_all | solution.py:89
  87.6 6.5 %shard_map.147 = (bf16[2304,128]{1,0:T(8,128)(2,1)}, bf16[2304,128]{1,0:T(8,128)(2,1)}, bf16[2304,128]{1,0:T(8,128)(2,1)S(1)}, f32[8,128]{1,0:T(8,128)S(1)}, bf16[768,128]{1,0:T(8,128)(2,1)}) custom-call(s32[3]{0:T(128)S(1)} %pad_add_fusion.sides_ref, f32[32,8,128]{2,1,0:T(8,128)} %copy-done, f32[32,8,128]{2,1,0:T(8,128)S(1)} %all-to-all-done.2.sums_ref, ...), custom_call_target="tpu_custom_call" | custom-call | bytes 20000000 | tf_op jit(solution)/shard_map/pallas_call | solution.py:34
  94.5 2.6 %all-to-all-start.3 = ((bf16[32,24,128]{2,1,0:T(8,128)(2,1)}), bf16[32,24,128]{2,1,0:T(8,128)(2,1)S(1)}, u32[]{:S(2)}, u32[]{:S(2)}) async-start(bf16[32,24,128]{2,1,0:T(8,128)(2,1)} %bitcast.15), calls=%async_computation.3 | async-start | bytes 393216 | tf_op jit(solution)/shard_map/all_to_all | solution.py:89
  97.9 8.5 %shard_map.148 = bf16[32,64,128]{2,1,0:T(8,128)(2,1)} custom-call(s32[3]{0:T(128)S(1)} %pad_add_fusion.sides_ref, bf16[2304,128]{1,0:T(8,128)(2,1)} %get-tuple-element.104.front_ref, bf16[2304,128]{1,0:T(8,128)(2,1)} %get-tuple-element.105.rear_ref, bf16[2304,128]{1,0:T(8,128)(2,1)S(1)} %collective-permute-done.9.before_ref.after_ref, ...), custom_call_target="tpu_custom_call" | custom-call | bytes 20000000 | tf_op jit(solution)/shard_map/pallas_call | solution.py:34
  106.7 5.8 %all-to-all-start.4 = ((bf16[32,64,128]{2,1,0:T(8,128)(2,1)}), bf16[32,64,128]{2,1,0:T(8,128)(2,1)S(1)}, u32[]{:S(2)}, u32[]{:S(2)}) async-start(bf16[32,64,128]{2,1,0:T(8,128)(2,1)} %shard_map.148), calls=%async_computation.4 | async-start | bytes 1048576 | tf_op jit(solution)/shard_map/all_to_all | solution.py:89
  112.5 2.7 %collective-permute-start.13 = (bf16[48,128]{1,0:T(8,128)(2,1)S(1)}, bf16[48,128]{1,0:T(8,128)(2,1)S(1)}, u32[]{:S(2)}, u32[]{:S(2)}) collective-permute-start(bf16[48,128]{1,0:T(8,128)(2,1)S(1)} %pad_maximum_fusion), channel_id=1, source_target_pairs={{0,24},{8,16},{16,8},{24,0},{1,25},{9,17},{17,9},{25,1},{2,26},{10... | collective-permute-start | bytes 36872 | tf_op jit(solution)/shard_map/ppermute | solution.py:724
  116.1 3.5 %collective-permute-done.11 = bf16[48,128]{1,0:T(8,128)(2,1)S(1)} collective-permute-done((bf16[48,128]{1,0:T(8,128)(2,1)S(1)}, bf16[48,128]{1,0:T(8,128)(2,1)S(1)}, u32[]{:S(2)}, u32[]{:S(2)}) %collective-permute-start.11) | collective-permute-done | bytes 12320 | tf_op jit(solution)/shard_map/ppermute | solution.py:724
  119.7 1.5 %collective-permute-start.14 = (bf16[192,128]{1,0:T(8,128)(2,1)S(1)}, bf16[192,128]{1,0:T(8,128)(2,1)S(1)}, u32[]{:S(2)}, u32[]{:S(2)}) collective-permute-start(bf16[192,128]{1,0:T(8,128)(2,1)S(1)} %get-tuple-element.114), channel_id=1, source_target_pairs={{0,2},{2,0},{4,6},{6,4},{1,3},{3,1},{5,7},{7,5},{8,10},{10,8},{12,... | collective-permute-start | bytes 147464 | tf_op jit(solution)/shard_map/ppermute | solution.py:724
  121.7 2.6 %collective-permute-start.16 = (bf16[192,128]{1,0:T(8,128)(2,1)S(1)}, bf16[192,128]{1,0:T(8,128)(2,1)S(1)}, u32[]{:S(2)}, u32[]{:S(2)}) collective-permute-start(bf16[192,128]{1,0:T(8,128)(2,1)S(1)} %get-tuple-element.114), channel_id=1, source_target_pairs={{0,6},{2,4},{4,2},{6,0},{1,7},{3,5},{5,3},{7,1},{8,14},{10,12},{12... | collective-permute-start | bytes 147464 | tf_op jit(solution)/shard_map/ppermute | solution.py:724
  125.0 6.7 %collective-permute-done.15 = bf16[192,128]{1,0:T(8,128)(2,1)S(1)} collective-permute-done((bf16[192,128]{1,0:T(8,128)(2,1)S(1)}, bf16[192,128]{1,0:T(8,128)(2,1)S(1)}, u32[]{:S(2)}, u32[]{:S(2)}) %collective-permute-start.15) | collective-permute-done | bytes 49184 | tf_op jit(solution)/shard_map/ppermute | solution.py:724
  131.8 1.4 %shard_map.151 = (f32[64,864]{1,0:T(8,128)}, f32[64,512]{1,0:T(8,128)}) custom-call(s32[3]{0:T(128)S(1)} %pad_add_fusion.1.at_ref, bf16[768,128]{1,0:T(8,128)(2,1)S(1)} %constant_dynamic-update-slice_fusion.5.got_ref, f32[8,128]{1,0:T(8,128)S(1)} %get-tuple-element.111.small_ref), custom_call_target="tpu_custom_call" | custom-call | bytes 500000 | tf_op jit(solution)/shard_map/pallas_call | solution.py:34
  133.2 0.9 shard_map.149
  (84 shorter events, 12.1 us)
Async XLA Ops:
  0.6 14.2 %copy-start.5 = (bf16[64,512]{1,0:T(8,128)(2,1)S(1)}, bf16[64,512]{1,0:T(8,128)(2,1)}, u32[]{:S(2)}) copy-start(bf16[64,512]{1,0:T(8,128)(2,1)} %down_ref.1) | copy-start | bytes 196612
  1.3 9.9 %copy-start.11 = (s32[4,4,256]{2,1,0:T(4,128)S(1)}, s32[4,4,256]{2,1,0:T(4,128)}, u32[]{:S(2)}) copy-start(s32[4,4,256]{2,1,0:T(4,128)} %param.12) | copy-start | bytes 49156
  1.3 9.9 %copy-start.10 = (bf16[64,2,2,128]{3,2,1,0:T(2,128)(2,1)S(1)}, bf16[64,2,2,128]{3,2,1,0:T(2,128)(2,1)}, u32[]{:S(2)}) copy-start(bf16[64,2,2,128]{3,2,1,0:T(2,128)(2,1)} %param.17) | copy-start | bytes 196612
  1.3 13.3 %copy-start.9 = (bf16[64,864]{1,0:T(8,128)(2,1)S(1)}, bf16[64,864]{1,0:T(8,128)(2,1)}, u32[]{:S(2)}) copy-start(bf16[64,864]{1,0:T(8,128)(2,1)} %param.13) | copy-start | bytes 331780
  3.9 25.1 %all-to-all-start = ((bf16[32,72,128]{2,1,0:T(8,128)(2,1)}), bf16[32,72,128]{2,1,0:T(8,128)(2,1)S(1)}, u32[]{:S(2)}, u32[]{:S(2)}) async-start(bf16[32,72,128]{2,1,0:T(8,128)(2,1)} %shard_map.136), calls=%async_computation | async-start | bytes 1179648 | tf_op jit(solution)/shard_map/all_to_all | solution.py:89
  11.3 23.1 %copy-start.2 = (f32[16,256]{1,0:T(8,128)}, f32[16,256]{1,0:T(8,128)S(1)}, u32[]{:S(2)}) copy-start(f32[16,256]{1,0:T(8,128)S(1)} %convert_element_type.12.act_ref) | copy-start | bytes 49156
  12.1 5.5 %collective-permute-start = (bf16[144,128]{1,0:T(8,128)(2,1)S(1)}, bf16[144,128]{1,0:T(8,128)(2,1)S(1)}, u32[]{:S(2)}, u32[]{:S(2)}) collective-permute-start(bf16[144,128]{1,0:T(8,128)(2,1)S(1)} %get-tuple-element.61), channel_id=1, source_target_pairs={{0,8},{16,24},{8,0},{24,16},{1,9},{17,25},{9,1},{25,17},{2,10},{18... | collective-permute-start | bytes 110600 | tf_op jit(solution)/shard_map/ppermute | solution.py:70
  14.0 3.7 %collective-permute-start.1 = (bf16[144,128]{1,0:T(8,128)(2,1)S(1)}, bf16[144,128]{1,0:T(8,128)(2,1)S(1)}, u32[]{:S(2)}, u32[]{:S(2)}) collective-permute-start(bf16[144,128]{1,0:T(8,128)(2,1)S(1)} %get-tuple-element.62), channel_id=1, source_target_pairs={{8,16},{16,8},{9,17},{17,9},{10,18},{18,10},{11,19},{19,11},{12,20... | collective-permute-start | bytes 110600 | tf_op jit(solution)/shard_map/ppermute | solution.py:70
  15.2 5.2 %copy-start.12 = (f32[64]{0:T(128)S(1)}, f32[64]{0:T(128)}, u32[]{:S(2)}) copy-start(f32[64]{0:T(128)} %param.16) | copy-start | bytes 772
  15.2 5.2 %copy-start.13 = (f32[64]{0:T(128)S(1)}, f32[64]{0:T(128)}, u32[]{:S(2)}) copy-start(f32[64]{0:T(128)} %param.15) | copy-start | bytes 772
  18.2 5.3 %collective-permute-start.2 = (bf16[272,128]{1,0:T(8,128)(2,1)S(1)}, bf16[272,128]{1,0:T(8,128)(2,1)S(1)}, u32[]{:S(2)}, u32[]{:S(2)}) collective-permute-start(bf16[272,128]{1,0:T(8,128)(2,1)S(1)} %get-tuple-element.63), channel_id=1, source_target_pairs={{0,2},{4,6},{2,0},{6,4},{1,3},{5,7},{3,1},{7,5},{8,10},{12,14},{10... | collective-permute-start | bytes 208904 | tf_op jit(solution)/shard_map/ppermute | solution.py:70
  19.8 3.8 %collective-permute-start.3 = (bf16[272,128]{1,0:T(8,128)(2,1)S(1)}, bf16[272,128]{1,0:T(8,128)(2,1)S(1)}, u32[]{:S(2)}, u32[]{:S(2)}) collective-permute-start(bf16[272,128]{1,0:T(8,128)(2,1)S(1)} %get-tuple-element.64), channel_id=1, source_target_pairs={{2,4},{4,2},{3,5},{5,3},{10,12},{12,10},{11,13},{13,11},{18,20},{2... | collective-permute-start | bytes 208904 | tf_op jit(solution)/shard_map/ppermute | solution.py:70
  33.7 5.4 %collective-permute-start.4 = (bf16[256,256]{1,0:T(8,128)(2,1)S(1)}, bf16[256,256]{1,0:T(8,128)(2,1)S(1)}, u32[]{:S(2)}, u32[]{:S(2)}) collective-permute-start(bf16[256,256]{1,0:T(8,128)(2,1)S(1)} %get-tuple-element.67.first_ref), channel_id=1, source_target_pairs={{0,8},{16,24},{8,0},{24,16},{1,9},{17,25},{9,1},{25,17},{2,10},{18... | collective-permute-start | bytes 393224 | tf_op jit(solution)/shard_map/ppermute | solution.py:70
  33.8 5.3 %collective-permute-start.5 = (bf16[256,256]{1,0:T(8,128)(2,1)S(1)}, bf16[256,256]{1,0:T(8,128)(2,1)S(1)}, u32[]{:S(2)}, u32[]{:S(2)}) collective-permute-start(bf16[256,256]{1,0:T(8,128)(2,1)S(1)} %get-tuple-element.68.second_ref), channel_id=1, source_target_pairs={{8,16},{16,8},{9,17},{17,9},{10,18},{18,10},{11,19},{19,11},{12,20... | collective-permute-start | bytes 393224 | tf_op jit(solution)/shard_map/ppermute | solution.py:70
  35.0 4.6 %copy-start.6 = (bf16[1024,128]{1,0:T(8,128)(2,1)}, bf16[1024,128]{1,0:T(8,128)(2,1)S(1)}, u32[]{:S(2)}) copy-start(bf16[1024,128]{1,0:T(8,128)(2,1)S(1)} %get-tuple-element.94.wide_ref) | copy-start | bytes 786436
  35.1 19.6 %copy-start.4 = (f32[40,256]{1,0:T(8,128)}, f32[40,256]{1,0:T(8,128)S(1)}, u32[]{:S(2)}) copy-start(f32[40,256]{1,0:T(8,128)S(1)} %get-tuple-element.90.acts_ref) | copy-start | bytes 122884
  39.7 7.3 %collective-permute-start.6 = (bf16[512,256]{1,0:T(8,128)(2,1)S(1)}, bf16[512,256]{1,0:T(8,128)(2,1)S(1)}, u32[]{:S(2)}, u32[]{:S(2)}) collective-permute-start(bf16[512,256]{1,0:T(8,128)(2,1)S(1)} %get-tuple-element.78), channel_id=1, source_target_pairs={{0,2},{4,6},{2,0},{6,4},{1,3},{5,7},{3,1},{7,5},{8,10},{12,14},{10... | collective-permute-start | bytes 786440 | tf_op jit(solution)/shard_map/ppermute | solution.py:70
  40.2 6.8 %collective-permute-start.7 = (bf16[512,256]{1,0:T(8,128)(2,1)S(1)}, bf16[512,256]{1,0:T(8,128)(2,1)S(1)}, u32[]{:S(2)}, u32[]{:S(2)}) collective-permute-start(bf16[512,256]{1,0:T(8,128)(2,1)S(1)} %get-tuple-element.79), channel_id=1, source_target_pairs={{2,4},{4,2},{3,5},{5,3},{10,12},{12,10},{11,13},{13,11},{18,20},{2... | collective-permute-start | bytes 786440 | tf_op jit(solution)/shard_map/ppermute | solution.py:70
  47.8 2.0 %collective-permute-start.8 = (bf16[2048,128]{1,0:T(8,128)(2,1)S(1)}, bf16[2048,128]{1,0:T(8,128)(2,1)S(1)}, u32[]{:S(2)}, u32[]{:S(2)}) collective-permute-start(bf16[2048,128]{1,0:T(8,128)(2,1)S(1)} %get-tuple-element.88), channel_id=1, source_target_pairs={{0,1},{1,0},{2,3},{3,2},{4,5},{5,4},{6,7},{7,6},{8,9},{9,8},{10,11... | collective-permute-start | bytes 1572872 | tf_op jit(solution)/shard_map/ppermute | solution.py:84
  71.2 16.4 %copy-start = (f32[32,8,128]{2,1,0:T(8,128)}, f32[32,8,128]{2,1,0:T(8,128)S(1)}, u32[]{:S(2)}) copy-start(f32[32,8,128]{2,1,0:T(8,128)S(1)} %all_to_all.25.stats_ref) | copy-start | bytes 393220
  76.8 10.8 %all-to-all-start.2 = ((f32[32,8,128]{2,1,0:T(8,128)}), f32[32,8,128]{2,1,0:T(8,128)S(1)}, u32[]{:S(2)}, u32[]{:S(2)}) async-start(f32[32,8,128]{2,1,0:T(8,128)} %get-tuple-element.99), calls=%async_computation.2 | async-start | bytes 262144 | tf_op jit(solution)/shard_map/all_to_all | solution.py:89
  79.6 1.0 copy-start.3
  94.1 3.8 %collective-permute-start.9 = (bf16[2304,128]{1,0:T(8,128)(2,1)S(1)}, bf16[2304,128]{1,0:T(8,128)(2,1)S(1)}, u32[]{:S(2)}, u32[]{:S(2)}) collective-permute-start(bf16[2304,128]{1,0:T(8,128)(2,1)S(1)} %get-tuple-element.106), channel_id=1, source_target_pairs={{0,1},{1,0},{2,3},{3,2},{4,5},{5,4},{6,7},{7,6},{8,9},{9,8},{10,11... | collective-permute-start | bytes 1769480 | tf_op jit(solution)/shard_map/ppermute | solution.py:84
  94.5 11.9 %all-to-all-start.3 = ((bf16[32,24,128]{2,1,0:T(8,128)(2,1)}), bf16[32,24,128]{2,1,0:T(8,128)(2,1)S(1)}, u32[]{:S(2)}, u32[]{:S(2)}) async-start(bf16[32,24,128]{2,1,0:T(8,128)(2,1)} %bitcast.15), calls=%async_computation.3 | async-start | bytes 393216 | tf_op jit(solution)/shard_map/all_to_all | solution.py:89
  106.4 6.1 %collective-permute-start.10 = (bf16[24,128]{1,0:T(8,128)(2,1)S(1)}, bf16[24,128]{1,0:T(8,128)(2,1)S(1)}, u32[]{:S(2)}, u32[]{:S(2)}) collective-permute-start(bf16[24,128]{1,0:T(8,128)(2,1)S(1)} %shard_map.150), channel_id=1, source_target_pairs={{0,1},{1,0},{2,3},{3,2},{4,5},{5,4},{6,7},{7,6},{8,9},{9,8},{10,11... | collective-permute-start | bytes 18440 | tf_op jit(solution)/shard_map/ppermute | solution.py:724
  106.7 26.5 %all-to-all-start.4 = ((bf16[32,64,128]{2,1,0:T(8,128)(2,1)}), bf16[32,64,128]{2,1,0:T(8,128)(2,1)S(1)}, u32[]{:S(2)}, u32[]{:S(2)}) async-start(bf16[32,64,128]{2,1,0:T(8,128)(2,1)} %shard_map.148), calls=%async_computation.4 | async-start | bytes 1048576 | tf_op jit(solution)/shard_map/all_to_all | solution.py:89
  112.5 7.1 %collective-permute-start.13 = (bf16[48,128]{1,0:T(8,128)(2,1)S(1)}, bf16[48,128]{1,0:T(8,128)(2,1)S(1)}, u32[]{:S(2)}, u32[]{:S(2)}) collective-permute-start(bf16[48,128]{1,0:T(8,128)(2,1)S(1)} %pad_maximum_fusion), channel_id=1, source_target_pairs={{0,24},{8,16},{16,8},{24,0},{1,25},{9,17},{17,9},{25,1},{2,26},{10... | collective-permute-start | bytes 36872 | tf_op jit(solution)/shard_map/ppermute | solution.py:724
  115.3 4.3 %collective-permute-start.12 = (bf16[48,128]{1,0:T(8,128)(2,1)S(1)}, bf16[48,128]{1,0:T(8,128)(2,1)S(1)}, u32[]{:S(2)}, u32[]{:S(2)}) collective-permute-start(bf16[48,128]{1,0:T(8,128)(2,1)S(1)} %pad_maximum_fusion), channel_id=1, source_target_pairs={{0,16},{8,24},{16,0},{24,8},{1,17},{9,25},{17,1},{25,9},{2,18},{10... | collective-permute-start | bytes 36872 | tf_op jit(solution)/shard_map/ppermute | solution.py:724
  115.8 3.8 %collective-permute-start.11 = (bf16[48,128]{1,0:T(8,128)(2,1)S(1)}, bf16[48,128]{1,0:T(8,128)(2,1)S(1)}, u32[]{:S(2)}, u32[]{:S(2)}) collective-permute-start(bf16[48,128]{1,0:T(8,128)(2,1)S(1)} %pad_maximum_fusion), channel_id=1, source_target_pairs={{0,8},{8,0},{16,24},{24,16},{1,9},{9,1},{17,25},{25,17},{2,10},{10... | collective-permute-start | bytes 36872 | tf_op jit(solution)/shard_map/ppermute | solution.py:724
  119.7 5.4 %collective-permute-start.14 = (bf16[192,128]{1,0:T(8,128)(2,1)S(1)}, bf16[192,128]{1,0:T(8,128)(2,1)S(1)}, u32[]{:S(2)}, u32[]{:S(2)}) collective-permute-start(bf16[192,128]{1,0:T(8,128)(2,1)S(1)} %get-tuple-element.114), channel_id=1, source_target_pairs={{0,2},{2,0},{4,6},{6,4},{1,3},{3,1},{5,7},{7,5},{8,10},{10,8},{12,... | collective-permute-start | bytes 147464 | tf_op jit(solution)/shard_map/ppermute | solution.py:724
  121.7 10.1 %collective-permute-start.16 = (bf16[192,128]{1,0:T(8,128)(2,1)S(1)}, bf16[192,128]{1,0:T(8,128)(2,1)S(1)}, u32[]{:S(2)}, u32[]{:S(2)}) collective-permute-start(bf16[192,128]{1,0:T(8,128)(2,1)S(1)} %get-tuple-element.114), channel_id=1, source_target_pairs={{0,6},{2,4},{4,2},{6,0},{1,7},{3,5},{5,3},{7,1},{8,14},{10,12},{12... | collective-permute-start | bytes 147464 | tf_op jit(solution)/shard_map/ppermute | solution.py:724
  124.2 7.5 %collective-permute-start.15 = (bf16[192,128]{1,0:T(8,128)(2,1)S(1)}, bf16[192,128]{1,0:T(8,128)(2,1)S(1)}, u32[]{:S(2)}, u32[]{:S(2)}) collective-permute-start(bf16[192,128]{1,0:T(8,128)(2,1)S(1)} %get-tuple-element.114), channel_id=1, source_target_pairs={{0,4},{2,6},{4,0},{6,2},{1,5},{3,7},{5,1},{7,3},{8,12},{10,14},{12... | collective-permute-start | bytes 147464 | tf_op jit(solution)/shard_map/ppermute | solution.py:724
  (3 other events, 2.4 us)

commit v3 on v2

--- a/solution.py
+++ b/solution.py
@@ -18,7 +18,9 @@
 NT = (((1,), (1,)), ((), ()))
 
 
-def local_call(kernel, outs, *args, scratch=(), smem=(), hbm=(), hbm_outs=(), copies=0, moved=0):
+def local_call(
+    kernel, outs, *args, scratch=(), scalars=(), smem=(), hbm=(), hbm_outs=(), copies=0, moved=0
+):
     held = sum(math.prod(shape) * jnp.dtype(kind).itemsize for shape, kind in scratch)
     limit = held // 2**20 + 6
     vmem = pl.BlockSpec(memory_space=pltpu.VMEM)
@@ -29,6 +31,7 @@
         for i, arg in enumerate(args)
     ]
     held = [pltpu.VMEM(shape, kind) for shape, kind in scratch]
+    held += [pltpu.SMEM(shape, kind) for shape, kind in scalars]
     if copies:
         held.append(pltpu.SemaphoreType.DMA((copies,)))
     return pl.pallas_call(
@@ -57,6 +60,18 @@
     return pl.ds(n * count, count)
 
 
+def started_rows(source, target, cuts, semaphores):
+    copies = []
+    for n, (begin, end) in enumerate(zip(cuts, cuts[1:])):
+        own = pl.ds(begin, end - begin)
+        copies.append(started(source.at[own, :], target.at[own, :], semaphores.at[n]))
+    return copies
+
+
+OWN = [(p, q) for p in range(1, 5) for q in range(1, 5)]
+RING = [(p, q) for p in range(6) for q in range(6) if (p, q) not in OWN]
+
+
 def neighbours(axis, step):
     count = lax.axis_size(axis)
     return [(i, i + step) for i in range(count) if 0 <= i + step < count]
@@ -90,25 +105,27 @@
 
 
 def pack_kernel(
-    halves, groups, depth, counts_ref, feats_ref, ids_ref, out_ref, feats, ids, sems
+    halves, groups, depth, counts_ref, feats_ref, ids_ref, out_ref, feats, ids, counts, sems
 ):
     devices = out_ref.shape[0]
     chan = feats_ref.shape[0]
     parts = 4
     width = feats.shape[1] // parts
     got_ids = started(ids_ref, ids, sems.at[parts])
+    got_counts = started(counts_ref, counts, sems.at[parts + 1])
     got = []
     for n in range(parts):
         lanes = pl.ds(n * width, width)
         got.append(started(feats_ref.at[:, lanes], feats.at[:, lanes], sems.at[n]))
     got_ids.wait()
+    got_counts.wait()
     rank = lax.broadcasted_iota(jnp.int32, (halves, LANES), 0) * LANES + lax.broadcasted_iota(
         jnp.int32, (halves, LANES), 1
     )
     blank = jnp.zeros((8 - 2 * halves, LANES), F32)
     for d in range(devices):
         those = ids[d * halves : (d + 1) * halves, :]
-        usable = rank < counts_ref[0, d]
+        usable = rank < counts[0, d]
         group = jnp.where(usable, those // depth, groups).astype(F32)
         place = (those % depth).astype(F32)
         tags = jnp.concatenate([group, place, blank], axis=0)
@@ -133,45 +150,37 @@
     return jnp.concatenate([rows, jnp.pad(tags, ((0, 0), (0, 6), (0, 0)))], axis=1)
 
 
+def hot_rows(row, first, count):
+    index = lax.broadcasted_iota(jnp.int32, (count, LANES), 0).astype(F32).astype(BF16)
+    row = jnp.broadcast_to(row, (count, LANES)).astype(BF16)
+    return jnp.where(index + jnp.asarray(first, BF16) == row, jnp.ones_like(row), jnp.zeros_like(row))
+
+
 def scatter_kernel(
     halves, chan, size_y, sides_ref, recv_ref, act_ref, first_ref, second_ref, tags_ref,
-    acc, masked, hot, tags_held, sems,
+    masked, hot, tags_held, sems,
 ):
     chunks = recv_ref.shape[0]
     groups, depth = act_ref.shape
-    per_step = masked.shape[1] // (halves * LANES)
-    steps = chunks // per_step
-    place = lax.broadcasted_iota(jnp.int32, (depth, LANES), 0).astype(F32)
-    tags_held[...] = recv_ref[:, halves * chan :, :].astype(F32)
+    for d in range(chunks):
+        tags_held[d] = recv_ref[d, halves * chan :, :]
     kept = started(tags_held, tags_ref, sems.at[0])
-
-    def step(s, carry):
-        for j in range(per_step):
-            block = recv_ref[s * per_step + j]
-            tags = tags_held[s * per_step + j]
-            for h in range(halves):
-                feats = block[h * chan : (h + 1) * chan, :]
-                col = (j * halves + h) * LANES
-                group = jnp.broadcast_to(tags[h : h + 1, :], (chan, LANES)).astype(BF16)
-                for k in range(groups):
-                    masked[k * chan : (k + 1) * chan, col : col + LANES] = jnp.where(
-                        group == k, feats, jnp.zeros_like(feats)
-                    )
-                low = tags[halves + h : halves + h + 1, :]
-                hot[:, col : col + LANES] = jnp.where(place == low, 1.0, 0.0).astype(BF16)
-        part = lax.dot_general(masked[...], hot[...], NT, preferred_element_type=F32)
-
-        @pl.when(s == 0)
-        def _():
-            acc[...] = part
-
-        @pl.when(s > 0)
-        def _():
-            acc[...] += part
-
-        return carry
-
-    lax.fori_loop(0, steps, step, 0)
+    for d in range(chunks):
+        block = recv_ref[d]
+        tags = block[halves * chan :, :].astype(F32)
+        for h in range(halves):
+            feats = block[h * chan : (h + 1) * chan, :]
+            lanes = slice((d * halves + h) * LANES, (d * halves + h + 1) * LANES)
+            group = jnp.broadcast_to(tags[h : h + 1, :], (chan, LANES)).astype(BF16)
+            for k in range(groups):
+                masked[k * chan : (k + 1) * chan, lanes] = jnp.where(
+                    group == k, feats, jnp.zeros_like(feats)
+                )
+            for row in range(0, depth, 32):
+                hot[row : row + 32, lanes] = hot_rows(
+                    tags[halves + h : halves + h + 1, :], row, 32
+                )
+    acc = lax.dot_general(masked[...], hot[...], NT, preferred_element_type=F32)
     odd = sides_ref[0] != 0
     half = size_y // 2
     for k in range(groups // 2):
@@ -242,8 +251,9 @@
         row += low.shape[0]
 
 
-def wide_kernel(
-    sides_ref, act_ref, grad_ref, xf_ref, xs_ref, yf_ref, ys_ref, wide_ref, acts_ref
+def fine_grad_kernel(
+    sides_ref, act_ref, grad_ref, xf_ref, xs_ref, yf_ref, ys_ref, down_ref, acts_ref, own_ref, ring_ref,
+    acts_held, wide, up, own, ring, sems,
 ):
     chan = grad_ref.shape[0] // 4
     depth = act_ref.shape[1]
@@ -263,7 +273,8 @@
                 rows.append(acts[4 * (p - 1) + q : 4 * (p - 1) + q + 1])
         rows.append(jnp.concatenate([ya[2 * p : 2 * p + 1], ya[2 * p + 1 : 2 * p + 2]], axis=1))
     rows.append(jnp.zeros((4, depth), F32))
-    acts_ref[...] = jnp.concatenate(rows, axis=0)
+    acts_held[...] = jnp.concatenate(rows, axis=0)
+    kept = [started(acts_held, acts_ref, sems.at[0])]
     for x in range(4):
         for y in range(4):
             if y in (0, 3):
@@ -273,23 +284,55 @@
             else:
                 first = ((x - 1) * 2 + y - 1) * chan
                 block = grad_ref[first : first + chan, :]
-            wide_ref[(x * 4 + y) * chan : (x * 4 + y + 1) * chan, :] = block
-
-
-def bands_kernel(front_ref, back_ref, bands_ref, back_bands_ref):
+            wide[(x * 4 + y) * chan : (x * 4 + y + 1) * chan, :] = block
+    coarse_z = lax.broadcasted_iota(jnp.int32, (LANES, 2 * depth), 0)
+    fine_z = lax.broadcasted_iota(jnp.int32, (LANES, 2 * depth), 1)
+    child = jnp.where(fine_z < depth, 0, 1)
+    spread = (2 * coarse_z + child == fine_z - child * depth).astype(BF16)
+    up[...] = jnp.dot(wide[...], spread, preferred_element_type=F32).astype(BF16)
+    for x in range(4):
+        for y in range(4):
+            those = slice((x * 4 + y) * chan, (x * 4 + y + 1) * chan)
+            both = jnp.concatenate([up[those, :depth], up[those, depth:]], axis=0)
+            grads = jnp.dot(down_ref[...], both, preferred_element_type=F32)
+            for a in range(2):
+                for b in range(2):
+                    column = (2 * x + a - 1, 2 * y + b - 1)
+                    block = grads[(a * 2 + b) * chan : (a * 2 + b + 1) * chan]
+                    if column in OWN:
+                        n = OWN.index(column)
+                        own[n * chan : (n + 1) * chan, :] = block
+                    elif column in RING:
+                        n = RING.index(column)
+                        ring[n * chan : (n + 1) * chan, :] = block
+    kept.append(started(own, own_ref, sems.at[1]))
+    kept.append(started(ring, ring_ref, sems.at[2]))
+    for copy in kept:
+        copy.wait()
+
+
+def bands_kernel(
+    front_ref, back_ref, bands_ref, back_bands_ref, own_ref, bands, back_bands, sems
+):
     rows, width = front_ref.shape[0], front_ref.shape[1] // 9
     back_rows, back_width = back_ref.shape[0], back_ref.shape[1] // 9
     for t in range(9):
         block = front_ref[:, t * width : (t + 1) * width].astype(F32)
         for q in range(6):
             moved = pltpu.roll(block, q * back_rows, 1) if q else block
-            bands_ref[q * rows : (q + 1) * rows, t * width : (t + 1) * width] = moved.astype(BF16)
+            bands[q * rows : (q + 1) * rows, t * width : (t + 1) * width] = moved.astype(BF16)
+    kept = [started(bands, bands_ref, sems.at[0])]
+    own_ref[...] = bands[rows : 5 * rows, :]
+    for t in range(9):
         block = back_ref[:, t * back_width : (t + 1) * back_width].astype(F32)
         for q in range(4):
             moved = pltpu.roll(block, q * rows, 1) if q else block
-            back_bands_ref[
+            back_bands[
                 q * back_rows : (q + 1) * back_rows, t * back_width : (t + 1) * back_width
             ] = moved.astype(BF16)
+    kept.append(started(back_bands, back_bands_ref, sems.at[1]))
+    for copy in kept:
+        copy.wait()
 
 
 def band_inputs(w_sub, in_chan):
@@ -374,10 +417,11 @@
 ):
     rows = low_ref.shape[0] // 8
     depth = acts_ref.shape[1]
-    wide = bands_ref.shape[0]
-    chan = wide // 6
+    chan = bands_ref.shape[0] // 4
     place = sides_ref[2]
     kept = []
+    total = jnp.zeros((chan, depth), F32)
+    count = jnp.zeros((1, depth), F32)
     for x in range(8):
         own = slice(x * rows, (x + 1) * rows)
         low, high = low_ref[own, :], high_ref[own, :]
@@ -389,46 +433,67 @@
             to = slice((x * 3 + n) * rows, (x * 3 + n + 1) * rows)
             stack[to, :LANES] = tiles[0]
             stack[to, LANES:] = tiles[1]
-        if 1 <= x <= 6:
-            kept.append(
-                started(
-                    stack.at[rows_of(x, 3 * rows), :],
-                    stack_ref.at[rows_of(x - 1, 3 * rows), :],
-                    sems.at[x - 1],
-                )
-            )
-    total = jnp.zeros((chan, depth), F32)
-    for p in range(6):
+        own = rows_of(x, 3 * rows)
+        kept.append(started(stack.at[own, :], stack_ref.at[own, :], sems.at[x]))
+        p = x - 2
+        if not 1 <= p <= 4:
+            continue
         first = p * 3 * rows
         out = jnp.dot(
             bands_ref[...], stack[first : first + 9 * rows, :], preferred_element_type=F32
         )
-        for q in range(6):
-            block = out[q * chan : (q + 1) * chan] * acts_ref[p * 6 + q : p * 6 + q + 1, :]
-            hidden[p * wide + q * chan : p * wide + (q + 1) * chan, :] = block
-            if 1 <= p <= 4 and 1 <= q <= 4:
-                total = total + block
-        own = rows_of(p, wide)
-        kept.append(started(hidden.at[own, :], hidden_ref.at[own, :], sems.at[6 + p]))
-    count = jnp.zeros((1, depth), F32)
-    for p in range(1, 5):
         for q in range(1, 5):
-            count = count + acts_ref[p * 6 + q : p * 6 + q + 1, :]
+            act = acts_ref[p * 6 + q : p * 6 + q + 1, :]
+            block = out[(q - 1) * chan : q * chan] * act
+            n = OWN.index((p, q))
+            hidden[n * chan : (n + 1) * chan, :] = block
+            total = total + block
+            count = count + act
+        own = rows_of(p - 1, 4 * chan)
+        kept.append(started(hidden.at[own, :], hidden_ref.at[own, :], sems.at[7 + p]))
     count = jnp.sum(count, axis=1, keepdims=True)
     total = jnp.sum(total, axis=1, keepdims=True)
     mean = total / jnp.maximum(count, 1.0)
     squares = jnp.zeros((chan, depth), F32)
-    for p in range(1, 5):
-        for q in range(1, 5):
-            row = p * wide + q * chan
-            centred = (hidden[row : row + chan, :] - mean) * acts_ref[p * 6 + q : p * 6 + q + 1, :]
-            squares = squares + centred * centred
+    for n, (p, q) in enumerate(OWN):
+        act = acts_ref[p * 6 + q : p * 6 + q + 1, :]
+        centred = (hidden[n * chan : (n + 1) * chan, :] - mean) * act
+        squares = squares + centred * centred
     squares = jnp.sum(squares, axis=1, keepdims=True)
     packed = to_rows([total, squares, jnp.broadcast_to(count, (chan, 1))])
     for d in range(stats_ref.shape[0]):
         stats_ref[d] = packed
     for copy in kept:
         copy.wait()
+
+
+def conv_ring_kernel(bands_ref, acts_ref, stack_ref, hidden_ref, bands, acts, stack, hidden, sems):
+    rows = stack.shape[0] // 24
+    wide = bands.shape[0]
+    chan = wide // 6
+    got = [
+        started(acts_ref, acts, sems.at[0]),
+        started(bands_ref, bands, sems.at[1]),
+        started(stack_ref, stack, sems.at[2]),
+    ]
+    for copy in got:
+        copy.wait()
+    for p in range(6):
+        taps = stack[p * 3 * rows : (p * 3 + 9) * rows, :]
+        if p in (0, 5):
+            out = jnp.dot(bands[...], taps, preferred_element_type=F32)
+            columns = range(6)
+        else:
+            ends = jnp.concatenate([bands[:chan, :], bands[5 * chan :, :]], axis=0)
+            out = jnp.dot(ends, taps, preferred_element_type=F32)
+            columns = (0, 5)
+        for i, q in enumerate(columns):
+            n = RING.index((p, q))
+            hidden[n * chan : (n + 1) * chan, :] = (
+                out[i * chan : (i + 1) * chan] * acts[p * 6 + q : p * 6 + q + 1, :]
+            )
+    kept = started(hidden, hidden_ref, sems.at[3])
+    kept.wait()
 
 
 def merged_stats(stats_ref):
@@ -441,39 +506,30 @@
 
 
 def norm_kernel(
-    stats_ref, params_ref, hidden_ref, wide_ref, acts_ref, down_ref, pre_ref, out_ref, sums_ref,
-    hidden, wide, acts, up, fine, pre, outs, sems,
+    columns, stats_ref, params_ref, hidden_ref, fine_ref, acts_ref, *rest
 ):
-    chan = hidden.shape[0] // 36
+    own = columns is OWN
+    if own:
+        pre_ref, out_ref, sums_ref, stats, hidden, fine, acts, pre, outs, sems = rest
+    else:
+        (out_ref, grad_ref, mask_ref, down_ref, pre_ref, coarse_ref, raw_ref) = rest[:7]
+        stats, hidden, fine, acts, pre, outs, grads, taps, sems = rest[7:]
+    chan = hidden.shape[0] // len(columns)
     depth = acts.shape[1]
-    got_acts = started(acts_ref, acts, sems.at[0])
-    got_wide = started(wide_ref, wide, sems.at[1])
-    got = []
-    for p in range(6):
-        own = rows_of(p, 6 * chan)
-        got.append(started(hidden_ref.at[own, :], hidden.at[own, :], sems.at[2 + p]))
-    coarse_z = lax.broadcasted_iota(jnp.int32, (LANES, 2 * depth), 0)
-    fine_z = lax.broadcasted_iota(jnp.int32, (LANES, 2 * depth), 1)
-    child = jnp.where(fine_z < depth, 0, 1)
-    spread = (2 * coarse_z + child == fine_z - child * depth).astype(BF16)
-    got_wide.wait()
-    up[...] = jnp.dot(wide[...], spread, preferred_element_type=F32).astype(BF16)
-    for x in range(4):
-        for y in range(4):
-            own = slice((x * 4 + y) * chan, (x * 4 + y + 1) * chan)
-            both = jnp.concatenate([up[own, :depth], up[own, depth:]], axis=0)
-            for a in range(2):
-                p = 2 * x + a - 1
-                if not 0 <= p < 6:
-                    continue
-                cols = [b for b in range(2) if 0 <= 2 * y + b - 1 < 6]
-                first = (a * 2 + cols[0]) * chan
-                grads = jnp.dot(
-                    down_ref[first : first + len(cols) * chan, :], both, preferred_element_type=F32
-                )
-                row = (p * 6 + 2 * y + cols[0] - 1) * chan
-                fine[row : row + len(cols) * chan, :] = grads
-    count, average, inverse = merged_stats(stats_ref)
+    got_stats = started(stats_ref, stats, sems.at[0])
+    got_acts = started(acts_ref, acts, sems.at[1])
+    cuts = [n * chan for n in range(0, len(columns) + 1, 4)]
+    parts = len(cuts) - 1
+    got = started_rows(hidden_ref, hidden, cuts, sems.at[pl.ds(2, parts)])
+    got_fine = started_rows(fine_ref, fine, cuts, sems.at[pl.ds(2 + parts, parts)])
+    if not own:
+        last = 2 + 2 * parts
+        got_down = [
+            started(out_ref, outs, sems.at[last + 1]),
+            started(grad_ref, grads, sems.at[last + 2]),
+        ]
+    got_stats.wait()
+    count, average, inverse = merged_stats(stats)
     full = (chan, LANES)
     average, inverse, gain, shift = [
         jnp.broadcast_to(column, full)
@@ -481,91 +537,92 @@
     ]
     sum_shift = jnp.zeros((chan, LANES), F32)
     sum_gain = jnp.zeros((chan, LANES), F32)
-    kept = []
     got_acts.wait()
-    for p in range(6):
-        got[p].wait()
-        for q in range(6):
-            row = (p * 6 + q) * chan
-            for half in range(depth // LANES):
-                lanes = slice(half * LANES, (half + 1) * LANES)
-                act = acts[p * 6 + q : p * 6 + q + 1, lanes]
-                normed = (hidden[row : row + chan, lanes] - average) * inverse
-                x = gain * normed + shift
-                square = x * x
-                bent = jnp.tanh(GELU_SCALE * (x + GELU_CUBE * (square * x)))
-                cdf = 0.5 + 0.5 * bent
-                slope = cdf + (0.5 * x) * (1.0 - bent * bent) * (
-                    GELU_SCALE + (3.0 * GELU_CUBE * GELU_SCALE) * square
-                )
-                grad = (act * slope) * fine[row : row + chan, lanes]
-                pre[row : row + chan, lanes] = grad
-                if 1 <= p <= 4 and 1 <= q <= 4:
-                    sum_shift = sum_shift + grad
-                    sum_gain = sum_gain + grad * normed
-                    to = ((p - 1) * 4 + q - 1) * chan
-                    outs[to : to + chan, lanes] = (x * cdf * act).astype(BF16)
-        own = rows_of(p, 6 * chan)
-        kept.append(started(pre.at[own, :], pre_ref.at[own, :], sems.at[8 + p]))
-    kept.append(started(outs, out_ref, sems.at[14]))
-    sums = to_rows(
-        [jnp.sum(sum_shift, axis=1, keepdims=True), jnp.sum(sum_gain, axis=1, keepdims=True)]
-    )
-    for d in range(sums_ref.shape[0]):
-        sums_ref[d] = sums
+    for n, (p, q) in enumerate(columns):
+        if n % 4 == 0:
+            got[n // 4].wait()
+            got_fine[n // 4].wait()
+        own_rows = slice(n * chan, (n + 1) * chan)
+        for half in range(depth // LANES):
+            lanes = slice(half * LANES, (half + 1) * LANES)
+            act = acts[p * 6 + q : p * 6 + q + 1, lanes]
+            normed = (hidden[own_rows, lanes] - average) * inverse
+            x = gain * normed + shift
+            square = x * x
+            bent = jnp.tanh(GELU_SCALE * (x + GELU_CUBE * (square * x)))
+            cdf = 0.5 + 0.5 * bent
+            slope = cdf + (0.5 * x) * (1.0 - bent * bent) * (
+                GELU_SCALE + (3.0 * GELU_CUBE * GELU_SCALE) * square
+            )
+            grad = (act * slope) * fine[own_rows, lanes]
+            pre[own_rows, lanes] = grad
+            if own:
+                sum_shift = sum_shift + grad
+                sum_gain = sum_gain + grad * normed
+                outs[own_rows, lanes] = (x * cdf * act).astype(BF16)
+    kept = [started(pre, pre_ref, sems.at[2 + 2 * parts])]
+    if own:
+        kept.append(started(outs, out_ref, sems.at[3 + 2 * parts]))
+        sums = to_rows(
+            [jnp.sum(sum_shift, axis=1, keepdims=True), jnp.sum(sum_gain, axis=1, keepdims=True)]
+        )
+        for d in range(sums_ref.shape[0]):
+            sums_ref[d] = sums
+    else:
+        for copy in got_down:
+            copy.wait()
+        down_conv(outs, grads, mask_ref, down_ref, coarse_ref, raw_ref, taps)
     for copy in kept:
         copy.wait()
 
 
-def down_kernel(out_ref, grad_ref, mask_ref, down_ref, coarse_ref, raw_ref, stack):
-    depth = out_ref.shape[1]
-    chan = grad_ref.shape[0] // 4
+def down_conv(outs, grads, mask_ref, down_ref, coarse_ref, raw_ref, stack):
+    depth = outs.shape[1]
+    chan = grads.shape[0] // 4
     source = lax.broadcasted_iota(jnp.int32, (depth, depth), 0)
     target = lax.broadcasted_iota(jnp.int32, (depth, depth), 1)
     wanted = jnp.where(target < LANES, 2 * target, 2 * (target - LANES) + 1)
     sort = (source == wanted).astype(BF16)
+    parted = jnp.dot(outs[...], sort, preferred_element_type=F32).astype(BF16)
     for x in range(2):
         for y in range(2):
             for a in range(2):
                 for b in range(2):
                     row = ((2 * x + a) * 4 + 2 * y + b) * chan
-                    parted = jnp.dot(
-                        out_ref[row : row + chan, :], sort, preferred_element_type=F32
-                    ).astype(BF16)
                     lanes = slice((x * 2 + y) * LANES, (x * 2 + y + 1) * LANES)
                     to = (a * 4 + b * 2) * chan
-                    stack[to : to + chan, lanes] = parted[:, :LANES]
-                    stack[to + chan : to + 2 * chan, lanes] = parted[:, LANES:]
+                    stack[to : to + chan, lanes] = parted[row : row + chan, :LANES]
+                    stack[to + chan : to + 2 * chan, lanes] = parted[row : row + chan, LANES:]
     sums = jnp.dot(down_ref[...], stack[...], preferred_element_type=F32)
     for n in range(4):
         coarse_ref[n] = (sums[:, n * LANES : (n + 1) * LANES] * mask_ref[n : n + 1, :]).astype(
             BF16
         )
-    grads = jnp.concatenate([grad_ref[n * chan : (n + 1) * chan, :] for n in range(4)], axis=1)
-    raw = lax.dot_general(grads, stack[...], NT, preferred_element_type=F32)
+    wide = jnp.concatenate([grads[n * chan : (n + 1) * chan, :] for n in range(4)], axis=1)
+    raw = lax.dot_general(wide, stack[...], NT, preferred_element_type=F32)
     for n in range(4):
         raw_ref[n * chan : (n + 1) * chan, :] = raw[:, n * LANES : (n + 1) * LANES]
 
 
 def hidden_grad_kernel(
-    in_chan, sides_ref, stats_ref, sums_ref, params_ref, hidden_ref, pre_ref, acts_ref, stack_ref,
-    raw_ref, front_ref, rear_ref, swap_ref, small_ref, out_ref,
-    stats, hidden, pre, acts, stack, raw, front, rear, acc, sems,
+    in_chan, sides_ref, stats_ref, sums_ref, params_ref, hidden_ref, hidden_ring_ref, pre_ref,
+    pre_ring_ref, acts_ref, stack_ref, raw_ref, front_ref, rear_ref, swap_ref, small_ref, out_ref,
+    stats, hidden, hidden_ring, pre, pre_ring, acts, stack, raw, front, rear, acc, sems,
 ):
-    chan = hidden.shape[0] // 36
+    chan = hidden.shape[0] // 16
     place = sides_ref[2]
     got_stats = started(stats_ref, stats, sems.at[0])
     got_acts = started(acts_ref, acts, sems.at[1])
     got = []
-    for p in range(6):
-        own = rows_of(p, 6 * chan)
-        got.append(
-            (
-                started(hidden_ref.at[own, :], hidden.at[own, :], sems.at[4 + p]),
-                started(pre_ref.at[own, :], pre.at[own, :], sems.at[10 + p]),
-            )
-        )
-    got_stack = started(stack_ref, stack, sems.at[2])
+    for n, (source, target) in enumerate(
+        ((hidden_ref, hidden), (pre_ref, pre), (hidden_ring_ref, hidden_ring), (pre_ring_ref, pre_ring))
+    ):
+        cuts = [n * chan for n in range(0, target.shape[0] // chan + 1, 4)]
+        got.append(started_rows(source, target, cuts, sems.at[pl.ds(4 + 5 * n, len(cuts) - 1)]))
+    got = list(zip(*got[:2])) + list(zip(*got[2:]))
+    got_stack = started(
+        stack_ref.at[pl.ds(stack.shape[0] // 6, stack.shape[0]), :], stack, sems.at[2]
+    )
     got_raw = started(raw_ref, raw, sems.at[3])
     raw_shift = jnp.sum(sums_ref[:, 0, :], axis=0, keepdims=True)
     raw_gain = jnp.sum(sums_ref[:, 1, :], axis=0, keepdims=True)
@@ -582,23 +639,24 @@
     weight = gain * inverse
     got_acts.wait()
     kept = []
-    for p in range(6):
-        for copy in got[p]:
-            copy.wait()
-        for n in range(6 * p, 6 * p + 6):
-            row = n * chan
-            tiles = []
-            for half, held in enumerate((front, rear)):
-                lanes = slice(half * LANES, (half + 1) * LANES)
-                act = acts[n : n + 1, lanes]
-                normed = (hidden[row : row + chan, lanes] - average) * inverse
-                grad = pre[row : row + chan, lanes] - (mean_shift + normed * mean_gain)
-                tiles.append(((act * weight) * grad).astype(BF16))
-                held[row : row + chan, :] = tiles[-1]
-            swap_ref[row : row + chan, :] = jnp.where(place == 0, tiles[1], tiles[0])
-        own = rows_of(p, 6 * chan)
-        kept.append(started(front.at[own, :], front_ref.at[own, :], sems.at[16 + p]))
-        kept.append(started(rear.at[own, :], rear_ref.at[own, :], sems.at[22 + p]))
+    for n, (p, q) in enumerate(OWN + RING):
+        if n % 4 == 0:
+            for copy in got[n // 4]:
+                copy.wait()
+        held_hidden, held_pre = (hidden, pre) if n < 16 else (hidden_ring, pre_ring)
+        own = slice(n * chan, (n + 1) * chan) if n < 16 else slice((n - 16) * chan, (n - 15) * chan)
+        to = slice((p * 6 + q) * chan, (p * 6 + q + 1) * chan)
+        tiles = []
+        for half, held in enumerate((front, rear)):
+            lanes = slice(half * LANES, (half + 1) * LANES)
+            act = acts[p * 6 + q : p * 6 + q + 1, lanes]
+            normed = (held_hidden[own, lanes] - average) * inverse
+            grad = held_pre[own, lanes] - (mean_shift + normed * mean_gain)
+            tiles.append(((act * weight) * grad).astype(BF16))
+            held[to, :] = tiles[-1]
+        swap_ref[to, :] = jnp.where(place == 0, tiles[1], tiles[0])
+    kept.append(started(front, front_ref, sems.at[24]))
+    kept.append(started(rear, rear_ref, sems.at[25]))
     got_stack.wait()
     got_raw.wait()
     rows = stack.shape[0] // 6
@@ -690,13 +748,12 @@
             cells[k * chan : (k + 1) * chan, :] = (
                 grid[q * chan : (q + 1) * chan] * acts[k : k + 1, :]
             ).astype(BF16)
-    place = lax.broadcasted_iota(jnp.int32, (depth, LANES), 0).astype(F32)
 
     def from_cells(d):
-        tags = tags_held[d]
-        lows = [tags[halves + h : halves + h + 1, :] for h in range(halves)]
-        hot = [jnp.where(place == low, 1.0, 0.0).astype(BF16) for low in lows]
-        hot = jnp.concatenate(hot, axis=1)
+        tags = tags_held[d].astype(F32)
+        hot = jnp.concatenate(
+            [hot_rows(tags[halves + h : halves + h + 1, :], 0, depth) for h in range(halves)], axis=1
+        )
         found = jnp.dot(cells[...], hot, preferred_element_type=F32)
         for h in range(halves):
             group = jnp.broadcast_to(tags[h : h + 1, :], (chan, LANES))
@@ -706,24 +763,28 @@
                 out = jnp.where(group == k, found[k * chan : (k + 1) * chan, lanes], out)
             out_ref[d, h * chan : (h + 1) * chan, :] = out.astype(BF16)
 
+    together = 16
+
     def step(s, carry):
-        for j in range(4):
-            from_cells(4 * s + j)
+        for j in range(together):
+            from_cells(together * s + j)
         return carry
 
-    lax.fori_loop(0, tags_held.shape[0] // 4, step, 0)
-
-
-def piece_kernel(parts_ref, out_ref):
-    out_ref[...] = jnp.sum(parts_ref[...].astype(F32), axis=0).astype(BF16)
-
-
-def gathered(piece, names, sizes):
-    for name, size in zip(names, sizes):
-        pairs = [[(i, i ^ k) for i in range(size)] for k in range(1, size)]
-        parts = [piece] + [lax.ppermute(piece, name, pair) for pair in pairs]
-        piece = jnp.concatenate(parts, axis=0)
-    return piece
+    lax.fori_loop(0, tags_held.shape[0] // together, step, 0)
+
+
+def piece_kernel(parts_ref, points_ref, out_ref):
+    rows = points_ref.shape[1]
+    piece = jnp.sum(parts_ref[...].astype(F32), axis=0).astype(BF16)
+    for d in range(out_ref.shape[0]):
+        out_ref[d, :rows, :] = points_ref[d]
+        out_ref[d, rows:, :] = piece
+
+
+def sum_kernel(parts_ref, out_ref):
+    piece = jnp.sum(parts_ref[...].astype(F32), axis=0).astype(BF16)
+    for d in range(out_ref.shape[0]):
+        out_ref[d] = piece
 
 
 def weights_out(rows, small_ref, in_chan, sub_ref, down_ref):
@@ -743,24 +804,22 @@
         down_ref[:, (2 * n + 1) * LANES : (2 * n + 2) * LANES] = both[chan:]
 
 
-def points_kernel(halves, chan, got_ref, points_ref):
-    for d in range(got_ref.shape[0]):
+def last_kernel(halves, chan, got_ref, small_ref, points_ref, sub_ref, down_ref, flat):
+    devices = got_ref.shape[0]
+    piece = got_ref.shape[1] - halves * chan
+    for d in range(devices):
         block = got_ref[d]
         for h in range(halves):
             first = (d * halves + h) * LANES
             points_ref[:, first : first + LANES] = block[h * chan : (h + 1) * chan, :]
-
-
-def weights_kernel(chan, sizes, at_ref, got_ref, small_ref, sub_ref, down_ref, flat):
-    nz, nx, ny = sizes
-    piece = got_ref.shape[0] // (nx * ny * nz)
-    for y in range(ny):
-        for x in range(nx):
-            for z in range(nz):
-                n = (y * nx + x) * nz + z
-                device = ((at_ref[1] ^ x) * ny + (at_ref[2] ^ y)) * nz + (at_ref[0] ^ z)
-                own = pl.ds(pl.multiple_of(device * piece, 8), piece)
-                flat[own, :] = got_ref[n * piece : (n + 1) * piece, :].astype(F32)
+        flat[d * piece : (d + 1) * piece, :] = block[halves * chan :, :].astype(F32)
+    weights_out(lambda n: flat[n * LANES : (n + 1) * LANES, :], small_ref, chan, sub_ref, down_ref)
+
+
+def weights_kernel(chan, got_ref, small_ref, sub_ref, down_ref, flat):
+    piece = got_ref.shape[1]
+    for d in range(got_ref.shape[0]):
+        flat[d * piece : (d + 1) * piece, :] = got_ref[d].astype(F32)
     weights_out(lambda n: flat[n * LANES : (n + 1) * LANES, :], small_ref, chan, sub_ref, down_ref)
 
 
@@ -788,7 +847,8 @@
             [((devices, halves * in_chan + 8, LANES), BF16)],
             send_counts, point_feats, voxel_ids.reshape(-1, LANES),
             scratch=[((in_chan, slot_total), BF16), ((devices * halves, LANES), jnp.int32)],
-            smem=(0,), hbm=(1, 2), copies=5, moved=2e6,
+            scalars=[((1, devices), jnp.int32)],
+            hbm=(0, 1, 2), copies=6, moved=2e6,
         )[0]
         recv = everyone(payload)
     else:
@@ -825,27 +885,33 @@
         (recv, acts, grad_c, cot_x, cot_y, by_child, front, back, params)
     )
 
-    per_step = min(chunks, 16 // halves)
     *mine, tags = local_call(
         functools.partial(scatter_kernel, halves, in_chan, size_y),
-        [((rows_x, size_z), BF16)] * 2 + [((chunks, 8, LANES), F32)],
+        [((rows_x, size_z), BF16)] * 2 + [((chunks, 8, LANES), BF16)],
         sides, recv, acts,
         scratch=[
-            ((groups * in_chan, size_z), F32),
-            ((groups * in_chan, per_step * halves * LANES), BF16),
-            ((size_z, per_step * halves * LANES), BF16),
-            ((chunks, 8, LANES), F32),
+            ((groups * in_chan, chunks * halves * LANES), BF16),
+            ((size_z, chunks * halves * LANES), BF16),
+            ((chunks, 8, LANES), BF16),
         ],
         smem=(0,), hbm_outs=(2,), copies=1, moved=2e7,
     )
     got_x = swaps(*mine, "gx")
-    grad_wide, acts_wide = local_call(
-        wide_kernel,
-        [((16 * out_chan, LANES), BF16), ((40, size_z), F32)],
-        sides, acts, grad_c, *cot_x, *cot_y,
-        smem=(0,), hbm_outs=(), moved=5e5,
-    )
-    got_x, grad_wide, acts_wide = lax.optimization_barrier((got_x, grad_wide, acts_wide))
+    own, ring = ((16 * out_chan, size_z), F32), ((20 * out_chan, size_z), F32)
+    acts_wide, *fine_grad = local_call(
+        fine_grad_kernel,
+        [((40, size_z), F32), own, ring],
+        sides, acts, grad_c, *cot_x, *cot_y, by_child,
+        scratch=[
+            ((40, size_z), F32),
+            ((16 * out_chan, LANES), BF16),
+            ((16 * out_chan, 2 * size_z), BF16),
+            own,
+            ring,
+        ],
+        smem=(0,), hbm_outs=(0, 1, 2), copies=3, moved=4e6,
+    )
+    got_x, acts_wide, fine_grad = lax.optimization_barrier((got_x, acts_wide, fine_grad))
     ends = local_call(
         rows_kernel,
         [((2 * rows_x, size_z), BF16)] * 2,
@@ -853,12 +919,17 @@
     )
     got_y = swaps(*ends, "gy")
     bands_shape, back_shape = (wide, 9 * 8 * in_chan), (back_wide, 9 * 6 * out_chan)
-    bands, back_bands = local_call(
+    own_bands_shape = (4 * out_chan, bands_shape[1])
+    bands, back_bands, own_bands = local_call(
         bands_kernel,
-        [(bands_shape, BF16), (back_shape, BF16)],
-        front, back, hbm_outs=(), moved=4e6,
-    )
-    got_y, bands, back_bands = lax.optimization_barrier((got_y, bands, back_bands))
+        [(bands_shape, BF16), (back_shape, BF16), (own_bands_shape, BF16)],
+        front, back,
+        scratch=[(bands_shape, BF16), (back_shape, BF16)],
+        hbm_outs=(0, 1), copies=2, moved=4e6,
+    )
+    got_y, bands, back_bands, own_bands = lax.optimization_barrier(
+        (got_y, bands, back_bands, own_bands)
+    )
     tile_low, tile_high, swap = local_call(
         functools.partial(columns_kernel, in_chan),
         [((rows_64, LANES), BF16)] * 3,
@@ -867,37 +938,49 @@
     before, after = z_exchange(tile_low, tile_high, swap)
 
     stats_shape = (devices, 8, LANES)
-    stack_shape = (rows_64 // 8 * 6 * 3, size_z)
-    hidden, stack, stats = local_call(
+    stack_shape = (3 * rows_64, size_z)
+    own_hidden, stack, stats = local_call(
         functools.partial(conv_kernel, only_two),
-        [((rows_6, size_z), F32), (stack_shape, BF16), (stats_shape, F32)],
-        sides, tile_low, tile_high, before, after, bands, acts_wide,
-        scratch=[((rows_6, size_z), F32), ((3 * rows_64, size_z), BF16)],
-        smem=(0,), hbm_outs=(0, 1), copies=12, moved=2e7,
-    )
-    stats = everyone(stats)
-    grad_pre, fine_out, sums = local_call(
-        norm_kernel,
-        [((rows_6, size_z), F32), ((groups * out_chan, size_z), BF16), (stats_shape, F32)],
-        stats, params, hidden, grad_wide, acts_wide, by_child,
-        scratch=[
-            ((rows_6, size_z), F32),
-            ((16 * out_chan, LANES), BF16),
+        [own, (stack_shape, BF16), (stats_shape, F32)],
+        sides, tile_low, tile_high, before, after, own_bands, acts_wide,
+        scratch=[own, (stack_shape, BF16)],
+        smem=(0,), hbm_outs=(0, 1), copies=12, moved=1e7,
+    )
+    stats_in = everyone(stats)
+    ring_hidden = local_call(
+        conv_ring_kernel,
+        [ring],
+        bands, acts_wide, stack,
+        scratch=[(bands_shape, BF16), ((40, size_z), F32), (stack_shape, BF16), ring],
+        hbm=(0, 1, 2), hbm_outs=(0,), copies=4, moved=1e7,
+    )[0]
+    stats_in, ring_hidden = lax.optimization_barrier((stats_in, ring_hidden))
+    held = [(stats_shape, F32)]
+    own_pre, fine_out, sums = local_call(
+        functools.partial(norm_kernel, OWN),
+        [own, ((groups * out_chan, size_z), BF16), (stats_shape, F32)],
+        stats_in, params, own_hidden, fine_grad[0], acts_wide,
+        scratch=held + [own, own, ((40, size_z), F32), own, ((groups * out_chan, size_z), BF16)],
+        hbm=(2, 3, 4), hbm_outs=(0, 1), copies=12, moved=5e6,
+    )
+    sums_in = everyone(sums)
+    ring_pre, coarse, raw_down = local_call(
+        functools.partial(norm_kernel, RING),
+        [ring, ((4, out_chan, LANES), BF16), ((4 * out_chan, LANES), F32)],
+        stats_in, params, ring_hidden, fine_grad[1], acts_wide, fine_out, grad_c, coarse_mask, w_down,
+        scratch=held
+        + [
+            ring,
+            ring,
             ((40, size_z), F32),
-            ((16 * out_chan, 2 * size_z), BF16),
-            ((rows_6, size_z), F32),
-            ((rows_6, size_z), F32),
+            ring,
             ((groups * out_chan, size_z), BF16),
+            ((4 * out_chan, LANES), BF16),
+            ((8 * out_chan, 4 * LANES), BF16),
         ],
-        hbm=(2, 3, 4), hbm_outs=(0, 1), copies=15, moved=1e7,
-    )
-    sums = everyone(sums)
-    coarse, raw_down = local_call(
-        down_kernel,
-        [((4, out_chan, LANES), BF16), ((4 * out_chan, LANES), F32)],
-        fine_out, grad_c, coarse_mask, w_down,
-        scratch=[((8 * out_chan, 4 * LANES), BF16)], moved=5e6,
-    )
+        hbm=(0, 2, 3, 4, 5, 6), hbm_outs=(0,), copies=15, moved=5e6,
+    )
+    sums_in, ring_pre, raw_down = lax.optimization_barrier((sums_in, ring_pre, raw_down))
     half_x, half_y, half_z = size_x // 2, size_y // 2, size_z // 2
     coarse_out = coarse.reshape(half_x, half_y, out_chan, half_z).transpose(2, 0, 1, 3)
 
@@ -906,19 +989,22 @@
     grad_low, grad_high, grad_swap, small, parts = local_call(
         functools.partial(hidden_grad_kernel, in_chan),
         [((rows_6, LANES), BF16)] * 3 + [((8, LANES), F32), ((devices * piece, LANES), BF16)],
-        sides, stats, sums, params, hidden, grad_pre, acts_wide, stack, raw_down,
+        sides, stats_in, sums_in, params, own_hidden, ring_hidden, own_pre, ring_pre, acts_wide,
+        stack, raw_down,
         scratch=[
             (stats_shape, F32),
-            ((rows_6, size_z), F32),
-            ((rows_6, size_z), F32),
+            own,
+            ring,
+            own,
+            ring,
             ((40, size_z), F32),
-            (stack_shape, BF16),
+            ((rows_64 // 8 * 6 * 3, size_z), BF16),
             ((4 * out_chan, LANES), F32),
             ((rows_6, LANES), BF16),
             ((rows_6, LANES), BF16),
             ((3, 24 * in_chan, 4 * out_chan), F32),
         ],
-        smem=(0,), hbm=(1, 4, 5, 6, 7, 8), hbm_outs=(0, 1), copies=28, moved=2e7,
+        smem=(0,), hbm=(1, 4, 5, 6, 7, 8, 9, 10), hbm_outs=(0, 1), copies=26, moved=2e7,
     )
     grad_before, grad_after = z_exchange(grad_low, grad_high, grad_swap)
     parts = everyone(parts.reshape(devices, piece, LANES))
@@ -932,34 +1018,34 @@
             ((rows_6, LANES), BF16),
             (back_shape, BF16),
             ((groups, size_z), F32),
-            ((chunks, 8, LANES), F32),
+            ((chunks, 8, LANES), BF16),
             ((3 * rows_6, size_z), BF16),
             ((groups * in_chan, size_z), BF16),
         ],
         smem=(0,), hbm=(1, 2, 5, 6, 7), copies=15, moved=2e7,
     )[0]
     parts, points = lax.optimization_barrier((parts, points))
+    shapes = [((out_chan, 27 * in_chan), F32), ((out_chan, 8 * out_chan), F32)]
+    flat = [((devices * piece, LANES), F32)]
     if aligned:
-        returned = local_call(
-            functools.partial(points_kernel, halves, in_chan),
-            [((in_chan, slot_total), BF16)],
-            everyone(points), moved=1e6,
+        both = local_call(
+            piece_kernel,
+            [((devices, halves * in_chan + piece, LANES), BF16)],
+            parts, points, moved=2e6,
         )[0]
+        returned, raw_sub, raw_down = local_call(
+            functools.partial(last_kernel, halves, in_chan),
+            [((in_chan, slot_total), BF16)] + shapes,
+            everyone(both), small, scratch=flat, moved=2e6,
+        )
     else:
         points = points.reshape(chunks, in_chan, together, slot_cap).transpose(0, 2, 1, 3)
         returned = everyone(points.reshape(devices, in_chan, slot_cap))
         returned = returned.transpose(1, 0, 2).reshape(in_chan, slot_total)
-
-    names = ("gz", "gx", "gy")
-    sizes = tuple(lax.axis_size(name) for name in names)
-    at = jnp.stack([lax.axis_index(name) for name in names]).astype(jnp.int32)
-    summed = local_call(piece_kernel, [((piece, LANES), BF16)], parts, moved=2e5)[0]
-    raw_sub, raw_down = local_call(
-        functools.partial(weights_kernel, in_chan, sizes),
-        [((out_chan, 27 * in_chan), F32), ((out_chan, 8 * out_chan), F32)],
-        at, gathered(summed, names, sizes), small,
-        scratch=[((devices * piece, LANES), F32)], smem=(0,), moved=5e5,
-    )
+        whole = local_call(sum_kernel, [((devices, piece, LANES), BF16)], parts)[0]
+        raw_sub, raw_down = local_call(
+            functools.partial(weights_kernel, in_chan), shapes, everyone(whole), small, scratch=flat
+        )
     return (
         coarse_out,
         returned,

time: 135 us -> 129 us (0.956)
  blocking collectives: 16.5 us -> 0 us
  waiting for transfers between devices: 36.6 us -> 45.9 us
  Pallas kernels: 39.6 us -> 45.7 us
  local copies, waits for them, and re-layouts: 6.18 us -> 3.37 us
  starting transfers between devices: 33.9 us -> 32.3 us
    all_to_all x4 -> x5, waiting for transfers between devices: 10.9 us -> 33.6 us  [everyone(): return lax.all_to_all(block, AXES, split_axis=0, concat_axis=0, tiled=True)]
    all_to_all x1 -> x0, blocking collectives: 16.5 us -> none  [everyone(): return lax.all_to_all(block, AXES, split_axis=0, concat_axis=0, tiled=True)]
    ppermute x7 -> x0, waiting for transfers between devices: 10.4 us -> none  [gathered(): parts = [piece] + [lax.ppermute(piece, name, pair) for pair in pairs]]
    ppermute x7 -> x0, starting transfers between devices: 8.45 us -> none  [gathered(): parts = [piece] + [lax.ppermute(piece, name, pair) for pair in pairs]]
    all_to_all x4 -> x5, starting transfers between devices: 18.4 us -> 25 us  [everyone(): return lax.all_to_all(block, AXES, split_axis=0, concat_axis=0, tiled=True)]
    pallas_call x16, Pallas kernels: 39.6 us -> 45.7 us  [local_call(): pl.pallas_call(kernel, out_shape=[pltpu.HBM(shape, kind) if i in hbm_outs...]
    ppermute x8, waiting for transfers between devices: 13.3 us -> 10.5 us  [swaps(): got.append(lax.ppermute(block, axis, pairs + [(j, i) for i, j in pairs]))]
    unnamed x39 -> x27, local copies, waits for them, and re-layouts: 4.1 us -> 1.32 us
  transfers between devices with their start and end apart: 21 -> 15, of which waited for: 10 -> 10; matrix products, arithmetic and copies ran while one was open for 2% -> 2% of each run, Pallas kernels for 10% -> 17%
where the time goes in v3:
time: 129 us; the launch traced here: 128 us
  waiting for transfers between devices  45.9 us (36%)
  Pallas kernels  45.7 us (35%)
  starting transfers between devices  32.3 us (25%)
  local copies, waits for them, and re-layouts  3.37 us (3%)
    pallas_call x16, Pallas kernels, local_call(): pl.pallas_call(kernel, out_shape=[pltpu.HBM(shape, kind) if i in hbm_outs...  45.7 us
    all_to_all x5, waiting for transfers between devices, everyone(): return lax.all_to_all(block, AXES, split_axis=0, concat_axis=0, tiled=True)  33.6 us
    all_to_all x5, starting transfers between devices, everyone(): return lax.all_to_all(block, AXES, split_axis=0, concat_axis=0, tiled=True)  25 us
    ppermute x8, waiting for transfers between devices, swaps(): got.append(lax.ppermute(block, axis, pairs + [(j, i) for i, j in pairs]))  10.5 us
    ppermute x8, starting transfers between devices, swaps(): got.append(lax.ppermute(block, axis, pairs + [(j, i) for i, j in pairs]))  6.84 us
  transfers between devices with their start and end apart: 15, of which 10 were waited for; matrix products, arithmetic and copies ran while one was open for 2% of the time, Pallas kernels for 17%

profile of v3, /device:TPU:0, one launch (start us, length us, event | category | flops | bytes accessed | tf_op | source)
XLA Modules:
  0.0 128.4 jit_solution(7996375937013441073)
XLA Ops:
  0.7 2.0 %shard_map.136 = bf16[32,72,128]{2,1,0:T(8,128)(2,1)} custom-call(s32[1,32]{1,0:T(1,128)} %counts_ref.1, bf16[32,8192]{1,0:T(8,128)(2,1)} %feats_ref.1, s32[64,128]{1,0:T(8,128)} %bitcast.38), custom_call_target="tpu_custom_call" | custom-call | bytes 2000000 | tf_op jit(solution)/shard_map/pallas_call | solution.py:37
  2.7 7.3 %all-to-all-start = ((bf16[32,72,128]{2,1,0:T(8,128)(2,1)}), bf16[32,72,128]{2,1,0:T(8,128)(2,1)S(1)}, u32[]{:S(2)}, u32[]{:S(2)}) async-start(bf16[32,72,128]{2,1,0:T(8,128)(2,1)} %shard_map.136), calls=%async_computation | async-start | bytes 1179648 | tf_op jit(solution)/shard_map/all_to_all | solution.py:104
  10.2 0.7 shard_map.137
  10.9 1.8 %collective-permute-start = (bf16[144,128]{1,0:T(8,128)(2,1)S(1)}, bf16[144,128]{1,0:T(8,128)(2,1)S(1)}, u32[]{:S(2)}, u32[]{:S(2)}) collective-permute-start(bf16[144,128]{1,0:T(8,128)(2,1)S(1)} %get-tuple-element.72), channel_id=1, source_target_pairs={{0,8},{16,24},{8,0},{24,16},{1,9},{17,25},{9,1},{25,17},{2,10},{18... | collective-permute-start | bytes 110600 | tf_op jit(solution)/shard_map/ppermute | solution.py:85
  15.0 1.5 %collective-permute-done.xf_ref = bf16[144,128]{1,0:T(8,128)(2,1)S(1)} collective-permute-done((bf16[144,128]{1,0:T(8,128)(2,1)S(1)}, bf16[144,128]{1,0:T(8,128)(2,1)S(1)}, u32[]{:S(2)}, u32[]{:S(2)}) %collective-permute-start) | collective-permute-done | bytes 36896 | tf_op jit(solution)/shard_map/ppermute | solution.py:85
  17.0 1.5 %collective-permute-start.2 = (bf16[272,128]{1,0:T(8,128)(2,1)S(1)}, bf16[272,128]{1,0:T(8,128)(2,1)S(1)}, u32[]{:S(2)}, u32[]{:S(2)}) collective-permute-start(bf16[272,128]{1,0:T(8,128)(2,1)S(1)} %get-tuple-element.74), channel_id=1, source_target_pairs={{0,2},{4,6},{2,0},{6,4},{1,3},{5,7},{3,1},{7,5},{8,10},{12,14},{10... | collective-permute-start | bytes 208904 | tf_op jit(solution)/shard_map/ppermute | solution.py:85
  19.3 3.1 %collective-permute-done.2.yf_ref = bf16[272,128]{1,0:T(8,128)(2,1)S(1)} collective-permute-done((bf16[272,128]{1,0:T(8,128)(2,1)S(1)}, bf16[272,128]{1,0:T(8,128)(2,1)S(1)}, u32[]{:S(2)}, u32[]{:S(2)}) %collective-permute-start.2) | collective-permute-done | bytes 69664 | tf_op jit(solution)/shard_map/ppermute | solution.py:85
  22.4 5.4 %all-to-all-done.recv_ref = bf16[32,72,128]{2,1,0:T(8,128)(2,1)S(1)} async-done(((bf16[32,72,128]{2,1,0:T(8,128)(2,1)}), bf16[32,72,128]{2,1,0:T(8,128)(2,1)S(1)}, u32[]{:S(2)}, u32[]{:S(2)}) %all-to-all-start) | async-done | bytes 589856 | tf_op jit(solution)/shard_map/all_to_all | solution.py:104
  27.8 3.8 %shard_map.139 = (bf16[256,256]{1,0:T(8,128)(2,1)S(1)}, bf16[256,256]{1,0:T(8,128)(2,1)S(1)}, bf16[32,8,128]{2,1,0:T(8,128)(2,1)}) custom-call(s32[3]{0:T(128)S(1)} %pad_add_fusion.sides_ref, bf16[32,72,128]{2,1,0:T(8,128)(2,1)S(1)} %all-to-all-done.recv_ref, f32[16,256]{1,0:T(8,128)S(1)} %convert_element_type.12.act_ref), custom_call_target="tpu_custom_call" | custom-call | bytes 20000000 | tf_op jit(solution)/shard_map/pallas_call | solution.py:37
  32.4 3.0 %shard_map.140 = (f32[40,256]{1,0:T(8,128)}, f32[1024,256]{1,0:T(8,128)}, f32[1280,256]{1,0:T(8,128)}) custom-call(s32[3]{0:T(128)S(1)} %pad_add_fusion.sides_ref, f32[16,256]{1,0:T(8,128)S(1)} %convert_element_type.12.act_ref, bf16[256,128]{1,0:T(8,128)(2,1)S(1)} %get-tuple-element.80.grad_ref.rest_1_, bf16[144,128]{1,0:T(8,128)(2,1)S(1)} %collective-permute-done.xf_ref, ...), custom_call_target="tpu_custom_call" | custom-call | bytes 4000000 | tf_op jit(solution)/shard_map/pallas_call | solution.py:37
  35.4 1.6 %collective-permute-done.4.gf_ref = bf16[256,256]{1,0:T(8,128)(2,1)S(1)} collective-permute-done((bf16[256,256]{1,0:T(8,128)(2,1)S(1)}, bf16[256,256]{1,0:T(8,128)(2,1)S(1)}, u32[]{:S(2)}, u32[]{:S(2)}) %collective-permute-start.4) | collective-permute-done | bytes 131104 | tf_op jit(solution)/shard_map/ppermute | solution.py:85
  37.6 0.8 collective-permute-start.6
  39.0 1.8 %shard_map.142 = (bf16[384,2304]{1,0:T(8,128)(2,1)}, bf16[128,3456]{1,0:T(8,128)(2,1)}, bf16[256,2304]{1,0:T(8,128)(2,1)S(1)}) custom-call(bf16[64,2304]{1,0:T(8,128)(2,1)S(1)} %copy.28.front_ref, bf16[32,3456]{1,0:T(8,128)(2,1)S(1)} %bitcast.28), custom_call_target="tpu_custom_call" | custom-call | bytes 4000000 | tf_op jit(solution)/shard_map/pallas_call | solution.py:37
  40.8 4.3 %collective-permute-done.6.yf_ref = bf16[512,256]{1,0:T(8,128)(2,1)S(1)} collective-permute-done((bf16[512,256]{1,0:T(8,128)(2,1)S(1)}, bf16[512,256]{1,0:T(8,128)(2,1)S(1)}, u32[]{:S(2)}, u32[]{:S(2)}) %collective-permute-start.6) | collective-permute-done | bytes 262176 | tf_op jit(solution)/shard_map/ppermute | solution.py:85
  45.1 0.8 shard_map.143
  46.0 1.9 %collective-permute-done.8.before_ref.after_ref = bf16[2048,128]{1,0:T(8,128)(2,1)S(1)} collective-permute-done((bf16[2048,128]{1,0:T(8,128)(2,1)S(1)}, bf16[2048,128]{1,0:T(8,128)(2,1)S(1)}, u32[]{:S(2)}, u32[]{:S(2)}) %collective-permute-start.8) | collective-permute-done | bytes 524320 | tf_op jit(solution)/shard_map/ppermute | solution.py:99
  47.9 4.4 %shard_map.144 = (f32[1024,256]{1,0:T(8,128)}, bf16[6144,256]{1,0:T(8,128)(2,1)}, f32[32,8,128]{2,1,0:T(8,128)}) custom-call(s32[3]{0:T(128)S(1)} %pad_add_fusion.sides_ref, bf16[2048,128]{1,0:T(8,128)(2,1)S(1)} %get-tuple-element.100.low_ref, bf16[2048,128]{1,0:T(8,128)(2,1)S(1)} %get-tuple-element.101.high_ref, ...), custom_call_target="tpu_custom_call" | custom-call | bytes 10000000 | tf_op jit(solution)/shard_map/pallas_call | solution.py:37
  52.2 8.3 %all-to-all-start.1 = ((f32[32,8,128]{2,1,0:T(8,128)}), f32[32,8,128]{2,1,0:T(8,128)S(1)}, u32[]{:S(2)}, u32[]{:S(2)}) async-start(f32[32,8,128]{2,1,0:T(8,128)} %get-tuple-element.105), calls=%async_computation.1 | async-start | bytes 262144 | tf_op jit(solution)/shard_map/all_to_all | solution.py:104
  60.5 5.2 %shard_map.145.hidden_ref.hidden_ring_ref = f32[1280,256]{1,0:T(8,128)} custom-call(bf16[384,2304]{1,0:T(8,128)(2,1)} %get-tuple-element.106.bands_ref, f32[40,256]{1,0:T(8,128)} %get-tuple-element.104.acts_ref, bf16[6144,256]{1,0:T(8,128)(2,1)} %get-tuple-element.107.stack_ref), custom_call_target="tpu_custom_call" | custom-call | bytes 10000000 | tf_op jit(solution)/shard_map/pallas_call | solution.py:37
  65.8 2.9 %all-to-all-done.1.stats_ref = f32[32,8,128]{2,1,0:T(8,128)S(1)} async-done(((f32[32,8,128]{2,1,0:T(8,128)}), f32[32,8,128]{2,1,0:T(8,128)S(1)}, u32[]{:S(2)}, u32[]{:S(2)}) %all-to-all-start.1) | async-done | bytes 131104 | tf_op jit(solution)/shard_map/all_to_all | solution.py:104
  68.7 4.3 %shard_map.146 = (f32[1024,256]{1,0:T(8,128)}, bf16[1024,256]{1,0:T(8,128)(2,1)}, f32[32,8,128]{2,1,0:T(8,128)}) custom-call(f32[32,8,128]{2,1,0:T(8,128)S(1)} %all-to-all-done.1.stats_ref, f32[8,128]{1,0:T(8,128)S(1)} %select_maximum_fusion.params_ref, f32[1024,256]{1,0:T(8,128)} %get-tuple-element.112.hidden_ref, f32[1024,256]{1,0:T(8,128)} %get-tuple-element.113.fine_ref, ...), custom_call_target="tpu_custom_call" | custom-call | bytes 5000000 | tf_op jit(solution)/shard_map/pallas_call | solution.py:37
  73.1 3.0 %all-to-all-start.2 = ((f32[32,8,128]{2,1,0:T(8,128)}), f32[32,8,128]{2,1,0:T(8,128)S(1)}, u32[]{:S(2)}, u32[]{:S(2)}) async-start(f32[32,8,128]{2,1,0:T(8,128)} %get-tuple-element.117), calls=%async_computation.2 | async-start | bytes 262144 | tf_op jit(solution)/shard_map/all_to_all | solution.py:104
  76.0 3.6 %shard_map.147 = (f32[1280,256]{1,0:T(8,128)}, bf16[4,64,128]{2,1,0:T(8,128)(2,1)S(1)}, f32[256,128]{1,0:T(8,128)S(1)}) custom-call(f32[32,8,128]{2,1,0:T(8,128)} %copy-done, f32[8,128]{1,0:T(8,128)S(1)} %select_maximum_fusion.params_ref, f32[1280,256]{1,0:T(8,128)} %shard_map.145.hidden_ref.hidden_ring_ref, f32[1280,256]{1,0:T(8,128)} %get-tuple-element.111.fine_ref, ...), custom_call_target="tpu_custom_call" | custom-call | bytes 5000000 | tf_op jit(solution)/shard_map/pallas_call | solution.py:37
  80.4 3.9 %all-to-all-done.2.sums_ref = f32[32,8,128]{2,1,0:T(8,128)S(1)} async-done(((f32[32,8,128]{2,1,0:T(8,128)}), f32[32,8,128]{2,1,0:T(8,128)S(1)}, u32[]{:S(2)}, u32[]{:S(2)}) %all-to-all-start.2) | async-done | bytes 131104 | tf_op jit(solution)/shard_map/all_to_all | solution.py:104
  84.2 6.1 %shard_map.148 = (bf16[2304,128]{1,0:T(8,128)(2,1)}, bf16[2304,128]{1,0:T(8,128)(2,1)}, bf16[2304,128]{1,0:T(8,128)(2,1)S(1)}, f32[8,128]{1,0:T(8,128)S(1)}, bf16[768,128]{1,0:T(8,128)(2,1)}) custom-call(s32[3]{0:T(128)S(1)} %pad_add_fusion.sides_ref, f32[32,8,128]{2,1,0:T(8,128)} %copy-done, f32[32,8,128]{2,1,0:T(8,128)S(1)} %all-to-all-done.2.sums_ref, ...), custom_call_target="tpu_custom_call" | custom-call | bytes 20000000 | tf_op jit(solution)/shard_map/pallas_call | solution.py:37
  90.7 2.6 %all-to-all-start.3 = ((bf16[32,24,128]{2,1,0:T(8,128)(2,1)}), bf16[32,24,128]{2,1,0:T(8,128)(2,1)S(1)}, u32[]{:S(2)}, u32[]{:S(2)}) async-start(bf16[32,24,128]{2,1,0:T(8,128)(2,1)} %bitcast.15), calls=%async_computation.3 | async-start | bytes 393216 | tf_op jit(solution)/shard_map/all_to_all | solution.py:104
  93.3 6.7 %shard_map.149.points_ref = bf16[32,64,128]{2,1,0:T(8,128)(2,1)S(1)} custom-call(s32[3]{0:T(128)S(1)} %pad_add_fusion.sides_ref, bf16[2304,128]{1,0:T(8,128)(2,1)} %get-tuple-element.125.front_ref, bf16[2304,128]{1,0:T(8,128)(2,1)} %get-tuple-element.126.rear_ref, bf16[2304,128]{1,0:T(8,128)(2,1)S(1)} %collective-permute-done.9.before_ref.after_ref, ...), custom_call_target="tpu_custom_call" | custom-call | bytes 20000000 | tf_op jit(solution)/shard_map/pallas_call | solution.py:37
  100.1 2.0 %all-to-all-done.3.parts_ref = bf16[32,24,128]{2,1,0:T(8,128)(2,1)S(1)} async-done(((bf16[32,24,128]{2,1,0:T(8,128)(2,1)}), bf16[32,24,128]{2,1,0:T(8,128)(2,1)S(1)}, u32[]{:S(2)}, u32[]{:S(2)}) %all-to-all-start.3) | async-done | bytes 196640 | tf_op jit(solution)/shard_map/all_to_all | solution.py:104
  102.1 0.9 shard_map.150
  103.0 3.8 %all-to-all-start.4 = ((bf16[32,88,128]{2,1,0:T(8,128)(2,1)}), bf16[32,88,128]{2,1,0:T(8,128)(2,1)S(1)}, u32[]{:S(2)}, u32[]{:S(2)}) async-start(bf16[32,88,128]{2,1,0:T(8,128)(2,1)} %shard_map.150), calls=%async_computation.4 | async-start | bytes 1441792 | tf_op jit(solution)/shard_map/all_to_all | solution.py:104
  108.1 19.4 %all-to-all-done.4.got_ref = bf16[32,88,128]{2,1,0:T(8,128)(2,1)S(1)} async-done(((bf16[32,88,128]{2,1,0:T(8,128)(2,1)}), bf16[32,88,128]{2,1,0:T(8,128)(2,1)S(1)}, u32[]{:S(2)}, u32[]{:S(2)}) %all-to-all-start.4) | async-done | bytes 720928 | tf_op jit(solution)/shard_map/all_to_all | solution.py:104
  127.4 1.0 shard_map.151
  (55 shorter events, 7.8 us)
Async XLA Ops:
  0.6 9.4 %copy-start.8 = (s32[4,4,256]{2,1,0:T(4,128)S(1)}, s32[4,4,256]{2,1,0:T(4,128)}, u32[]{:S(2)}) copy-start(s32[4,4,256]{2,1,0:T(4,128)} %param.12) | copy-start | bytes 49156
  0.6 9.5 %copy-start.7 = (bf16[64,2,2,128]{3,2,1,0:T(2,128)(2,1)S(1)}, bf16[64,2,2,128]{3,2,1,0:T(2,128)(2,1)}, u32[]{:S(2)}) copy-start(bf16[64,2,2,128]{3,2,1,0:T(2,128)(2,1)} %param.17) | copy-start | bytes 196612
  0.7 12.8 %copy-start.6 = (bf16[64,864]{1,0:T(8,128)(2,1)S(1)}, bf16[64,864]{1,0:T(8,128)(2,1)}, u32[]{:S(2)}) copy-start(bf16[64,864]{1,0:T(8,128)(2,1)} %param.13) | copy-start | bytes 331780
  2.7 10.9 %copy-start.4 = (bf16[64,512]{1,0:T(8,128)(2,1)S(1)}, bf16[64,512]{1,0:T(8,128)(2,1)}, u32[]{:S(2)}) copy-start(bf16[64,512]{1,0:T(8,128)(2,1)} %rest_3_.1) | copy-start | bytes 196612
  2.7 25.1 %all-to-all-start = ((bf16[32,72,128]{2,1,0:T(8,128)(2,1)}), bf16[32,72,128]{2,1,0:T(8,128)(2,1)S(1)}, u32[]{:S(2)}, u32[]{:S(2)}) async-start(bf16[32,72,128]{2,1,0:T(8,128)(2,1)} %shard_map.136), calls=%async_computation | async-start | bytes 1179648 | tf_op jit(solution)/shard_map/all_to_all | solution.py:104
  10.1 22.2 %copy-start.2 = (f32[16,256]{1,0:T(8,128)}, f32[16,256]{1,0:T(8,128)S(1)}, u32[]{:S(2)}) copy-start(f32[16,256]{1,0:T(8,128)S(1)} %convert_element_type.12.act_ref) | copy-start | bytes 49156
  10.9 21.4 %copy-start.3 = (bf16[256,128]{1,0:T(8,128)(2,1)}, bf16[256,128]{1,0:T(8,128)(2,1)S(1)}, u32[]{:S(2)}) copy-start(bf16[256,128]{1,0:T(8,128)(2,1)S(1)} %get-tuple-element.80.grad_ref.rest_1_) | copy-start | bytes 196612
  10.9 5.5 %collective-permute-start = (bf16[144,128]{1,0:T(8,128)(2,1)S(1)}, bf16[144,128]{1,0:T(8,128)(2,1)S(1)}, u32[]{:S(2)}, u32[]{:S(2)}) collective-permute-start(bf16[144,128]{1,0:T(8,128)(2,1)S(1)} %get-tuple-element.72), channel_id=1, source_target_pairs={{0,8},{16,24},{8,0},{24,16},{1,9},{17,25},{9,1},{25,17},{2,10},{18... | collective-permute-start | bytes 110600 | tf_op jit(solution)/shard_map/ppermute | solution.py:85
  12.8 3.7 %collective-permute-start.1 = (bf16[144,128]{1,0:T(8,128)(2,1)S(1)}, bf16[144,128]{1,0:T(8,128)(2,1)S(1)}, u32[]{:S(2)}, u32[]{:S(2)}) collective-permute-start(bf16[144,128]{1,0:T(8,128)(2,1)S(1)} %get-tuple-element.73), channel_id=1, source_target_pairs={{8,16},{16,8},{9,17},{17,9},{10,18},{18,10},{11,19},{19,11},{12,20... | collective-permute-start | bytes 110600 | tf_op jit(solution)/shard_map/ppermute | solution.py:85
  14.5 4.7 %copy-start.9 = (f32[64]{0:T(128)S(1)}, f32[64]{0:T(128)}, u32[]{:S(2)}) copy-start(f32[64]{0:T(128)} %param.16) | copy-start | bytes 772
  14.5 4.7 %copy-start.10 = (f32[64]{0:T(128)S(1)}, f32[64]{0:T(128)}, u32[]{:S(2)}) copy-start(f32[64]{0:T(128)} %param.15) | copy-start | bytes 772
  17.0 5.3 %collective-permute-start.2 = (bf16[272,128]{1,0:T(8,128)(2,1)S(1)}, bf16[272,128]{1,0:T(8,128)(2,1)S(1)}, u32[]{:S(2)}, u32[]{:S(2)}) collective-permute-start(bf16[272,128]{1,0:T(8,128)(2,1)S(1)} %get-tuple-element.74), channel_id=1, source_target_pairs={{0,2},{4,6},{2,0},{6,4},{1,3},{5,7},{3,1},{7,5},{8,10},{12,14},{10... | collective-permute-start | bytes 208904 | tf_op jit(solution)/shard_map/ppermute | solution.py:85
  18.6 3.8 %collective-permute-start.3 = (bf16[272,128]{1,0:T(8,128)(2,1)S(1)}, bf16[272,128]{1,0:T(8,128)(2,1)S(1)}, u32[]{:S(2)}, u32[]{:S(2)}) collective-permute-start(bf16[272,128]{1,0:T(8,128)(2,1)S(1)} %get-tuple-element.75), channel_id=1, source_target_pairs={{2,4},{4,2},{3,5},{5,3},{10,12},{12,10},{11,13},{13,11},{18,20},{2... | collective-permute-start | bytes 208904 | tf_op jit(solution)/shard_map/ppermute | solution.py:85
  31.6 5.4 %collective-permute-start.4 = (bf16[256,256]{1,0:T(8,128)(2,1)S(1)}, bf16[256,256]{1,0:T(8,128)(2,1)S(1)}, u32[]{:S(2)}, u32[]{:S(2)}) collective-permute-start(bf16[256,256]{1,0:T(8,128)(2,1)S(1)} %get-tuple-element.78.first_ref), channel_id=1, source_target_pairs={{0,8},{16,24},{8,0},{24,16},{1,9},{17,25},{9,1},{25,17},{2,10},{18... | collective-permute-start | bytes 393224 | tf_op jit(solution)/shard_map/ppermute | solution.py:85
  31.7 5.3 %collective-permute-start.5 = (bf16[256,256]{1,0:T(8,128)(2,1)S(1)}, bf16[256,256]{1,0:T(8,128)(2,1)S(1)}, u32[]{:S(2)}, u32[]{:S(2)}) collective-permute-start(bf16[256,256]{1,0:T(8,128)(2,1)S(1)} %get-tuple-element.79.second_ref), channel_id=1, source_target_pairs={{8,16},{16,8},{9,17},{17,9},{10,18},{18,10},{11,19},{19,11},{12,20... | collective-permute-start | bytes 393224 | tf_op jit(solution)/shard_map/ppermute | solution.py:85
  35.3 12.5 %copy-start.1 = (f32[40,256]{1,0:T(8,128)S(1)}, f32[40,256]{1,0:T(8,128)}, u32[]{:S(2)}) copy-start(f32[40,256]{1,0:T(8,128)} %get-tuple-element.104.acts_ref) | copy-start | bytes 122884
  37.6 7.5 %collective-permute-start.6 = (bf16[512,256]{1,0:T(8,128)(2,1)S(1)}, bf16[512,256]{1,0:T(8,128)(2,1)S(1)}, u32[]{:S(2)}, u32[]{:S(2)}) collective-permute-start(bf16[512,256]{1,0:T(8,128)(2,1)S(1)} %get-tuple-element.91), channel_id=1, source_target_pairs={{0,2},{4,6},{2,0},{6,4},{1,3},{5,7},{3,1},{7,5},{8,10},{12,14},{10... | collective-permute-start | bytes 786440 | tf_op jit(solution)/shard_map/ppermute | solution.py:85
  38.3 6.8 %collective-permute-start.7 = (bf16[512,256]{1,0:T(8,128)(2,1)S(1)}, bf16[512,256]{1,0:T(8,128)(2,1)S(1)}, u32[]{:S(2)}, u32[]{:S(2)}) collective-permute-start(bf16[512,256]{1,0:T(8,128)(2,1)S(1)} %get-tuple-element.92), channel_id=1, source_target_pairs={{2,4},{4,2},{3,5},{5,3},{10,12},{12,10},{11,13},{13,11},{18,20},{2... | collective-permute-start | bytes 786440 | tf_op jit(solution)/shard_map/ppermute | solution.py:85
  45.9 2.0 %collective-permute-start.8 = (bf16[2048,128]{1,0:T(8,128)(2,1)S(1)}, bf16[2048,128]{1,0:T(8,128)(2,1)S(1)}, u32[]{:S(2)}, u32[]{:S(2)}) collective-permute-start(bf16[2048,128]{1,0:T(8,128)(2,1)S(1)} %get-tuple-element.102), channel_id=1, source_target_pairs={{0,1},{1,0},{2,3},{3,2},{4,5},{5,4},{6,7},{7,6},{8,9},{9,8},{10,11... | collective-permute-start | bytes 1572872 | tf_op jit(solution)/shard_map/ppermute | solution.py:99
  52.2 16.5 %all-to-all-start.1 = ((f32[32,8,128]{2,1,0:T(8,128)}), f32[32,8,128]{2,1,0:T(8,128)S(1)}, u32[]{:S(2)}, u32[]{:S(2)}) async-start(f32[32,8,128]{2,1,0:T(8,128)} %get-tuple-element.105), calls=%async_computation.1 | async-start | bytes 262144 | tf_op jit(solution)/shard_map/all_to_all | solution.py:104
  68.7 7.3 %copy-start = (f32[32,8,128]{2,1,0:T(8,128)}, f32[32,8,128]{2,1,0:T(8,128)S(1)}, u32[]{:S(2)}) copy-start(f32[32,8,128]{2,1,0:T(8,128)S(1)} %all-to-all-done.1.stats_ref) | copy-start | bytes 393220
  73.1 11.1 %all-to-all-start.2 = ((f32[32,8,128]{2,1,0:T(8,128)}), f32[32,8,128]{2,1,0:T(8,128)S(1)}, u32[]{:S(2)}, u32[]{:S(2)}) async-start(f32[32,8,128]{2,1,0:T(8,128)} %get-tuple-element.117), calls=%async_computation.2 | async-start | bytes 262144 | tf_op jit(solution)/shard_map/all_to_all | solution.py:104
  79.7 0.7 copy-start.5
  90.4 3.0 %collective-permute-start.9 = (bf16[2304,128]{1,0:T(8,128)(2,1)S(1)}, bf16[2304,128]{1,0:T(8,128)(2,1)S(1)}, u32[]{:S(2)}, u32[]{:S(2)}) collective-permute-start(bf16[2304,128]{1,0:T(8,128)(2,1)S(1)} %get-tuple-element.127), channel_id=1, source_target_pairs={{0,1},{1,0},{2,3},{3,2},{4,5},{5,4},{6,7},{7,6},{8,9},{9,8},{10,11... | collective-permute-start | bytes 1769480 | tf_op jit(solution)/shard_map/ppermute | solution.py:99
  90.7 11.3 %all-to-all-start.3 = ((bf16[32,24,128]{2,1,0:T(8,128)(2,1)}), bf16[32,24,128]{2,1,0:T(8,128)(2,1)S(1)}, u32[]{:S(2)}, u32[]{:S(2)}) async-start(bf16[32,24,128]{2,1,0:T(8,128)(2,1)} %bitcast.15), calls=%async_computation.3 | async-start | bytes 393216 | tf_op jit(solution)/shard_map/all_to_all | solution.py:104
  103.0 24.4 %all-to-all-start.4 = ((bf16[32,88,128]{2,1,0:T(8,128)(2,1)}), bf16[32,88,128]{2,1,0:T(8,128)(2,1)S(1)}, u32[]{:S(2)}, u32[]{:S(2)}) async-start(bf16[32,88,128]{2,1,0:T(8,128)(2,1)} %shard_map.150), calls=%async_computation.4 | async-start | bytes 1441792 | tf_op jit(solution)/shard_map/all_to_all | solution.py:104

commit v4 on v3

--- a/solution.py
+++ b/solution.py
@@ -19,7 +19,7 @@
 
 
 def local_call(
-    kernel, outs, *args, scratch=(), scalars=(), smem=(), hbm=(), hbm_outs=(), copies=0, moved=0
+    kernel, outs, *args, scratch=(), scalars=(), smem=(), hbm=(), hbm_outs=(), copies=0, moved=0, aliases=None
 ):
     held = sum(math.prod(shape) * jnp.dtype(kind).itemsize for shape, kind in scratch)
     limit = held // 2**20 + 6
@@ -45,6 +45,7 @@
         ],
         out_specs=[far if i in hbm_outs else vmem for i in range(len(outs))],
         scratch_shapes=held,
+        input_output_aliases=aliases or {},
         compiler_params=pltpu.CompilerParams(vmem_limit_bytes=limit * 1024 * 1024),
         cost_estimate=pl.CostEstimate(flops=0, bytes_accessed=int(moved), transcendentals=0),
     )(*args)
@@ -252,8 +253,8 @@
 
 
 def fine_grad_kernel(
-    sides_ref, act_ref, grad_ref, xf_ref, xs_ref, yf_ref, ys_ref, down_ref, acts_ref, own_ref, ring_ref,
-    acts_held, wide, up, own, ring, sems,
+    sides_ref, act_ref, grad_ref, xf_ref, xs_ref, yf_ref, ys_ref, down_ref, acts_ref, own, ring_ref,
+    acts_held, wide, up, ring, sems,
 ):
     chan = grad_ref.shape[0] // 4
     depth = act_ref.shape[1]
@@ -305,8 +306,7 @@
                     elif column in RING:
                         n = RING.index(column)
                         ring[n * chan : (n + 1) * chan, :] = block
-    kept.append(started(own, own_ref, sems.at[1]))
-    kept.append(started(ring, ring_ref, sems.at[2]))
+    kept.append(started(ring, ring_ref, sems.at[1]))
     for copy in kept:
         copy.wait()
 
@@ -411,11 +411,35 @@
     return [wide[:chan, n : n + 1] for n in range(len(rows))]
 
 
+def stack_kernel(low_ref, high_ref, stack_ref):
+    rows = low_ref.shape[0] // 8
+    for x in range(8):
+        own = slice(x * rows, (x + 1) * rows)
+        low, high = low_ref[own, :], high_ref[own, :]
+        for n, step in enumerate((-1, 0, 1)):
+            tiles = (low, high) if step == 0 else shifted(low, high, high, low, step)
+            to = slice((x * 3 + n) * rows, (x * 3 + n + 1) * rows)
+            stack_ref[to, :LANES] = tiles[0]
+            stack_ref[to, LANES:] = tiles[1]
+
+
+def patch(stack, x, rows, before, after):
+    lane = lax.broadcasted_iota(jnp.int32, before.shape, 1)
+    to = slice(x * 3 * rows, (x * 3 + 1) * rows)
+    edge = pltpu.roll(before.astype(F32), 1, 1)
+    own = stack[to, :LANES].astype(F32)
+    stack[to, :LANES] = jnp.where(lane == 0, edge, own).astype(BF16)
+    to = slice((x * 3 + 2) * rows, (x * 3 + 3) * rows)
+    edge = pltpu.roll(after.astype(F32), LANES - 1, 1)
+    own = stack[to, LANES:].astype(F32)
+    stack[to, LANES:] = jnp.where(lane == LANES - 1, edge, own).astype(BF16)
+
+
 def conv_kernel(
-    only_two, sides_ref, low_ref, high_ref, before_ref, after_ref, bands_ref, acts_ref,
-    hidden_ref, stack_ref, stats_ref, hidden, stack, sems,
+    only_two, sides_ref, stack_in_ref, before_ref, after_ref, bands_ref, acts_ref,
+    hidden, stack_ref, stats_ref, stack, sems,
 ):
-    rows = low_ref.shape[0] // 8
+    rows = before_ref.shape[0] // 8
     depth = acts_ref.shape[1]
     chan = bands_ref.shape[0] // 4
     place = sides_ref[2]
@@ -424,15 +448,10 @@
     count = jnp.zeros((1, depth), F32)
     for x in range(8):
         own = slice(x * rows, (x + 1) * rows)
-        low, high = low_ref[own, :], high_ref[own, :]
         before, after = before_ref[own, :], after_ref[own, :]
         if only_two:
             before, after = keep(before, place != 0), keep(after, place == 0)
-        for n, step in enumerate((-1, 0, 1)):
-            tiles = (low, high) if step == 0 else shifted(low, high, before, after, step)
-            to = slice((x * 3 + n) * rows, (x * 3 + n + 1) * rows)
-            stack[to, :LANES] = tiles[0]
-            stack[to, LANES:] = tiles[1]
+        patch(stack, x, rows, before, after)
         own = rows_of(x, 3 * rows)
         kept.append(started(stack.at[own, :], stack_ref.at[own, :], sems.at[x]))
         p = x - 2
@@ -449,8 +468,6 @@
             hidden[n * chan : (n + 1) * chan, :] = block
             total = total + block
             count = count + act
-        own = rows_of(p - 1, 4 * chan)
-        kept.append(started(hidden.at[own, :], hidden_ref.at[own, :], sems.at[7 + p]))
     count = jnp.sum(count, axis=1, keepdims=True)
     total = jnp.sum(total, axis=1, keepdims=True)
     mean = total / jnp.maximum(count, 1.0)
@@ -506,23 +523,24 @@
 
 
 def norm_kernel(
-    columns, stats_ref, params_ref, hidden_ref, fine_ref, acts_ref, *rest
+    columns, stats_ref, params_ref, hidden, fine, acts_ref, *rest
 ):
     own = columns is OWN
     if own:
-        pre_ref, out_ref, sums_ref, stats, hidden, fine, acts, pre, outs, sems = rest
+        pre, out_ref, sums_ref, stats, acts, outs, sums_held, sems = rest
     else:
+        hidden_ref, fine_ref = hidden, fine
         (out_ref, grad_ref, mask_ref, down_ref, pre_ref, coarse_ref, raw_ref) = rest[:7]
-        stats, hidden, fine, acts, pre, outs, grads, taps, sems = rest[7:]
+        stats, hidden, fine, acts, pre, outs, grads, taps, raw, sems = rest[7:]
     chan = hidden.shape[0] // len(columns)
     depth = acts.shape[1]
     got_stats = started(stats_ref, stats, sems.at[0])
     got_acts = started(acts_ref, acts, sems.at[1])
     cuts = [n * chan for n in range(0, len(columns) + 1, 4)]
     parts = len(cuts) - 1
-    got = started_rows(hidden_ref, hidden, cuts, sems.at[pl.ds(2, parts)])
-    got_fine = started_rows(fine_ref, fine, cuts, sems.at[pl.ds(2 + parts, parts)])
     if not own:
+        got = started_rows(hidden_ref, hidden, cuts, sems.at[pl.ds(2, parts)])
+        got_fine = started_rows(fine_ref, fine, cuts, sems.at[pl.ds(2 + parts, parts)])
         last = 2 + 2 * parts
         got_down = [
             started(out_ref, outs, sems.at[last + 1]),
@@ -539,7 +557,7 @@
     sum_gain = jnp.zeros((chan, LANES), F32)
     got_acts.wait()
     for n, (p, q) in enumerate(columns):
-        if n % 4 == 0:
+        if n % 4 == 0 and not own:
             got[n // 4].wait()
             got_fine[n // 4].wait()
         own_rows = slice(n * chan, (n + 1) * chan)
@@ -560,18 +578,20 @@
                 sum_shift = sum_shift + grad
                 sum_gain = sum_gain + grad * normed
                 outs[own_rows, lanes] = (x * cdf * act).astype(BF16)
-    kept = [started(pre, pre_ref, sems.at[2 + 2 * parts])]
     if own:
-        kept.append(started(outs, out_ref, sems.at[3 + 2 * parts]))
+        kept = [started(outs, out_ref, sems.at[2])]
         sums = to_rows(
             [jnp.sum(sum_shift, axis=1, keepdims=True), jnp.sum(sum_gain, axis=1, keepdims=True)]
         )
         for d in range(sums_ref.shape[0]):
-            sums_ref[d] = sums
+            sums_held[d] = sums
+        kept.append(started(sums_held, sums_ref, sems.at[3]))
     else:
+        kept = [started(pre, pre_ref, sems.at[2 + 2 * parts])]
         for copy in got_down:
             copy.wait()
-        down_conv(outs, grads, mask_ref, down_ref, coarse_ref, raw_ref, taps)
+        down_conv(outs, grads, mask_ref, down_ref, coarse_ref, raw, taps)
+        kept.append(started(raw, raw_ref, sems.at[last + 3]))
     for copy in kept:
         copy.wait()
 
@@ -605,9 +625,9 @@
 
 
 def hidden_grad_kernel(
-    in_chan, sides_ref, stats_ref, sums_ref, params_ref, hidden_ref, hidden_ring_ref, pre_ref,
-    pre_ring_ref, acts_ref, stack_ref, raw_ref, front_ref, rear_ref, swap_ref, small_ref, out_ref,
-    stats, hidden, hidden_ring, pre, pre_ring, acts, stack, raw, front, rear, acc, sems,
+    in_chan, sides_ref, stats_ref, sums_ref, params_ref, hidden, hidden_ring_ref, pre,
+    pre_ring_ref, acts_ref, stack_ref, raw_ref, front, rear, swap_ref, small_ref, out_ref,
+    stats, hidden_ring, pre_ring, acts, stack, raw, acc, sems,
 ):
     chan = hidden.shape[0] // 16
     place = sides_ref[2]
@@ -615,11 +635,11 @@
     got_acts = started(acts_ref, acts, sems.at[1])
     got = []
     for n, (source, target) in enumerate(
-        ((hidden_ref, hidden), (pre_ref, pre), (hidden_ring_ref, hidden_ring), (pre_ring_ref, pre_ring))
+        ((hidden_ring_ref, hidden_ring), (pre_ring_ref, pre_ring))
     ):
         cuts = [n * chan for n in range(0, target.shape[0] // chan + 1, 4)]
         got.append(started_rows(source, target, cuts, sems.at[pl.ds(4 + 5 * n, len(cuts) - 1)]))
-    got = list(zip(*got[:2])) + list(zip(*got[2:]))
+    got = list(zip(*got))
     got_stack = started(
         stack_ref.at[pl.ds(stack.shape[0] // 6, stack.shape[0]), :], stack, sems.at[2]
     )
@@ -638,10 +658,9 @@
     ]
     weight = gain * inverse
     got_acts.wait()
-    kept = []
     for n, (p, q) in enumerate(OWN + RING):
-        if n % 4 == 0:
-            for copy in got[n // 4]:
+        if n % 4 == 0 and n >= 16:
+            for copy in got[n // 4 - 4]:
                 copy.wait()
         held_hidden, held_pre = (hidden, pre) if n < 16 else (hidden_ring, pre_ring)
         own = slice(n * chan, (n + 1) * chan) if n < 16 else slice((n - 16) * chan, (n - 15) * chan)
@@ -655,8 +674,6 @@
             tiles.append(((act * weight) * grad).astype(BF16))
             held[to, :] = tiles[-1]
         swap_ref[to, :] = jnp.where(place == 0, tiles[1], tiles[0])
-    kept.append(started(front, front_ref, sems.at[24]))
-    kept.append(started(rear, rear_ref, sems.at[25]))
     got_stack.wait()
     got_raw.wait()
     rows = stack.shape[0] // 6
@@ -698,34 +715,21 @@
     left = out_ref.shape[0] - tail - 4 * chan
     if left:
         out_ref[tail + 4 * chan :, :] = jnp.zeros((left, LANES), out_ref.dtype)
-    for copy in kept:
-        copy.wait()
 
 
 def point_grad_kernel(
-    only_two, halves, chan, sides_ref, front_ref, rear_ref, before_ref, after_ref, bands_ref, act_ref,
-    tags_ref, out_ref, front, rear, bands, acts, tags_held, stack, cells, sems,
+    only_two, halves, chan, sides_ref, front, rear, before_ref, after_ref, bands_ref, act_ref,
+    tags_ref, out_ref, bands, acts, tags_held, stack, cells, sems,
 ):
     rows = front.shape[0] // 6
     groups, depth = acts.shape
     place_z = sides_ref[2]
-    got = []
-    for x in range(6):
-        own = rows_of(x, rows)
-        got.append(
-            (
-                started(front_ref.at[own, :], front.at[own, :], sems.at[3 + x]),
-                started(rear_ref.at[own, :], rear.at[own, :], sems.at[9 + x]),
-            )
-        )
     late = [
         started(bands_ref, bands, sems.at[0]),
         started(act_ref, acts, sems.at[1]),
         started(tags_ref, tags_held, sems.at[2]),
     ]
     for x in range(6):
-        for copy in got[x]:
-            copy.wait()
         own = slice(x * rows, (x + 1) * rows)
         low, high = front[own, :], rear[own, :]
         before, after = before_ref[own, :], after_ref[own, :]
@@ -906,10 +910,9 @@
             ((40, size_z), F32),
             ((16 * out_chan, LANES), BF16),
             ((16 * out_chan, 2 * size_z), BF16),
-            own,
             ring,
         ],
-        smem=(0,), hbm_outs=(0, 1, 2), copies=3, moved=4e6,
+        smem=(0,), hbm_outs=(0, 2), copies=2, moved=4e6,
     )
     got_x, acts_wide, fine_grad = lax.optimization_barrier((got_x, acts_wide, fine_grad))
     ends = local_call(
@@ -936,15 +939,16 @@
         sides, *mine, *got_x, *got_y, smem=(0,), moved=3e6,
     )
     before, after = z_exchange(tile_low, tile_high, swap)
+    stack_shape = (3 * rows_64, size_z)
+    stack = local_call(stack_kernel, [(stack_shape, BF16)], tile_low, tile_high, moved=4e6)[0]
+    before, after, stack = lax.optimization_barrier((before, after, stack))
 
     stats_shape = (devices, 8, LANES)
-    stack_shape = (3 * rows_64, size_z)
-    own_hidden, stack, stats = local_call(
+    own_hidden, stack, stats, _ = local_call(
         functools.partial(conv_kernel, only_two),
-        [own, (stack_shape, BF16), (stats_shape, F32)],
-        sides, tile_low, tile_high, before, after, own_bands, acts_wide,
-        scratch=[own, (stack_shape, BF16)],
-        smem=(0,), hbm_outs=(0, 1), copies=12, moved=1e7,
+        [own, (stack_shape, BF16), (stats_shape, F32), (stack_shape, BF16)],
+        sides, stack, before, after, own_bands, acts_wide,
+        aliases={1: 3}, smem=(0,), hbm_outs=(1,), copies=8, moved=1e7,
     )
     stats_in = everyone(stats)
     ring_hidden = local_call(
@@ -960,8 +964,9 @@
         functools.partial(norm_kernel, OWN),
         [own, ((groups * out_chan, size_z), BF16), (stats_shape, F32)],
         stats_in, params, own_hidden, fine_grad[0], acts_wide,
-        scratch=held + [own, own, ((40, size_z), F32), own, ((groups * out_chan, size_z), BF16)],
-        hbm=(2, 3, 4), hbm_outs=(0, 1), copies=12, moved=5e6,
+        scratch=held
+        + [((40, size_z), F32), ((groups * out_chan, size_z), BF16), (stats_shape, F32)],
+        hbm=(4,), hbm_outs=(1, 2), copies=4, moved=5e6,
     )
     sums_in = everyone(sums)
     ring_pre, coarse, raw_down = local_call(
@@ -977,8 +982,9 @@
             ((groups * out_chan, size_z), BF16),
             ((4 * out_chan, LANES), BF16),
             ((8 * out_chan, 4 * LANES), BF16),
+            ((4 * out_chan, LANES), F32),
         ],
-        hbm=(0, 2, 3, 4, 5, 6), hbm_outs=(0,), copies=15, moved=5e6,
+        hbm=(0, 2, 3, 4, 5, 6), hbm_outs=(0, 2), copies=16, moved=5e6,
     )
     sums_in, ring_pre, raw_down = lax.optimization_barrier((sums_in, ring_pre, raw_down))
     half_x, half_y, half_z = size_x // 2, size_y // 2, size_z // 2
@@ -993,18 +999,14 @@
         stack, raw_down,
         scratch=[
             (stats_shape, F32),
-            own,
             ring,
-            own,
             ring,
             ((40, size_z), F32),
             ((rows_64 // 8 * 6 * 3, size_z), BF16),
             ((4 * out_chan, LANES), F32),
-            ((rows_6, LANES), BF16),
-            ((rows_6, LANES), BF16),
             ((3, 24 * in_chan, 4 * out_chan), F32),
         ],
-        smem=(0,), hbm=(1, 4, 5, 6, 7, 8, 9, 10), hbm_outs=(0, 1), copies=26, moved=2e7,
+        smem=(0,), hbm=(1, 5, 7, 8, 9, 10), copies=24, moved=2e7,
     )
     grad_before, grad_after = z_exchange(grad_low, grad_high, grad_swap)
     parts = everyone(parts.reshape(devices, piece, LANES))
@@ -1014,15 +1016,13 @@
         [((chunks, halves * in_chan, LANES), BF16)],
         sides, grad_low, grad_high, grad_before, grad_after, back_bands, acts, tags,
         scratch=[
-            ((rows_6, LANES), BF16),
-            ((rows_6, LANES), BF16),
             (back_shape, BF16),
             ((groups, size_z), F32),
             ((chunks, 8, LANES), BF16),
             ((3 * rows_6, size_z), BF16),
             ((groups * in_chan, size_z), BF16),
         ],
-        smem=(0,), hbm=(1, 2, 5, 6, 7), copies=15, moved=2e7,
+        smem=(0,), hbm=(5, 6, 7), copies=3, moved=2e7,
     )[0]
     parts, points = lax.optimization_barrier((parts, points))
     shapes = [((out_chan, 27 * in_chan), F32), ((out_chan, 8 * out_chan), F32)]

time: 129 us -> 126 us (0.977)
  Pallas kernels: 45.7 us -> 43.3 us
    pallas_call x16 -> x17, Pallas kernels: 45.7 us -> 43.3 us  [local_call(): pl.pallas_call(kernel, out_shape=[pltpu.HBM(shape, kind) if i in hbm_outs...]
  transfers between devices with their start and end apart: 15 -> 15, of which waited for: 10 -> 10; matrix products, arithmetic and copies ran while one was open for 2% -> 2% of each run, Pallas kernels for 17% -> 18%
where the time goes in v4:
time: 126 us
  waiting for transfers between devices  45.3 us (36%)
  Pallas kernels  43.3 us (34%)
  starting transfers between devices  32.1 us (25%)
  local copies, waits for them, and re-layouts  3.64 us (3%)
    pallas_call x17, Pallas kernels, local_call(): pl.pallas_call(kernel, out_shape=[pltpu.HBM(shape, kind) if i in hbm_outs...  43.3 us
    all_to_all x5, waiting for transfers between devices, everyone(): return lax.all_to_all(block, AXES, split_axis=0, concat_axis=0, tiled=True)  33.3 us
    all_to_all x5, starting transfers between devices, everyone(): return lax.all_to_all(block, AXES, split_axis=0, concat_axis=0, tiled=True)  25.1 us
    ppermute x8, waiting for transfers between devices, swaps(): got.append(lax.ppermute(block, axis, pairs + [(j, i) for i, j in pairs]))  10.9 us
    ppermute x8, starting transfers between devices, swaps(): got.append(lax.ppermute(block, axis, pairs + [(j, i) for i, j in pairs]))  6.58 us
  transfers between devices with their start and end apart: 15, of which 10 were waited for; matrix products, arithmetic and copies ran while one was open for 2% of the time, Pallas kernels for 18%

profile of v4, /device:TPU:0, one launch (start us, length us, event | category | flops | bytes accessed | tf_op | source)
XLA Modules:
  0.0 125.7 jit_solution(6611822024149097321)
XLA Ops:
  0.7 2.1 %shard_map.136 = bf16[32,72,128]{2,1,0:T(8,128)(2,1)} custom-call(s32[1,32]{1,0:T(1,128)} %counts_ref.1, bf16[32,8192]{1,0:T(8,128)(2,1)} %feats_ref.1, s32[64,128]{1,0:T(8,128)} %bitcast.39), custom_call_target="tpu_custom_call" | custom-call | bytes 2000000 | tf_op jit(solution)/shard_map/pallas_call | solution.py:37
  2.7 7.3 %all-to-all-start = ((bf16[32,72,128]{2,1,0:T(8,128)(2,1)}), bf16[32,72,128]{2,1,0:T(8,128)(2,1)S(1)}, u32[]{:S(2)}, u32[]{:S(2)}) async-start(bf16[32,72,128]{2,1,0:T(8,128)(2,1)} %shard_map.136), calls=%async_computation | async-start | bytes 1179648 | tf_op jit(solution)/shard_map/all_to_all | solution.py:105
  10.2 0.7 shard_map.137
  11.0 1.8 %collective-permute-start = (bf16[144,128]{1,0:T(8,128)(2,1)S(1)}, bf16[144,128]{1,0:T(8,128)(2,1)S(1)}, u32[]{:S(2)}, u32[]{:S(2)}) collective-permute-start(bf16[144,128]{1,0:T(8,128)(2,1)S(1)} %get-tuple-element.75), channel_id=1, source_target_pairs={{0,8},{16,24},{8,0},{24,16},{1,9},{17,25},{9,1},{25,17},{2,10},{18... | collective-permute-start | bytes 110600 | tf_op jit(solution)/shard_map/ppermute | solution.py:86
  15.0 1.5 %collective-permute-done.xf_ref = bf16[144,128]{1,0:T(8,128)(2,1)S(1)} collective-permute-done((bf16[144,128]{1,0:T(8,128)(2,1)S(1)}, bf16[144,128]{1,0:T(8,128)(2,1)S(1)}, u32[]{:S(2)}, u32[]{:S(2)}) %collective-permute-start) | collective-permute-done | bytes 36896 | tf_op jit(solution)/shard_map/ppermute | solution.py:86
  17.1 1.5 %collective-permute-start.2 = (bf16[272,128]{1,0:T(8,128)(2,1)S(1)}, bf16[272,128]{1,0:T(8,128)(2,1)S(1)}, u32[]{:S(2)}, u32[]{:S(2)}) collective-permute-start(bf16[272,128]{1,0:T(8,128)(2,1)S(1)} %get-tuple-element.77), channel_id=1, source_target_pairs={{0,2},{4,6},{2,0},{6,4},{1,3},{5,7},{3,1},{7,5},{8,10},{12,14},{10... | collective-permute-start | bytes 208904 | tf_op jit(solution)/shard_map/ppermute | solution.py:86
  19.3 3.1 %collective-permute-done.2.yf_ref = bf16[272,128]{1,0:T(8,128)(2,1)S(1)} collective-permute-done((bf16[272,128]{1,0:T(8,128)(2,1)S(1)}, bf16[272,128]{1,0:T(8,128)(2,1)S(1)}, u32[]{:S(2)}, u32[]{:S(2)}) %collective-permute-start.2) | collective-permute-done | bytes 69664 | tf_op jit(solution)/shard_map/ppermute | solution.py:86
  22.4 5.4 %all-to-all-done.recv_ref = bf16[32,72,128]{2,1,0:T(8,128)(2,1)S(1)} async-done(((bf16[32,72,128]{2,1,0:T(8,128)(2,1)}), bf16[32,72,128]{2,1,0:T(8,128)(2,1)S(1)}, u32[]{:S(2)}, u32[]{:S(2)}) %all-to-all-start) | async-done | bytes 589856 | tf_op jit(solution)/shard_map/all_to_all | solution.py:105
  27.8 3.8 %shard_map.139 = (bf16[256,256]{1,0:T(8,128)(2,1)S(1)}, bf16[256,256]{1,0:T(8,128)(2,1)S(1)}, bf16[32,8,128]{2,1,0:T(8,128)(2,1)}) custom-call(s32[3]{0:T(128)S(1)} %pad_add_fusion.sides_ref, bf16[32,72,128]{2,1,0:T(8,128)(2,1)S(1)} %all-to-all-done.recv_ref, f32[16,256]{1,0:T(8,128)S(1)} %convert_element_type.12.act_ref), custom_call_target="tpu_custom_call" | custom-call | bytes 20000000 | tf_op jit(solution)/shard_map/pallas_call | solution.py:37
  32.4 2.6 %shard_map.140 = (f32[40,256]{1,0:T(8,128)}, f32[1024,256]{1,0:T(8,128)S(1)}, f32[1280,256]{1,0:T(8,128)}) custom-call(s32[3]{0:T(128)S(1)} %pad_add_fusion.sides_ref, f32[16,256]{1,0:T(8,128)S(1)} %convert_element_type.12.act_ref, bf16[256,128]{1,0:T(8,128)(2,1)S(1)} %get-tuple-element.83.grad_ref.rest_1_, ...), custom_call_target="tpu_custom_call" | custom-call | bytes 4000000 | tf_op jit(solution)/shard_map/pallas_call | solution.py:37
  34.9 2.0 %collective-permute-done.4.gf_ref = bf16[256,256]{1,0:T(8,128)(2,1)S(1)} collective-permute-done((bf16[256,256]{1,0:T(8,128)(2,1)S(1)}, bf16[256,256]{1,0:T(8,128)(2,1)S(1)}, u32[]{:S(2)}, u32[]{:S(2)}) %collective-permute-start.4) | collective-permute-done | bytes 131104 | tf_op jit(solution)/shard_map/ppermute | solution.py:86
  38.8 1.9 %shard_map.142 = (bf16[384,2304]{1,0:T(8,128)(2,1)}, bf16[128,3456]{1,0:T(8,128)(2,1)}, bf16[256,2304]{1,0:T(8,128)(2,1)S(1)}) custom-call(bf16[64,2304]{1,0:T(8,128)(2,1)S(1)} %copy.29.front_ref, bf16[32,3456]{1,0:T(8,128)(2,1)S(1)} %bitcast.28), custom_call_target="tpu_custom_call" | custom-call | bytes 4000000 | tf_op jit(solution)/shard_map/pallas_call | solution.py:37
  40.6 4.3 %collective-permute-done.6.yf_ref = bf16[512,256]{1,0:T(8,128)(2,1)S(1)} collective-permute-done((bf16[512,256]{1,0:T(8,128)(2,1)S(1)}, bf16[512,256]{1,0:T(8,128)(2,1)S(1)}, u32[]{:S(2)}, u32[]{:S(2)}) %collective-permute-start.6) | collective-permute-done | bytes 262176 | tf_op jit(solution)/shard_map/ppermute | solution.py:86
  44.9 0.8 shard_map.143
  45.8 0.8 shard_map.144.stack_in_ref
  46.5 1.1 collective-permute-done.8.before_ref.after_ref
  47.7 4.0 %shard_map.145 = (f32[1024,256]{1,0:T(8,128)S(1)}, bf16[6144,256]{1,0:T(8,128)(2,1)}, f32[32,8,128]{2,1,0:T(8,128)}, bf16[6144,256]{1,0:T(8,128)(2,1)S(1)}) custom-call(s32[3]{0:T(128)S(1)} %pad_add_fusion.sides_ref, bf16[6144,256]{1,0:T(8,128)(2,1)S(1)} %shard_map.144.stack_in_ref, ...), custom_call_target="tpu_custom_call", output_to_operand_aliasing={{3}: (1, {})} | custom-call | bytes 10000000 | tf_op jit(solution)/shard_map/pallas_call | solution.py:37
  51.7 8.7 %all-to-all-start.1 = ((f32[32,8,128]{2,1,0:T(8,128)}), f32[32,8,128]{2,1,0:T(8,128)S(1)}, u32[]{:S(2)}, u32[]{:S(2)}) async-start(f32[32,8,128]{2,1,0:T(8,128)} %get-tuple-element.111), calls=%async_computation.1 | async-start | bytes 262144 | tf_op jit(solution)/shard_map/all_to_all | solution.py:105
  60.4 5.2 %shard_map.146.hidden.hidden_ring_ref = f32[1280,256]{1,0:T(8,128)} custom-call(bf16[384,2304]{1,0:T(8,128)(2,1)} %get-tuple-element.112.bands_ref, f32[40,256]{1,0:T(8,128)} %get-tuple-element.110.acts_ref, bf16[6144,256]{1,0:T(8,128)(2,1)} %get-tuple-element.113.stack_ref), custom_call_target="tpu_custom_call" | custom-call | bytes 10000000 | tf_op jit(solution)/shard_map/pallas_call | solution.py:37
  65.7 2.7 %all-to-all-done.1.stats_ref = f32[32,8,128]{2,1,0:T(8,128)S(1)} async-done(((f32[32,8,128]{2,1,0:T(8,128)}), f32[32,8,128]{2,1,0:T(8,128)S(1)}, u32[]{:S(2)}, u32[]{:S(2)}) %all-to-all-start.1) | async-done | bytes 131104 | tf_op jit(solution)/shard_map/all_to_all | solution.py:105
  68.4 2.9 %shard_map.147 = (f32[1024,256]{1,0:T(8,128)S(1)}, bf16[1024,256]{1,0:T(8,128)(2,1)}, f32[32,8,128]{2,1,0:T(8,128)}) custom-call(f32[32,8,128]{2,1,0:T(8,128)S(1)} %all-to-all-done.1.stats_ref, f32[8,128]{1,0:T(8,128)S(1)} %select_maximum_fusion.params_ref, f32[1024,256]{1,0:T(8,128)S(1)} %get-tuple-element.118.hidden, ...), custom_call_target="tpu_custom_call" | custom-call | bytes 5000000 | tf_op jit(solution)/shard_map/pallas_call | solution.py:37
  71.3 3.0 %all-to-all-start.2 = ((f32[32,8,128]{2,1,0:T(8,128)}), f32[32,8,128]{2,1,0:T(8,128)S(1)}, u32[]{:S(2)}, u32[]{:S(2)}) async-start(f32[32,8,128]{2,1,0:T(8,128)} %get-tuple-element.123), calls=%async_computation.2 | async-start | bytes 262144 | tf_op jit(solution)/shard_map/all_to_all | solution.py:105
  74.3 4.0 %shard_map.148 = (f32[1280,256]{1,0:T(8,128)}, bf16[4,64,128]{2,1,0:T(8,128)(2,1)S(1)}, f32[256,128]{1,0:T(8,128)}) custom-call(f32[32,8,128]{2,1,0:T(8,128)} %copy-done, f32[8,128]{1,0:T(8,128)S(1)} %select_maximum_fusion.params_ref, f32[1280,256]{1,0:T(8,128)} %shard_map.146.hidden.hidden_ring_ref, f32[1280,256]{1,0:T(8,128)} %get-tuple-element.117.fine, ...), custom_call_target="tpu_custom_call" | custom-call | bytes 5000000 | tf_op jit(solution)/shard_map/pallas_call | solution.py:37
  79.0 3.5 %all-to-all-done.2.sums_ref = f32[32,8,128]{2,1,0:T(8,128)S(1)} async-done(((f32[32,8,128]{2,1,0:T(8,128)}), f32[32,8,128]{2,1,0:T(8,128)S(1)}, u32[]{:S(2)}, u32[]{:S(2)}) %all-to-all-start.2) | async-done | bytes 131104 | tf_op jit(solution)/shard_map/all_to_all | solution.py:105
  82.5 5.1 %shard_map.149 = (bf16[2304,128]{1,0:T(8,128)(2,1)S(1)}, bf16[2304,128]{1,0:T(8,128)(2,1)S(1)}, bf16[2304,128]{1,0:T(8,128)(2,1)}, f32[8,128]{1,0:T(8,128)S(1)}, bf16[768,128]{1,0:T(8,128)(2,1)S(1)}) custom-call(s32[3]{0:T(128)S(1)} %pad_add_fusion.sides_ref, f32[32,8,128]{2,1,0:T(8,128)} %copy-done, f32[32,8,128]{2,1,0:T(8,128)S(1)} %all-to-all-done.2.sums_ref, ...), custom_call_target="tpu_custom_call" | custom-call | bytes 20000000 | tf_op jit(solution)/shard_map/pallas_call | solution.py:37
  88.3 2.6 %all-to-all-start.3 = ((bf16[32,24,128]{2,1,0:T(8,128)(2,1)}), bf16[32,24,128]{2,1,0:T(8,128)(2,1)S(1)}, u32[]{:S(2)}, u32[]{:S(2)}) async-start(bf16[32,24,128]{2,1,0:T(8,128)(2,1)} %bitcast.30), calls=%async_computation.3 | async-start | bytes 393216 | tf_op jit(solution)/shard_map/all_to_all | solution.py:105
  90.9 6.4 %shard_map.150.points_ref = bf16[32,64,128]{2,1,0:T(8,128)(2,1)S(1)} custom-call(s32[3]{0:T(128)S(1)} %pad_add_fusion.sides_ref, bf16[2304,128]{1,0:T(8,128)(2,1)S(1)} %get-tuple-element.131.front, bf16[2304,128]{1,0:T(8,128)(2,1)S(1)} %get-tuple-element.132.rear, bf16[2304,128]{1,0:T(8,128)(2,1)S(1)} %collective-permute-done.9.before_ref.after_ref, ...), custom_call_target="tpu_custom_call" | custom-call | bytes 20000000 | tf_op jit(solution)/shard_map/pallas_call | solution.py:37
  97.3 2.3 %all-to-all-done.3.parts_ref = bf16[32,24,128]{2,1,0:T(8,128)(2,1)S(1)} async-done(((bf16[32,24,128]{2,1,0:T(8,128)(2,1)}), bf16[32,24,128]{2,1,0:T(8,128)(2,1)S(1)}, u32[]{:S(2)}, u32[]{:S(2)}) %all-to-all-start.3) | async-done | bytes 196640 | tf_op jit(solution)/shard_map/all_to_all | solution.py:105
  99.6 0.9 shard_map.151
  100.5 3.5 %all-to-all-start.4 = ((bf16[32,88,128]{2,1,0:T(8,128)(2,1)}), bf16[32,88,128]{2,1,0:T(8,128)(2,1)S(1)}, u32[]{:S(2)}, u32[]{:S(2)}) async-start(bf16[32,88,128]{2,1,0:T(8,128)(2,1)} %shard_map.151), calls=%async_computation.4 | async-start | bytes 1441792 | tf_op jit(solution)/shard_map/all_to_all | solution.py:105
  105.3 19.3 %all-to-all-done.4.got_ref = bf16[32,88,128]{2,1,0:T(8,128)(2,1)S(1)} async-done(((bf16[32,88,128]{2,1,0:T(8,128)(2,1)}), bf16[32,88,128]{2,1,0:T(8,128)(2,1)S(1)}, u32[]{:S(2)}, u32[]{:S(2)}) %all-to-all-start.4) | async-done | bytes 720928 | tf_op jit(solution)/shard_map/all_to_all | solution.py:105
  124.6 1.0 shard_map.152
  (62 shorter events, 8.6 us)
Async XLA Ops:
  0.6 9.4 %copy-start.11 = (s32[4,4,256]{2,1,0:T(4,128)S(1)}, s32[4,4,256]{2,1,0:T(4,128)}, u32[]{:S(2)}) copy-start(s32[4,4,256]{2,1,0:T(4,128)} %param.12) | copy-start | bytes 49156
  0.6 9.5 %copy-start.10 = (bf16[64,2,2,128]{3,2,1,0:T(2,128)(2,1)S(1)}, bf16[64,2,2,128]{3,2,1,0:T(2,128)(2,1)}, u32[]{:S(2)}) copy-start(bf16[64,2,2,128]{3,2,1,0:T(2,128)(2,1)} %param.17) | copy-start | bytes 196612
  0.7 12.8 %copy-start.9 = (bf16[64,864]{1,0:T(8,128)(2,1)S(1)}, bf16[64,864]{1,0:T(8,128)(2,1)}, u32[]{:S(2)}) copy-start(bf16[64,864]{1,0:T(8,128)(2,1)} %param.13) | copy-start | bytes 331780
  0.7 13.0 %copy-start.4 = (bf16[64,512]{1,0:T(8,128)(2,1)S(1)}, bf16[64,512]{1,0:T(8,128)(2,1)}, u32[]{:S(2)}) copy-start(bf16[64,512]{1,0:T(8,128)(2,1)} %rest_3_.1) | copy-start | bytes 196612
  2.7 25.1 %all-to-all-start = ((bf16[32,72,128]{2,1,0:T(8,128)(2,1)}), bf16[32,72,128]{2,1,0:T(8,128)(2,1)S(1)}, u32[]{:S(2)}, u32[]{:S(2)}) async-start(bf16[32,72,128]{2,1,0:T(8,128)(2,1)} %shard_map.136), calls=%async_computation | async-start | bytes 1179648 | tf_op jit(solution)/shard_map/all_to_all | solution.py:105
  10.1 22.2 %copy-start.2 = (f32[16,256]{1,0:T(8,128)}, f32[16,256]{1,0:T(8,128)S(1)}, u32[]{:S(2)}) copy-start(f32[16,256]{1,0:T(8,128)S(1)} %convert_element_type.12.act_ref) | copy-start | bytes 49156
  10.9 21.4 %copy-start.3 = (bf16[256,128]{1,0:T(8,128)(2,1)}, bf16[256,128]{1,0:T(8,128)(2,1)S(1)}, u32[]{:S(2)}) copy-start(bf16[256,128]{1,0:T(8,128)(2,1)S(1)} %get-tuple-element.83.grad_ref.rest_1_) | copy-start | bytes 196612
  11.0 5.5 %collective-permute-start = (bf16[144,128]{1,0:T(8,128)(2,1)S(1)}, bf16[144,128]{1,0:T(8,128)(2,1)S(1)}, u32[]{:S(2)}, u32[]{:S(2)}) collective-permute-start(bf16[144,128]{1,0:T(8,128)(2,1)S(1)} %get-tuple-element.75), channel_id=1, source_target_pairs={{0,8},{16,24},{8,0},{24,16},{1,9},{17,25},{9,1},{25,17},{2,10},{18... | collective-permute-start | bytes 110600 | tf_op jit(solution)/shard_map/ppermute | solution.py:86
  12.8 3.7 %collective-permute-start.1 = (bf16[144,128]{1,0:T(8,128)(2,1)S(1)}, bf16[144,128]{1,0:T(8,128)(2,1)S(1)}, u32[]{:S(2)}, u32[]{:S(2)}) collective-permute-start(bf16[144,128]{1,0:T(8,128)(2,1)S(1)} %get-tuple-element.76), channel_id=1, source_target_pairs={{8,16},{16,8},{9,17},{17,9},{10,18},{18,10},{11,19},{19,11},{12,20... | collective-permute-start | bytes 110600 | tf_op jit(solution)/shard_map/ppermute | solution.py:86
  14.5 4.8 %copy-start.12 = (f32[64]{0:T(128)S(1)}, f32[64]{0:T(128)}, u32[]{:S(2)}) copy-start(f32[64]{0:T(128)} %param.16) | copy-start | bytes 772
  14.5 4.8 %copy-start.13 = (f32[64]{0:T(128)S(1)}, f32[64]{0:T(128)}, u32[]{:S(2)}) copy-start(f32[64]{0:T(128)} %param.15) | copy-start | bytes 772
  17.1 5.3 %collective-permute-start.2 = (bf16[272,128]{1,0:T(8,128)(2,1)S(1)}, bf16[272,128]{1,0:T(8,128)(2,1)S(1)}, u32[]{:S(2)}, u32[]{:S(2)}) collective-permute-start(bf16[272,128]{1,0:T(8,128)(2,1)S(1)} %get-tuple-element.77), channel_id=1, source_target_pairs={{0,2},{4,6},{2,0},{6,4},{1,3},{5,7},{3,1},{7,5},{8,10},{12,14},{10... | collective-permute-start | bytes 208904 | tf_op jit(solution)/shard_map/ppermute | solution.py:86
  18.6 3.8 %collective-permute-start.3 = (bf16[272,128]{1,0:T(8,128)(2,1)S(1)}, bf16[272,128]{1,0:T(8,128)(2,1)S(1)}, u32[]{:S(2)}, u32[]{:S(2)}) collective-permute-start(bf16[272,128]{1,0:T(8,128)(2,1)S(1)} %get-tuple-element.78), channel_id=1, source_target_pairs={{2,4},{4,2},{3,5},{5,3},{10,12},{12,10},{11,13},{13,11},{18,20},{2... | collective-permute-start | bytes 208904 | tf_op jit(solution)/shard_map/ppermute | solution.py:86
  31.6 5.4 %collective-permute-start.4 = (bf16[256,256]{1,0:T(8,128)(2,1)S(1)}, bf16[256,256]{1,0:T(8,128)(2,1)S(1)}, u32[]{:S(2)}, u32[]{:S(2)}) collective-permute-start(bf16[256,256]{1,0:T(8,128)(2,1)S(1)} %get-tuple-element.81.first_ref), channel_id=1, source_target_pairs={{0,8},{16,24},{8,0},{24,16},{1,9},{17,25},{9,1},{25,17},{2,10},{18... | collective-permute-start | bytes 393224 | tf_op jit(solution)/shard_map/ppermute | solution.py:86
  31.7 5.3 %collective-permute-start.5 = (bf16[256,256]{1,0:T(8,128)(2,1)S(1)}, bf16[256,256]{1,0:T(8,128)(2,1)S(1)}, u32[]{:S(2)}, u32[]{:S(2)}) collective-permute-start(bf16[256,256]{1,0:T(8,128)(2,1)S(1)} %get-tuple-element.82.second_ref), channel_id=1, source_target_pairs={{8,16},{16,8},{9,17},{17,9},{10,18},{18,10},{11,19},{19,11},{12,20... | collective-permute-start | bytes 393224 | tf_op jit(solution)/shard_map/ppermute | solution.py:86
  37.6 7.3 %collective-permute-start.6 = (bf16[512,256]{1,0:T(8,128)(2,1)S(1)}, bf16[512,256]{1,0:T(8,128)(2,1)S(1)}, u32[]{:S(2)}, u32[]{:S(2)}) collective-permute-start(bf16[512,256]{1,0:T(8,128)(2,1)S(1)} %get-tuple-element.94), channel_id=1, source_target_pairs={{0,2},{4,6},{2,0},{6,4},{1,3},{5,7},{3,1},{7,5},{8,10},{12,14},{10... | collective-permute-start | bytes 786440 | tf_op jit(solution)/shard_map/ppermute | solution.py:86
  38.1 6.8 %collective-permute-start.7 = (bf16[512,256]{1,0:T(8,128)(2,1)S(1)}, bf16[512,256]{1,0:T(8,128)(2,1)S(1)}, u32[]{:S(2)}, u32[]{:S(2)}) collective-permute-start(bf16[512,256]{1,0:T(8,128)(2,1)S(1)} %get-tuple-element.95), channel_id=1, source_target_pairs={{2,4},{4,2},{3,5},{5,3},{10,12},{12,10},{11,13},{13,11},{18,20},{2... | collective-permute-start | bytes 786440 | tf_op jit(solution)/shard_map/ppermute | solution.py:86
  45.7 2.0 %collective-permute-start.8 = (bf16[2048,128]{1,0:T(8,128)(2,1)S(1)}, bf16[2048,128]{1,0:T(8,128)(2,1)S(1)}, u32[]{:S(2)}, u32[]{:S(2)}) collective-permute-start(bf16[2048,128]{1,0:T(8,128)(2,1)S(1)} %get-tuple-element.103), channel_id=1, source_target_pairs={{0,1},{1,0},{2,3},{3,2},{4,5},{5,4},{6,7},{7,6},{8,9},{9,8},{10,11... | collective-permute-start | bytes 1572872 | tf_op jit(solution)/shard_map/ppermute | solution.py:100
  45.8 1.9 %copy-start.1 = (f32[40,256]{1,0:T(8,128)S(1)}, f32[40,256]{1,0:T(8,128)}, u32[]{:S(2)}) copy-start(f32[40,256]{1,0:T(8,128)} %get-tuple-element.110.acts_ref) | copy-start | bytes 122884
  51.7 16.7 %all-to-all-start.1 = ((f32[32,8,128]{2,1,0:T(8,128)}), f32[32,8,128]{2,1,0:T(8,128)S(1)}, u32[]{:S(2)}, u32[]{:S(2)}) async-start(f32[32,8,128]{2,1,0:T(8,128)} %get-tuple-element.111), calls=%async_computation.1 | async-start | bytes 262144 | tf_op jit(solution)/shard_map/all_to_all | solution.py:105
  65.6 8.7 %copy-start.5 = (bf16[64,512]{1,0:T(8,128)(2,1)S(1)}, bf16[64,512]{1,0:T(8,128)(2,1)}, u32[]{:S(2)}) copy-start(bf16[64,512]{1,0:T(8,128)(2,1)} %rest_3_.1) | copy-start | bytes 196612
  68.4 5.9 %copy-start = (f32[32,8,128]{2,1,0:T(8,128)}, f32[32,8,128]{2,1,0:T(8,128)S(1)}, u32[]{:S(2)}) copy-start(f32[32,8,128]{2,1,0:T(8,128)S(1)} %all-to-all-done.1.stats_ref) | copy-start | bytes 393220
  71.3 11.2 %all-to-all-start.2 = ((f32[32,8,128]{2,1,0:T(8,128)}), f32[32,8,128]{2,1,0:T(8,128)S(1)}, u32[]{:S(2)}, u32[]{:S(2)}) async-start(f32[32,8,128]{2,1,0:T(8,128)} %get-tuple-element.123), calls=%async_computation.2 | async-start | bytes 262144 | tf_op jit(solution)/shard_map/all_to_all | solution.py:105
  78.3 0.6 copy-start.7
  87.6 0.7 copy-start.6
  87.6 3.3 %collective-permute-start.9 = (bf16[2304,128]{1,0:T(8,128)(2,1)}, bf16[2304,128]{1,0:T(8,128)(2,1)S(1)}, u32[]{:S(2)}, u32[]{:S(2)}) collective-permute-start(bf16[2304,128]{1,0:T(8,128)(2,1)} %get-tuple-element.133), channel_id=1, source_target_pairs={{0,1},{1,0},{2,3},{3,2},{4,5},{5,4},{6,7},{7,6},{8,9},{9,8},{10,11... | collective-permute-start | bytes 1769480 | tf_op jit(solution)/shard_map/ppermute | solution.py:100
  88.3 11.3 %all-to-all-start.3 = ((bf16[32,24,128]{2,1,0:T(8,128)(2,1)}), bf16[32,24,128]{2,1,0:T(8,128)(2,1)S(1)}, u32[]{:S(2)}, u32[]{:S(2)}) async-start(bf16[32,24,128]{2,1,0:T(8,128)(2,1)} %bitcast.30), calls=%async_computation.3 | async-start | bytes 393216 | tf_op jit(solution)/shard_map/all_to_all | solution.py:105
  97.3 6.8 %copy-start.8 = (bf16[4,64,128]{2,1,0:T(8,128)(2,1)S(1)}, bf16[4,64,128]{2,1,0:T(8,128)(2,1)}, u32[]{:S(2)}) copy-start(bf16[4,64,128]{2,1,0:T(8,128)(2,1)} %copy-done.7) | copy-start | bytes 196612
  100.5 24.1 %all-to-all-start.4 = ((bf16[32,88,128]{2,1,0:T(8,128)(2,1)}), bf16[32,88,128]{2,1,0:T(8,128)(2,1)S(1)}, u32[]{:S(2)}, u32[]{:S(2)}) async-start(bf16[32,88,128]{2,1,0:T(8,128)(2,1)} %shard_map.151), calls=%async_computation.4 | async-start | bytes 1441792 | tf_op jit(solution)/shard_map/all_to_all | solution.py:105

commit v5 on v4

--- a/solution.py
+++ b/solution.py
@@ -164,11 +164,11 @@
     chunks = recv_ref.shape[0]
     groups, depth = act_ref.shape
     for d in range(chunks):
-        tags_held[d] = recv_ref[d, halves * chan :, :]
+        tags_held[d] = recv_ref[d][halves * chan :, :].astype(F32)
     kept = started(tags_held, tags_ref, sems.at[0])
     for d in range(chunks):
         block = recv_ref[d]
-        tags = block[halves * chan :, :].astype(F32)
+        tags = tags_held[d]
         for h in range(halves):
             feats = block[h * chan : (h + 1) * chan, :]
             lanes = slice((d * halves + h) * LANES, (d * halves + h + 1) * LANES)
@@ -626,8 +626,8 @@
 
 def hidden_grad_kernel(
     in_chan, sides_ref, stats_ref, sums_ref, params_ref, hidden, hidden_ring_ref, pre,
-    pre_ring_ref, acts_ref, stack_ref, raw_ref, front, rear, swap_ref, small_ref, out_ref,
-    stats, hidden_ring, pre_ring, acts, stack, raw, acc, sems,
+    pre_ring_ref, acts_ref, stack_ref, raw_ref, front, rear, swap_out_ref, small_ref, out_ref,
+    stats, hidden_ring, pre_ring, acts, stack, raw, acc, swap_ref, sems,
 ):
     chan = hidden.shape[0] // 16
     place = sides_ref[2]
@@ -674,6 +674,7 @@
             tiles.append(((act * weight) * grad).astype(BF16))
             held[to, :] = tiles[-1]
         swap_ref[to, :] = jnp.where(place == 0, tiles[1], tiles[0])
+    kept = started(swap_ref, swap_out_ref, sems.at[24])
     got_stack.wait()
     got_raw.wait()
     rows = stack.shape[0] // 6
@@ -715,6 +716,7 @@
     left = out_ref.shape[0] - tail - 4 * chan
     if left:
         out_ref[tail + 4 * chan :, :] = jnp.zeros((left, LANES), out_ref.dtype)
+    kept.wait()
 
 
 def point_grad_kernel(
@@ -754,7 +756,7 @@
             ).astype(BF16)
 
     def from_cells(d):
-        tags = tags_held[d].astype(F32)
+        tags = tags_held[d]
         hot = jnp.concatenate(
             [hot_rows(tags[halves + h : halves + h + 1, :], 0, depth) for h in range(halves)], axis=1
         )
@@ -891,12 +893,12 @@
 
     *mine, tags = local_call(
         functools.partial(scatter_kernel, halves, in_chan, size_y),
-        [((rows_x, size_z), BF16)] * 2 + [((chunks, 8, LANES), BF16)],
+        [((rows_x, size_z), BF16)] * 2 + [((chunks, 8, LANES), F32)],
         sides, recv, acts,
         scratch=[
             ((groups * in_chan, chunks * halves * LANES), BF16),
             ((size_z, chunks * halves * LANES), BF16),
-            ((chunks, 8, LANES), BF16),
+            ((chunks, 8, LANES), F32),
         ],
         smem=(0,), hbm_outs=(2,), copies=1, moved=2e7,
     )
@@ -1005,8 +1007,9 @@
             ((rows_64 // 8 * 6 * 3, size_z), BF16),
             ((4 * out_chan, LANES), F32),
             ((3, 24 * in_chan, 4 * out_chan), F32),
+            ((rows_6, LANES), BF16),
         ],
-        smem=(0,), hbm=(1, 5, 7, 8, 9, 10), copies=24, moved=2e7,
+        smem=(0,), hbm=(1, 5, 7, 8, 9, 10), hbm_outs=(2,), copies=25, moved=2e7,
     )
     grad_before, grad_after = z_exchange(grad_low, grad_high, grad_swap)
     parts = everyone(parts.reshape(devices, piece, LANES))
@@ -1018,7 +1021,7 @@
         scratch=[
             (back_shape, BF16),
             ((groups, size_z), F32),
-            ((chunks, 8, LANES), BF16),
+            ((chunks, 8, LANES), F32),
             ((3 * rows_6, size_z), BF16),
             ((groups * in_chan, size_z), BF16),
         ],

time: 126 us -> 126 us (level)
  no operation moved by 1% of the time
where the time goes in v5:
time: 126 us; the launch traced here: 125 us
  waiting for transfers between devices  45.3 us (36%)
  Pallas kernels  42.7 us (34%)
  starting transfers between devices  32.2 us (26%)
  local copies, waits for them, and re-layouts  3.65 us (3%)
    pallas_call x17, Pallas kernels, local_call(): pl.pallas_call(kernel, out_shape=[pltpu.HBM(shape, kind) if i in hbm_outs...  42.7 us
    all_to_all x5, waiting for transfers between devices, everyone(): return lax.all_to_all(block, AXES, split_axis=0, concat_axis=0, tiled=True)  33.3 us
    all_to_all x5, starting transfers between devices, everyone(): return lax.all_to_all(block, AXES, split_axis=0, concat_axis=0, tiled=True)  25.1 us
    ppermute x8, waiting for transfers between devices, swaps(): got.append(lax.ppermute(block, axis, pairs + [(j, i) for i, j in pairs]))  10.8 us
    ppermute x8, starting transfers between devices, swaps(): got.append(lax.ppermute(block, axis, pairs + [(j, i) for i, j in pairs]))  6.58 us
  transfers between devices with their start and end apart: 15, of which 10 were waited for; matrix products, arithmetic and copies ran while one was open for 2% of the time, Pallas kernels for 18%

profile of v5, /device:TPU:0, one launch (start us, length us, event | category | flops | bytes accessed | tf_op | source)
XLA Modules:
  0.0 125.1 jit_solution(8313282552827145163)
XLA Ops:
  0.7 2.1 %shard_map.136 = bf16[32,72,128]{2,1,0:T(8,128)(2,1)} custom-call(s32[1,32]{1,0:T(1,128)} %counts_ref.1, bf16[32,8192]{1,0:T(8,128)(2,1)} %feats_ref.1, s32[64,128]{1,0:T(8,128)} %bitcast.39), custom_call_target="tpu_custom_call" | custom-call | bytes 2000000 | tf_op jit(solution)/shard_map/pallas_call | solution.py:37
  2.7 7.3 %all-to-all-start = ((bf16[32,72,128]{2,1,0:T(8,128)(2,1)}), bf16[32,72,128]{2,1,0:T(8,128)(2,1)S(1)}, u32[]{:S(2)}, u32[]{:S(2)}) async-start(bf16[32,72,128]{2,1,0:T(8,128)(2,1)} %shard_map.136), calls=%async_computation | async-start | bytes 1179648 | tf_op jit(solution)/shard_map/all_to_all | solution.py:105
  10.2 0.7 shard_map.137
  11.0 1.8 %collective-permute-start = (bf16[144,128]{1,0:T(8,128)(2,1)S(1)}, bf16[144,128]{1,0:T(8,128)(2,1)S(1)}, u32[]{:S(2)}, u32[]{:S(2)}) collective-permute-start(bf16[144,128]{1,0:T(8,128)(2,1)S(1)} %get-tuple-element.75), channel_id=1, source_target_pairs={{0,8},{16,24},{8,0},{24,16},{1,9},{17,25},{9,1},{25,17},{2,10},{18... | collective-permute-start | bytes 110600 | tf_op jit(solution)/shard_map/ppermute | solution.py:86
  15.0 1.5 %collective-permute-done.xf_ref = bf16[144,128]{1,0:T(8,128)(2,1)S(1)} collective-permute-done((bf16[144,128]{1,0:T(8,128)(2,1)S(1)}, bf16[144,128]{1,0:T(8,128)(2,1)S(1)}, u32[]{:S(2)}, u32[]{:S(2)}) %collective-permute-start) | collective-permute-done | bytes 36896 | tf_op jit(solution)/shard_map/ppermute | solution.py:86
  17.1 1.5 %collective-permute-start.2 = (bf16[272,128]{1,0:T(8,128)(2,1)S(1)}, bf16[272,128]{1,0:T(8,128)(2,1)S(1)}, u32[]{:S(2)}, u32[]{:S(2)}) collective-permute-start(bf16[272,128]{1,0:T(8,128)(2,1)S(1)} %get-tuple-element.77), channel_id=1, source_target_pairs={{0,2},{4,6},{2,0},{6,4},{1,3},{5,7},{3,1},{7,5},{8,10},{12,14},{10... | collective-permute-start | bytes 208904 | tf_op jit(solution)/shard_map/ppermute | solution.py:86
  19.3 3.1 %collective-permute-done.2.yf_ref = bf16[272,128]{1,0:T(8,128)(2,1)S(1)} collective-permute-done((bf16[272,128]{1,0:T(8,128)(2,1)S(1)}, bf16[272,128]{1,0:T(8,128)(2,1)S(1)}, u32[]{:S(2)}, u32[]{:S(2)}) %collective-permute-start.2) | collective-permute-done | bytes 69664 | tf_op jit(solution)/shard_map/ppermute | solution.py:86
  22.4 5.4 %all-to-all-done.recv_ref = bf16[32,72,128]{2,1,0:T(8,128)(2,1)S(1)} async-done(((bf16[32,72,128]{2,1,0:T(8,128)(2,1)}), bf16[32,72,128]{2,1,0:T(8,128)(2,1)S(1)}, u32[]{:S(2)}, u32[]{:S(2)}) %all-to-all-start) | async-done | bytes 589856 | tf_op jit(solution)/shard_map/all_to_all | solution.py:105
  27.8 3.4 %shard_map.139 = (bf16[256,256]{1,0:T(8,128)(2,1)S(1)}, bf16[256,256]{1,0:T(8,128)(2,1)S(1)}, f32[32,8,128]{2,1,0:T(8,128)}) custom-call(s32[3]{0:T(128)S(1)} %pad_add_fusion.sides_ref, bf16[32,72,128]{2,1,0:T(8,128)(2,1)S(1)} %all-to-all-done.recv_ref, f32[16,256]{1,0:T(8,128)S(1)} %convert_element_type.12.act_ref), custom_call_target="tpu_custom_call" | custom-call | bytes 20000000 | tf_op jit(solution)/shard_map/pallas_call | solution.py:37
  32.0 2.6 %shard_map.140 = (f32[40,256]{1,0:T(8,128)}, f32[1024,256]{1,0:T(8,128)S(1)}, f32[1280,256]{1,0:T(8,128)}) custom-call(s32[3]{0:T(128)S(1)} %pad_add_fusion.sides_ref, f32[16,256]{1,0:T(8,128)S(1)} %convert_element_type.12.act_ref, bf16[256,128]{1,0:T(8,128)(2,1)S(1)} %get-tuple-element.83.grad_ref.rest_1_, ...), custom_call_target="tpu_custom_call" | custom-call | bytes 4000000 | tf_op jit(solution)/shard_map/pallas_call | solution.py:37
  34.6 2.0 %collective-permute-done.4.gf_ref = bf16[256,256]{1,0:T(8,128)(2,1)S(1)} collective-permute-done((bf16[256,256]{1,0:T(8,128)(2,1)S(1)}, bf16[256,256]{1,0:T(8,128)(2,1)S(1)}, u32[]{:S(2)}, u32[]{:S(2)}) %collective-permute-start.4) | collective-permute-done | bytes 131104 | tf_op jit(solution)/shard_map/ppermute | solution.py:86
  38.4 1.9 %shard_map.142 = (bf16[384,2304]{1,0:T(8,128)(2,1)}, bf16[128,3456]{1,0:T(8,128)(2,1)}, bf16[256,2304]{1,0:T(8,128)(2,1)S(1)}) custom-call(bf16[64,2304]{1,0:T(8,128)(2,1)S(1)} %copy.29.front_ref, bf16[32,3456]{1,0:T(8,128)(2,1)S(1)} %bitcast.28), custom_call_target="tpu_custom_call" | custom-call | bytes 4000000 | tf_op jit(solution)/shard_map/pallas_call | solution.py:37
  40.3 4.3 %collective-permute-done.6.yf_ref = bf16[512,256]{1,0:T(8,128)(2,1)S(1)} collective-permute-done((bf16[512,256]{1,0:T(8,128)(2,1)S(1)}, bf16[512,256]{1,0:T(8,128)(2,1)S(1)}, u32[]{:S(2)}, u32[]{:S(2)}) %collective-permute-start.6) | collective-permute-done | bytes 262176 | tf_op jit(solution)/shard_map/ppermute | solution.py:86
  44.6 0.8 shard_map.143
  45.4 0.8 shard_map.144.stack_in_ref
  46.2 1.1 collective-permute-done.8.before_ref.after_ref
  47.3 4.0 %shard_map.145 = (f32[1024,256]{1,0:T(8,128)S(1)}, bf16[6144,256]{1,0:T(8,128)(2,1)}, f32[32,8,128]{2,1,0:T(8,128)}, bf16[6144,256]{1,0:T(8,128)(2,1)S(1)}) custom-call(s32[3]{0:T(128)S(1)} %pad_add_fusion.sides_ref, bf16[6144,256]{1,0:T(8,128)(2,1)S(1)} %shard_map.144.stack_in_ref, ...), custom_call_target="tpu_custom_call", output_to_operand_aliasing={{3}: (1, {})} | custom-call | bytes 10000000 | tf_op jit(solution)/shard_map/pallas_call | solution.py:37
  51.3 8.7 %all-to-all-start.1 = ((f32[32,8,128]{2,1,0:T(8,128)}), f32[32,8,128]{2,1,0:T(8,128)S(1)}, u32[]{:S(2)}, u32[]{:S(2)}) async-start(f32[32,8,128]{2,1,0:T(8,128)} %get-tuple-element.111), calls=%async_computation.1 | async-start | bytes 262144 | tf_op jit(solution)/shard_map/all_to_all | solution.py:105
  60.1 5.3 %shard_map.146.hidden.hidden_ring_ref = f32[1280,256]{1,0:T(8,128)} custom-call(bf16[384,2304]{1,0:T(8,128)(2,1)} %get-tuple-element.112.bands_ref, f32[40,256]{1,0:T(8,128)} %get-tuple-element.110.acts_ref, bf16[6144,256]{1,0:T(8,128)(2,1)} %get-tuple-element.113.stack_ref), custom_call_target="tpu_custom_call" | custom-call | bytes 10000000 | tf_op jit(solution)/shard_map/pallas_call | solution.py:37
  65.3 2.7 %all-to-all-done.1.stats_ref = f32[32,8,128]{2,1,0:T(8,128)S(1)} async-done(((f32[32,8,128]{2,1,0:T(8,128)}), f32[32,8,128]{2,1,0:T(8,128)S(1)}, u32[]{:S(2)}, u32[]{:S(2)}) %all-to-all-start.1) | async-done | bytes 131104 | tf_op jit(solution)/shard_map/all_to_all | solution.py:105
  68.1 2.9 %shard_map.147 = (f32[1024,256]{1,0:T(8,128)S(1)}, bf16[1024,256]{1,0:T(8,128)(2,1)}, f32[32,8,128]{2,1,0:T(8,128)}) custom-call(f32[32,8,128]{2,1,0:T(8,128)S(1)} %all-to-all-done.1.stats_ref, f32[8,128]{1,0:T(8,128)S(1)} %select_maximum_fusion.params_ref, f32[1024,256]{1,0:T(8,128)S(1)} %get-tuple-element.118.hidden, ...), custom_call_target="tpu_custom_call" | custom-call | bytes 5000000 | tf_op jit(solution)/shard_map/pallas_call | solution.py:37
  71.0 3.0 %all-to-all-start.2 = ((f32[32,8,128]{2,1,0:T(8,128)}), f32[32,8,128]{2,1,0:T(8,128)S(1)}, u32[]{:S(2)}, u32[]{:S(2)}) async-start(f32[32,8,128]{2,1,0:T(8,128)} %get-tuple-element.123), calls=%async_computation.2 | async-start | bytes 262144 | tf_op jit(solution)/shard_map/all_to_all | solution.py:105
  74.0 4.0 %shard_map.148 = (f32[1280,256]{1,0:T(8,128)}, bf16[4,64,128]{2,1,0:T(8,128)(2,1)S(1)}, f32[256,128]{1,0:T(8,128)}) custom-call(f32[32,8,128]{2,1,0:T(8,128)} %copy-done, f32[8,128]{1,0:T(8,128)S(1)} %select_maximum_fusion.params_ref, f32[1280,256]{1,0:T(8,128)} %shard_map.146.hidden.hidden_ring_ref, f32[1280,256]{1,0:T(8,128)} %get-tuple-element.117.fine, ...), custom_call_target="tpu_custom_call" | custom-call | bytes 5000000 | tf_op jit(solution)/shard_map/pallas_call | solution.py:37
  78.6 3.5 %all-to-all-done.2.sums_ref = f32[32,8,128]{2,1,0:T(8,128)S(1)} async-done(((f32[32,8,128]{2,1,0:T(8,128)}), f32[32,8,128]{2,1,0:T(8,128)S(1)}, u32[]{:S(2)}, u32[]{:S(2)}) %all-to-all-start.2) | async-done | bytes 131104 | tf_op jit(solution)/shard_map/all_to_all | solution.py:105
  82.1 4.8 %shard_map.149 = (bf16[2304,128]{1,0:T(8,128)(2,1)S(1)}, bf16[2304,128]{1,0:T(8,128)(2,1)S(1)}, bf16[2304,128]{1,0:T(8,128)(2,1)}, f32[8,128]{1,0:T(8,128)S(1)}, bf16[768,128]{1,0:T(8,128)(2,1)S(1)}) custom-call(s32[3]{0:T(128)S(1)} %pad_add_fusion.sides_ref, f32[32,8,128]{2,1,0:T(8,128)} %copy-done, f32[32,8,128]{2,1,0:T(8,128)S(1)} %all-to-all-done.2.sums_ref, ...), custom_call_target="tpu_custom_call" | custom-call | bytes 20000000 | tf_op jit(solution)/shard_map/pallas_call | solution.py:37
  87.6 2.6 %all-to-all-start.3 = ((bf16[32,24,128]{2,1,0:T(8,128)(2,1)}), bf16[32,24,128]{2,1,0:T(8,128)(2,1)S(1)}, u32[]{:S(2)}, u32[]{:S(2)}) async-start(bf16[32,24,128]{2,1,0:T(8,128)(2,1)} %bitcast.30), calls=%async_computation.3 | async-start | bytes 393216 | tf_op jit(solution)/shard_map/all_to_all | solution.py:105
  90.2 6.4 %shard_map.150.points_ref = bf16[32,64,128]{2,1,0:T(8,128)(2,1)S(1)} custom-call(s32[3]{0:T(128)S(1)} %pad_add_fusion.sides_ref, bf16[2304,128]{1,0:T(8,128)(2,1)S(1)} %get-tuple-element.131.front, bf16[2304,128]{1,0:T(8,128)(2,1)S(1)} %get-tuple-element.132.rear, bf16[2304,128]{1,0:T(8,128)(2,1)S(1)} %collective-permute-done.9.before_ref.after_ref, ...), custom_call_target="tpu_custom_call" | custom-call | bytes 20000000 | tf_op jit(solution)/shard_map/pallas_call | solution.py:37
  96.7 2.3 %all-to-all-done.3.parts_ref = bf16[32,24,128]{2,1,0:T(8,128)(2,1)S(1)} async-done(((bf16[32,24,128]{2,1,0:T(8,128)(2,1)}), bf16[32,24,128]{2,1,0:T(8,128)(2,1)S(1)}, u32[]{:S(2)}, u32[]{:S(2)}) %all-to-all-start.3) | async-done | bytes 196640 | tf_op jit(solution)/shard_map/all_to_all | solution.py:105
  99.0 0.9 shard_map.151
  99.9 3.5 %all-to-all-start.4 = ((bf16[32,88,128]{2,1,0:T(8,128)(2,1)}), bf16[32,88,128]{2,1,0:T(8,128)(2,1)S(1)}, u32[]{:S(2)}, u32[]{:S(2)}) async-start(bf16[32,88,128]{2,1,0:T(8,128)(2,1)} %shard_map.151), calls=%async_computation.4 | async-start | bytes 1441792 | tf_op jit(solution)/shard_map/all_to_all | solution.py:105
  104.7 19.3 %all-to-all-done.4.got_ref = bf16[32,88,128]{2,1,0:T(8,128)(2,1)S(1)} async-done(((bf16[32,88,128]{2,1,0:T(8,128)(2,1)}), bf16[32,88,128]{2,1,0:T(8,128)(2,1)S(1)}, u32[]{:S(2)}, u32[]{:S(2)}) %all-to-all-start.4) | async-done | bytes 720928 | tf_op jit(solution)/shard_map/all_to_all | solution.py:105
  124.0 1.0 shard_map.152
  (62 shorter events, 8.6 us)
Async XLA Ops:
  0.6 9.4 %copy-start.11 = (s32[4,4,256]{2,1,0:T(4,128)S(1)}, s32[4,4,256]{2,1,0:T(4,128)}, u32[]{:S(2)}) copy-start(s32[4,4,256]{2,1,0:T(4,128)} %param.12) | copy-start | bytes 49156
  0.6 9.5 %copy-start.10 = (bf16[64,2,2,128]{3,2,1,0:T(2,128)(2,1)S(1)}, bf16[64,2,2,128]{3,2,1,0:T(2,128)(2,1)}, u32[]{:S(2)}) copy-start(bf16[64,2,2,128]{3,2,1,0:T(2,128)(2,1)} %param.17) | copy-start | bytes 196612
  0.7 12.8 %copy-start.9 = (bf16[64,864]{1,0:T(8,128)(2,1)S(1)}, bf16[64,864]{1,0:T(8,128)(2,1)}, u32[]{:S(2)}) copy-start(bf16[64,864]{1,0:T(8,128)(2,1)} %param.13) | copy-start | bytes 331780
  0.7 13.0 %copy-start.4 = (bf16[64,512]{1,0:T(8,128)(2,1)S(1)}, bf16[64,512]{1,0:T(8,128)(2,1)}, u32[]{:S(2)}) copy-start(bf16[64,512]{1,0:T(8,128)(2,1)} %rest_3_.1) | copy-start | bytes 196612
  2.7 25.1 %all-to-all-start = ((bf16[32,72,128]{2,1,0:T(8,128)(2,1)}), bf16[32,72,128]{2,1,0:T(8,128)(2,1)S(1)}, u32[]{:S(2)}, u32[]{:S(2)}) async-start(bf16[32,72,128]{2,1,0:T(8,128)(2,1)} %shard_map.136), calls=%async_computation | async-start | bytes 1179648 | tf_op jit(solution)/shard_map/all_to_all | solution.py:105
  10.1 21.9 %copy-start.2 = (f32[16,256]{1,0:T(8,128)}, f32[16,256]{1,0:T(8,128)S(1)}, u32[]{:S(2)}) copy-start(f32[16,256]{1,0:T(8,128)S(1)} %convert_element_type.12.act_ref) | copy-start | bytes 49156
  10.9 21.1 %copy-start.3 = (bf16[256,128]{1,0:T(8,128)(2,1)}, bf16[256,128]{1,0:T(8,128)(2,1)S(1)}, u32[]{:S(2)}) copy-start(bf16[256,128]{1,0:T(8,128)(2,1)S(1)} %get-tuple-element.83.grad_ref.rest_1_) | copy-start | bytes 196612
  11.0 5.5 %collective-permute-start = (bf16[144,128]{1,0:T(8,128)(2,1)S(1)}, bf16[144,128]{1,0:T(8,128)(2,1)S(1)}, u32[]{:S(2)}, u32[]{:S(2)}) collective-permute-start(bf16[144,128]{1,0:T(8,128)(2,1)S(1)} %get-tuple-element.75), channel_id=1, source_target_pairs={{0,8},{16,24},{8,0},{24,16},{1,9},{17,25},{9,1},{25,17},{2,10},{18... | collective-permute-start | bytes 110600 | tf_op jit(solution)/shard_map/ppermute | solution.py:86
  12.8 3.7 %collective-permute-start.1 = (bf16[144,128]{1,0:T(8,128)(2,1)S(1)}, bf16[144,128]{1,0:T(8,128)(2,1)S(1)}, u32[]{:S(2)}, u32[]{:S(2)}) collective-permute-start(bf16[144,128]{1,0:T(8,128)(2,1)S(1)} %get-tuple-element.76), channel_id=1, source_target_pairs={{8,16},{16,8},{9,17},{17,9},{10,18},{18,10},{11,19},{19,11},{12,20... | collective-permute-start | bytes 110600 | tf_op jit(solution)/shard_map/ppermute | solution.py:86
  14.5 4.8 %copy-start.12 = (f32[64]{0:T(128)S(1)}, f32[64]{0:T(128)}, u32[]{:S(2)}) copy-start(f32[64]{0:T(128)} %param.16) | copy-start | bytes 772
  14.5 4.8 %copy-start.13 = (f32[64]{0:T(128)S(1)}, f32[64]{0:T(128)}, u32[]{:S(2)}) copy-start(f32[64]{0:T(128)} %param.15) | copy-start | bytes 772
  17.1 5.3 %collective-permute-start.2 = (bf16[272,128]{1,0:T(8,128)(2,1)S(1)}, bf16[272,128]{1,0:T(8,128)(2,1)S(1)}, u32[]{:S(2)}, u32[]{:S(2)}) collective-permute-start(bf16[272,128]{1,0:T(8,128)(2,1)S(1)} %get-tuple-element.77), channel_id=1, source_target_pairs={{0,2},{4,6},{2,0},{6,4},{1,3},{5,7},{3,1},{7,5},{8,10},{12,14},{10... | collective-permute-start | bytes 208904 | tf_op jit(solution)/shard_map/ppermute | solution.py:86
  18.6 3.8 %collective-permute-start.3 = (bf16[272,128]{1,0:T(8,128)(2,1)S(1)}, bf16[272,128]{1,0:T(8,128)(2,1)S(1)}, u32[]{:S(2)}, u32[]{:S(2)}) collective-permute-start(bf16[272,128]{1,0:T(8,128)(2,1)S(1)} %get-tuple-element.78), channel_id=1, source_target_pairs={{2,4},{4,2},{3,5},{5,3},{10,12},{12,10},{11,13},{13,11},{18,20},{2... | collective-permute-start | bytes 208904 | tf_op jit(solution)/shard_map/ppermute | solution.py:86
  31.2 5.4 %collective-permute-start.4 = (bf16[256,256]{1,0:T(8,128)(2,1)S(1)}, bf16[256,256]{1,0:T(8,128)(2,1)S(1)}, u32[]{:S(2)}, u32[]{:S(2)}) collective-permute-start(bf16[256,256]{1,0:T(8,128)(2,1)S(1)} %get-tuple-element.81.first_ref), channel_id=1, source_target_pairs={{0,8},{16,24},{8,0},{24,16},{1,9},{17,25},{9,1},{25,17},{2,10},{18... | collective-permute-start | bytes 393224 | tf_op jit(solution)/shard_map/ppermute | solution.py:86
  31.3 5.3 %collective-permute-start.5 = (bf16[256,256]{1,0:T(8,128)(2,1)S(1)}, bf16[256,256]{1,0:T(8,128)(2,1)S(1)}, u32[]{:S(2)}, u32[]{:S(2)}) collective-permute-start(bf16[256,256]{1,0:T(8,128)(2,1)S(1)} %get-tuple-element.82.second_ref), channel_id=1, source_target_pairs={{8,16},{16,8},{9,17},{17,9},{10,18},{18,10},{11,19},{19,11},{12,20... | collective-permute-start | bytes 393224 | tf_op jit(solution)/shard_map/ppermute | solution.py:86
  37.2 7.3 %collective-permute-start.6 = (bf16[512,256]{1,0:T(8,128)(2,1)S(1)}, bf16[512,256]{1,0:T(8,128)(2,1)S(1)}, u32[]{:S(2)}, u32[]{:S(2)}) collective-permute-start(bf16[512,256]{1,0:T(8,128)(2,1)S(1)} %get-tuple-element.94), channel_id=1, source_target_pairs={{0,2},{4,6},{2,0},{6,4},{1,3},{5,7},{3,1},{7,5},{8,10},{12,14},{10... | collective-permute-start | bytes 786440 | tf_op jit(solution)/shard_map/ppermute | solution.py:86
  37.7 6.8 %collective-permute-start.7 = (bf16[512,256]{1,0:T(8,128)(2,1)S(1)}, bf16[512,256]{1,0:T(8,128)(2,1)S(1)}, u32[]{:S(2)}, u32[]{:S(2)}) collective-permute-start(bf16[512,256]{1,0:T(8,128)(2,1)S(1)} %get-tuple-element.95), channel_id=1, source_target_pairs={{2,4},{4,2},{3,5},{5,3},{10,12},{12,10},{11,13},{13,11},{18,20},{2... | collective-permute-start | bytes 786440 | tf_op jit(solution)/shard_map/ppermute | solution.py:86
  45.3 2.0 %collective-permute-start.8 = (bf16[2048,128]{1,0:T(8,128)(2,1)S(1)}, bf16[2048,128]{1,0:T(8,128)(2,1)S(1)}, u32[]{:S(2)}, u32[]{:S(2)}) collective-permute-start(bf16[2048,128]{1,0:T(8,128)(2,1)S(1)} %get-tuple-element.103), channel_id=1, source_target_pairs={{0,1},{1,0},{2,3},{3,2},{4,5},{5,4},{6,7},{7,6},{8,9},{9,8},{10,11... | collective-permute-start | bytes 1572872 | tf_op jit(solution)/shard_map/ppermute | solution.py:100
  45.4 1.9 %copy-start.1 = (f32[40,256]{1,0:T(8,128)S(1)}, f32[40,256]{1,0:T(8,128)}, u32[]{:S(2)}) copy-start(f32[40,256]{1,0:T(8,128)} %get-tuple-element.110.acts_ref) | copy-start | bytes 122884
  51.3 16.7 %all-to-all-start.1 = ((f32[32,8,128]{2,1,0:T(8,128)}), f32[32,8,128]{2,1,0:T(8,128)S(1)}, u32[]{:S(2)}, u32[]{:S(2)}) async-start(f32[32,8,128]{2,1,0:T(8,128)} %get-tuple-element.111), calls=%async_computation.1 | async-start | bytes 262144 | tf_op jit(solution)/shard_map/all_to_all | solution.py:105
  65.3 8.6 %copy-start.5 = (bf16[64,512]{1,0:T(8,128)(2,1)S(1)}, bf16[64,512]{1,0:T(8,128)(2,1)}, u32[]{:S(2)}) copy-start(bf16[64,512]{1,0:T(8,128)(2,1)} %rest_3_.1) | copy-start | bytes 196612
  68.1 5.9 %copy-start = (f32[32,8,128]{2,1,0:T(8,128)}, f32[32,8,128]{2,1,0:T(8,128)S(1)}, u32[]{:S(2)}) copy-start(f32[32,8,128]{2,1,0:T(8,128)S(1)} %all-to-all-done.1.stats_ref) | copy-start | bytes 393220
  71.0 11.2 %all-to-all-start.2 = ((f32[32,8,128]{2,1,0:T(8,128)}), f32[32,8,128]{2,1,0:T(8,128)S(1)}, u32[]{:S(2)}, u32[]{:S(2)}) async-start(f32[32,8,128]{2,1,0:T(8,128)} %get-tuple-element.123), calls=%async_computation.2 | async-start | bytes 262144 | tf_op jit(solution)/shard_map/all_to_all | solution.py:105
  78.0 0.6 copy-start.7
  87.0 0.7 copy-start.6
  87.0 3.3 %collective-permute-start.9 = (bf16[2304,128]{1,0:T(8,128)(2,1)}, bf16[2304,128]{1,0:T(8,128)(2,1)S(1)}, u32[]{:S(2)}, u32[]{:S(2)}) collective-permute-start(bf16[2304,128]{1,0:T(8,128)(2,1)} %get-tuple-element.133), channel_id=1, source_target_pairs={{0,1},{1,0},{2,3},{3,2},{4,5},{5,4},{6,7},{7,6},{8,9},{9,8},{10,11... | collective-permute-start | bytes 1769480 | tf_op jit(solution)/shard_map/ppermute | solution.py:100
  87.6 11.3 %all-to-all-start.3 = ((bf16[32,24,128]{2,1,0:T(8,128)(2,1)}), bf16[32,24,128]{2,1,0:T(8,128)(2,1)S(1)}, u32[]{:S(2)}, u32[]{:S(2)}) async-start(bf16[32,24,128]{2,1,0:T(8,128)(2,1)} %bitcast.30), calls=%async_computation.3 | async-start | bytes 393216 | tf_op jit(solution)/shard_map/all_to_all | solution.py:105
  96.7 6.8 %copy-start.8 = (bf16[4,64,128]{2,1,0:T(8,128)(2,1)S(1)}, bf16[4,64,128]{2,1,0:T(8,128)(2,1)}, u32[]{:S(2)}) copy-start(bf16[4,64,128]{2,1,0:T(8,128)(2,1)} %copy-done.7) | copy-start | bytes 196612
  99.9 24.1 %all-to-all-start.4 = ((bf16[32,88,128]{2,1,0:T(8,128)(2,1)}), bf16[32,88,128]{2,1,0:T(8,128)(2,1)S(1)}, u32[]{:S(2)}, u32[]{:S(2)}) async-start(bf16[32,88,128]{2,1,0:T(8,128)(2,1)} %shard_map.151), calls=%async_computation.4 | async-start | bytes 1441792 | tf_op jit(solution)/shard_map/all_to_all | solution.py:105

commit v6 on v5

--- a/solution.py
+++ b/solution.py
@@ -679,18 +679,13 @@
     got_raw.wait()
     rows = stack.shape[0] // 6
     band = rows // 3
-    for p in range(4):
-        own = slice(((p + 1) * 6 + 1) * chan, ((p + 1) * 6 + 5) * chan)
-        grads = jnp.concatenate([front[own, :], rear[own, :]], axis=1)
-        for dx in range(3):
-            first = (p + dx) * rows
-            part = lax.dot_general(
-                stack[first : first + rows, :], grads, NT, preferred_element_type=F32
-            )
-            if p == 0:
-                acc[dx] = part
-            else:
-                acc[dx] += part
+    owned = [slice(((p + 1) * 6 + 1) * chan, ((p + 1) * 6 + 5) * chan) for p in range(4)]
+    grads = jnp.concatenate([held[own, :] for own in owned for held in (front, rear)], axis=1)
+    for dx in range(3):
+        taps = jnp.concatenate(
+            [stack[(p + dx) * rows : (p + dx + 1) * rows, :] for p in range(4)], axis=1
+        )
+        acc[dx] = lax.dot_general(taps, grads, NT, preferred_element_type=F32)
     low = lax.broadcasted_iota(jnp.int32, (in_chan, LANES), 1) < chan
     for dx in range(3):
         for dy in range(3):

time: 126 us -> 126 us (level)
  no operation moved by 1% of the time
where the time goes in v6:
time: 126 us; the launch traced here: 125 us
  waiting for transfers between devices  45.3 us (36%)
  Pallas kernels  42.7 us (34%)
  starting transfers between devices  32.2 us (26%)
  local copies, waits for them, and re-layouts  3.65 us (3%)
    pallas_call x17, Pallas kernels, local_call(): pl.pallas_call(kernel, out_shape=[pltpu.HBM(shape, kind) if i in hbm_outs...  42.7 us
    all_to_all x5, waiting for transfers between devices, everyone(): return lax.all_to_all(block, AXES, split_axis=0, concat_axis=0, tiled=True)  33.3 us
    all_to_all x5, starting transfers between devices, everyone(): return lax.all_to_all(block, AXES, split_axis=0, concat_axis=0, tiled=True)  25.1 us
    ppermute x8, waiting for transfers between devices, swaps(): got.append(lax.ppermute(block, axis, pairs + [(j, i) for i, j in pairs]))  10.8 us
    ppermute x8, starting transfers between devices, swaps(): got.append(lax.ppermute(block, axis, pairs + [(j, i) for i, j in pairs]))  6.58 us
  transfers between devices with their start and end apart: 15, of which 10 were waited for; matrix products, arithmetic and copies ran while one was open for 2% of the time, Pallas kernels for 18%

profile of v6, /device:TPU:0, one launch (start us, length us, event | category | flops | bytes accessed | tf_op | source)
XLA Modules:
  0.0 125.1 jit_solution(11488394793492055138)
XLA Ops:
  0.7 2.1 %shard_map.136 = bf16[32,72,128]{2,1,0:T(8,128)(2,1)} custom-call(s32[1,32]{1,0:T(1,128)} %counts_ref.1, bf16[32,8192]{1,0:T(8,128)(2,1)} %feats_ref.1, s32[64,128]{1,0:T(8,128)} %bitcast.39), custom_call_target="tpu_custom_call" | custom-call | bytes 2000000 | tf_op jit(solution)/shard_map/pallas_call | solution.py:37
  2.7 7.3 %all-to-all-start = ((bf16[32,72,128]{2,1,0:T(8,128)(2,1)}), bf16[32,72,128]{2,1,0:T(8,128)(2,1)S(1)}, u32[]{:S(2)}, u32[]{:S(2)}) async-start(bf16[32,72,128]{2,1,0:T(8,128)(2,1)} %shard_map.136), calls=%async_computation | async-start | bytes 1179648 | tf_op jit(solution)/shard_map/all_to_all | solution.py:105
  10.2 0.7 shard_map.137
  11.0 1.8 %collective-permute-start = (bf16[144,128]{1,0:T(8,128)(2,1)S(1)}, bf16[144,128]{1,0:T(8,128)(2,1)S(1)}, u32[]{:S(2)}, u32[]{:S(2)}) collective-permute-start(bf16[144,128]{1,0:T(8,128)(2,1)S(1)} %get-tuple-element.75), channel_id=1, source_target_pairs={{0,8},{16,24},{8,0},{24,16},{1,9},{17,25},{9,1},{25,17},{2,10},{18... | collective-permute-start | bytes 110600 | tf_op jit(solution)/shard_map/ppermute | solution.py:86
  15.0 1.5 %collective-permute-done.xf_ref = bf16[144,128]{1,0:T(8,128)(2,1)S(1)} collective-permute-done((bf16[144,128]{1,0:T(8,128)(2,1)S(1)}, bf16[144,128]{1,0:T(8,128)(2,1)S(1)}, u32[]{:S(2)}, u32[]{:S(2)}) %collective-permute-start) | collective-permute-done | bytes 36896 | tf_op jit(solution)/shard_map/ppermute | solution.py:86
  17.1 1.5 %collective-permute-start.2 = (bf16[272,128]{1,0:T(8,128)(2,1)S(1)}, bf16[272,128]{1,0:T(8,128)(2,1)S(1)}, u32[]{:S(2)}, u32[]{:S(2)}) collective-permute-start(bf16[272,128]{1,0:T(8,128)(2,1)S(1)} %get-tuple-element.77), channel_id=1, source_target_pairs={{0,2},{4,6},{2,0},{6,4},{1,3},{5,7},{3,1},{7,5},{8,10},{12,14},{10... | collective-permute-start | bytes 208904 | tf_op jit(solution)/shard_map/ppermute | solution.py:86
  19.3 3.1 %collective-permute-done.2.yf_ref = bf16[272,128]{1,0:T(8,128)(2,1)S(1)} collective-permute-done((bf16[272,128]{1,0:T(8,128)(2,1)S(1)}, bf16[272,128]{1,0:T(8,128)(2,1)S(1)}, u32[]{:S(2)}, u32[]{:S(2)}) %collective-permute-start.2) | collective-permute-done | bytes 69664 | tf_op jit(solution)/shard_map/ppermute | solution.py:86
  22.4 5.4 %all-to-all-done.recv_ref = bf16[32,72,128]{2,1,0:T(8,128)(2,1)S(1)} async-done(((bf16[32,72,128]{2,1,0:T(8,128)(2,1)}), bf16[32,72,128]{2,1,0:T(8,128)(2,1)S(1)}, u32[]{:S(2)}, u32[]{:S(2)}) %all-to-all-start) | async-done | bytes 589856 | tf_op jit(solution)/shard_map/all_to_all | solution.py:105
  27.8 3.4 %shard_map.139 = (bf16[256,256]{1,0:T(8,128)(2,1)S(1)}, bf16[256,256]{1,0:T(8,128)(2,1)S(1)}, f32[32,8,128]{2,1,0:T(8,128)}) custom-call(s32[3]{0:T(128)S(1)} %pad_add_fusion.sides_ref, bf16[32,72,128]{2,1,0:T(8,128)(2,1)S(1)} %all-to-all-done.recv_ref, f32[16,256]{1,0:T(8,128)S(1)} %convert_element_type.12.act_ref), custom_call_target="tpu_custom_call" | custom-call | bytes 20000000 | tf_op jit(solution)/shard_map/pallas_call | solution.py:37
  32.0 2.6 %shard_map.140 = (f32[40,256]{1,0:T(8,128)}, f32[1024,256]{1,0:T(8,128)S(1)}, f32[1280,256]{1,0:T(8,128)}) custom-call(s32[3]{0:T(128)S(1)} %pad_add_fusion.sides_ref, f32[16,256]{1,0:T(8,128)S(1)} %convert_element_type.12.act_ref, bf16[256,128]{1,0:T(8,128)(2,1)S(1)} %get-tuple-element.83.grad_ref.rest_1_, ...), custom_call_target="tpu_custom_call" | custom-call | bytes 4000000 | tf_op jit(solution)/shard_map/pallas_call | solution.py:37
  34.6 2.0 %collective-permute-done.4.gf_ref = bf16[256,256]{1,0:T(8,128)(2,1)S(1)} collective-permute-done((bf16[256,256]{1,0:T(8,128)(2,1)S(1)}, bf16[256,256]{1,0:T(8,128)(2,1)S(1)}, u32[]{:S(2)}, u32[]{:S(2)}) %collective-permute-start.4) | collective-permute-done | bytes 131104 | tf_op jit(solution)/shard_map/ppermute | solution.py:86
  38.4 1.9 %shard_map.142 = (bf16[384,2304]{1,0:T(8,128)(2,1)}, bf16[128,3456]{1,0:T(8,128)(2,1)}, bf16[256,2304]{1,0:T(8,128)(2,1)S(1)}) custom-call(bf16[64,2304]{1,0:T(8,128)(2,1)S(1)} %copy.29.front_ref, bf16[32,3456]{1,0:T(8,128)(2,1)S(1)} %bitcast.28), custom_call_target="tpu_custom_call" | custom-call | bytes 4000000 | tf_op jit(solution)/shard_map/pallas_call | solution.py:37
  40.3 4.3 %collective-permute-done.6.yf_ref = bf16[512,256]{1,0:T(8,128)(2,1)S(1)} collective-permute-done((bf16[512,256]{1,0:T(8,128)(2,1)S(1)}, bf16[512,256]{1,0:T(8,128)(2,1)S(1)}, u32[]{:S(2)}, u32[]{:S(2)}) %collective-permute-start.6) | collective-permute-done | bytes 262176 | tf_op jit(solution)/shard_map/ppermute | solution.py:86
  44.6 0.8 shard_map.143
  45.4 0.8 shard_map.144.stack_in_ref
  46.2 1.1 collective-permute-done.8.before_ref.after_ref
  47.3 4.0 %shard_map.145 = (f32[1024,256]{1,0:T(8,128)S(1)}, bf16[6144,256]{1,0:T(8,128)(2,1)}, f32[32,8,128]{2,1,0:T(8,128)}, bf16[6144,256]{1,0:T(8,128)(2,1)S(1)}) custom-call(s32[3]{0:T(128)S(1)} %pad_add_fusion.sides_ref, bf16[6144,256]{1,0:T(8,128)(2,1)S(1)} %shard_map.144.stack_in_ref, ...), custom_call_target="tpu_custom_call", output_to_operand_aliasing={{3}: (1, {})} | custom-call | bytes 10000000 | tf_op jit(solution)/shard_map/pallas_call | solution.py:37
  51.3 8.7 %all-to-all-start.1 = ((f32[32,8,128]{2,1,0:T(8,128)}), f32[32,8,128]{2,1,0:T(8,128)S(1)}, u32[]{:S(2)}, u32[]{:S(2)}) async-start(f32[32,8,128]{2,1,0:T(8,128)} %get-tuple-element.111), calls=%async_computation.1 | async-start | bytes 262144 | tf_op jit(solution)/shard_map/all_to_all | solution.py:105
  60.1 5.3 %shard_map.146.hidden.hidden_ring_ref = f32[1280,256]{1,0:T(8,128)} custom-call(bf16[384,2304]{1,0:T(8,128)(2,1)} %get-tuple-element.112.bands_ref, f32[40,256]{1,0:T(8,128)} %get-tuple-element.110.acts_ref, bf16[6144,256]{1,0:T(8,128)(2,1)} %get-tuple-element.113.stack_ref), custom_call_target="tpu_custom_call" | custom-call | bytes 10000000 | tf_op jit(solution)/shard_map/pallas_call | solution.py:37
  65.3 2.7 %all-to-all-done.1.stats_ref = f32[32,8,128]{2,1,0:T(8,128)S(1)} async-done(((f32[32,8,128]{2,1,0:T(8,128)}), f32[32,8,128]{2,1,0:T(8,128)S(1)}, u32[]{:S(2)}, u32[]{:S(2)}) %all-to-all-start.1) | async-done | bytes 131104 | tf_op jit(solution)/shard_map/all_to_all | solution.py:105
  68.1 2.9 %shard_map.147 = (f32[1024,256]{1,0:T(8,128)S(1)}, bf16[1024,256]{1,0:T(8,128)(2,1)}, f32[32,8,128]{2,1,0:T(8,128)}) custom-call(f32[32,8,128]{2,1,0:T(8,128)S(1)} %all-to-all-done.1.stats_ref, f32[8,128]{1,0:T(8,128)S(1)} %select_maximum_fusion.params_ref, f32[1024,256]{1,0:T(8,128)S(1)} %get-tuple-element.118.hidden, ...), custom_call_target="tpu_custom_call" | custom-call | bytes 5000000 | tf_op jit(solution)/shard_map/pallas_call | solution.py:37
  71.0 3.0 %all-to-all-start.2 = ((f32[32,8,128]{2,1,0:T(8,128)}), f32[32,8,128]{2,1,0:T(8,128)S(1)}, u32[]{:S(2)}, u32[]{:S(2)}) async-start(f32[32,8,128]{2,1,0:T(8,128)} %get-tuple-element.123), calls=%async_computation.2 | async-start | bytes 262144 | tf_op jit(solution)/shard_map/all_to_all | solution.py:105
  74.0 4.0 %shard_map.148 = (f32[1280,256]{1,0:T(8,128)}, bf16[4,64,128]{2,1,0:T(8,128)(2,1)S(1)}, f32[256,128]{1,0:T(8,128)}) custom-call(f32[32,8,128]{2,1,0:T(8,128)} %copy-done, f32[8,128]{1,0:T(8,128)S(1)} %select_maximum_fusion.params_ref, f32[1280,256]{1,0:T(8,128)} %shard_map.146.hidden.hidden_ring_ref, f32[1280,256]{1,0:T(8,128)} %get-tuple-element.117.fine, ...), custom_call_target="tpu_custom_call" | custom-call | bytes 5000000 | tf_op jit(solution)/shard_map/pallas_call | solution.py:37
  78.6 3.5 %all-to-all-done.2.sums_ref = f32[32,8,128]{2,1,0:T(8,128)S(1)} async-done(((f32[32,8,128]{2,1,0:T(8,128)}), f32[32,8,128]{2,1,0:T(8,128)S(1)}, u32[]{:S(2)}, u32[]{:S(2)}) %all-to-all-start.2) | async-done | bytes 131104 | tf_op jit(solution)/shard_map/all_to_all | solution.py:105
  82.1 4.8 %shard_map.149 = (bf16[2304,128]{1,0:T(8,128)(2,1)S(1)}, bf16[2304,128]{1,0:T(8,128)(2,1)S(1)}, bf16[2304,128]{1,0:T(8,128)(2,1)}, f32[8,128]{1,0:T(8,128)S(1)}, bf16[768,128]{1,0:T(8,128)(2,1)S(1)}) custom-call(s32[3]{0:T(128)S(1)} %pad_add_fusion.sides_ref, f32[32,8,128]{2,1,0:T(8,128)} %copy-done, f32[32,8,128]{2,1,0:T(8,128)S(1)} %all-to-all-done.2.sums_ref, ...), custom_call_target="tpu_custom_call" | custom-call | bytes 20000000 | tf_op jit(solution)/shard_map/pallas_call | solution.py:37
  87.6 2.6 %all-to-all-start.3 = ((bf16[32,24,128]{2,1,0:T(8,128)(2,1)}), bf16[32,24,128]{2,1,0:T(8,128)(2,1)S(1)}, u32[]{:S(2)}, u32[]{:S(2)}) async-start(bf16[32,24,128]{2,1,0:T(8,128)(2,1)} %bitcast.30), calls=%async_computation.3 | async-start | bytes 393216 | tf_op jit(solution)/shard_map/all_to_all | solution.py:105
  90.2 6.4 %shard_map.150.points_ref = bf16[32,64,128]{2,1,0:T(8,128)(2,1)S(1)} custom-call(s32[3]{0:T(128)S(1)} %pad_add_fusion.sides_ref, bf16[2304,128]{1,0:T(8,128)(2,1)S(1)} %get-tuple-element.131.front, bf16[2304,128]{1,0:T(8,128)(2,1)S(1)} %get-tuple-element.132.rear, bf16[2304,128]{1,0:T(8,128)(2,1)S(1)} %collective-permute-done.9.before_ref.after_ref, ...), custom_call_target="tpu_custom_call" | custom-call | bytes 20000000 | tf_op jit(solution)/shard_map/pallas_call | solution.py:37
  96.7 2.3 %all-to-all-done.3.parts_ref = bf16[32,24,128]{2,1,0:T(8,128)(2,1)S(1)} async-done(((bf16[32,24,128]{2,1,0:T(8,128)(2,1)}), bf16[32,24,128]{2,1,0:T(8,128)(2,1)S(1)}, u32[]{:S(2)}, u32[]{:S(2)}) %all-to-all-start.3) | async-done | bytes 196640 | tf_op jit(solution)/shard_map/all_to_all | solution.py:105
  99.0 0.9 shard_map.151
  99.9 3.5 %all-to-all-start.4 = ((bf16[32,88,128]{2,1,0:T(8,128)(2,1)}), bf16[32,88,128]{2,1,0:T(8,128)(2,1)S(1)}, u32[]{:S(2)}, u32[]{:S(2)}) async-start(bf16[32,88,128]{2,1,0:T(8,128)(2,1)} %shard_map.151), calls=%async_computation.4 | async-start | bytes 1441792 | tf_op jit(solution)/shard_map/all_to_all | solution.py:105
  104.7 19.3 %all-to-all-done.4.got_ref = bf16[32,88,128]{2,1,0:T(8,128)(2,1)S(1)} async-done(((bf16[32,88,128]{2,1,0:T(8,128)(2,1)}), bf16[32,88,128]{2,1,0:T(8,128)(2,1)S(1)}, u32[]{:S(2)}, u32[]{:S(2)}) %all-to-all-start.4) | async-done | bytes 720928 | tf_op jit(solution)/shard_map/all_to_all | solution.py:105
  124.0 1.0 shard_map.152
  (62 shorter events, 8.6 us)
Async XLA Ops:
  0.6 9.4 %copy-start.11 = (s32[4,4,256]{2,1,0:T(4,128)S(1)}, s32[4,4,256]{2,1,0:T(4,128)}, u32[]{:S(2)}) copy-start(s32[4,4,256]{2,1,0:T(4,128)} %param.12) | copy-start | bytes 49156
  0.6 9.5 %copy-start.10 = (bf16[64,2,2,128]{3,2,1,0:T(2,128)(2,1)S(1)}, bf16[64,2,2,128]{3,2,1,0:T(2,128)(2,1)}, u32[]{:S(2)}) copy-start(bf16[64,2,2,128]{3,2,1,0:T(2,128)(2,1)} %param.17) | copy-start | bytes 196612
  0.7 12.8 %copy-start.9 = (bf16[64,864]{1,0:T(8,128)(2,1)S(1)}, bf16[64,864]{1,0:T(8,128)(2,1)}, u32[]{:S(2)}) copy-start(bf16[64,864]{1,0:T(8,128)(2,1)} %param.13) | copy-start | bytes 331780
  0.7 13.0 %copy-start.4 = (bf16[64,512]{1,0:T(8,128)(2,1)S(1)}, bf16[64,512]{1,0:T(8,128)(2,1)}, u32[]{:S(2)}) copy-start(bf16[64,512]{1,0:T(8,128)(2,1)} %rest_3_.1) | copy-start | bytes 196612
  2.7 25.1 %all-to-all-start = ((bf16[32,72,128]{2,1,0:T(8,128)(2,1)}), bf16[32,72,128]{2,1,0:T(8,128)(2,1)S(1)}, u32[]{:S(2)}, u32[]{:S(2)}) async-start(bf16[32,72,128]{2,1,0:T(8,128)(2,1)} %shard_map.136), calls=%async_computation | async-start | bytes 1179648 | tf_op jit(solution)/shard_map/all_to_all | solution.py:105
  10.1 21.9 %copy-start.2 = (f32[16,256]{1,0:T(8,128)}, f32[16,256]{1,0:T(8,128)S(1)}, u32[]{:S(2)}) copy-start(f32[16,256]{1,0:T(8,128)S(1)} %convert_element_type.12.act_ref) | copy-start | bytes 49156
  10.9 21.1 %copy-start.3 = (bf16[256,128]{1,0:T(8,128)(2,1)}, bf16[256,128]{1,0:T(8,128)(2,1)S(1)}, u32[]{:S(2)}) copy-start(bf16[256,128]{1,0:T(8,128)(2,1)S(1)} %get-tuple-element.83.grad_ref.rest_1_) | copy-start | bytes 196612
  11.0 5.5 %collective-permute-start = (bf16[144,128]{1,0:T(8,128)(2,1)S(1)}, bf16[144,128]{1,0:T(8,128)(2,1)S(1)}, u32[]{:S(2)}, u32[]{:S(2)}) collective-permute-start(bf16[144,128]{1,0:T(8,128)(2,1)S(1)} %get-tuple-element.75), channel_id=1, source_target_pairs={{0,8},{16,24},{8,0},{24,16},{1,9},{17,25},{9,1},{25,17},{2,10},{18... | collective-permute-start | bytes 110600 | tf_op jit(solution)/shard_map/ppermute | solution.py:86
  12.8 3.7 %collective-permute-start.1 = (bf16[144,128]{1,0:T(8,128)(2,1)S(1)}, bf16[144,128]{1,0:T(8,128)(2,1)S(1)}, u32[]{:S(2)}, u32[]{:S(2)}) collective-permute-start(bf16[144,128]{1,0:T(8,128)(2,1)S(1)} %get-tuple-element.76), channel_id=1, source_target_pairs={{8,16},{16,8},{9,17},{17,9},{10,18},{18,10},{11,19},{19,11},{12,20... | collective-permute-start | bytes 110600 | tf_op jit(solution)/shard_map/ppermute | solution.py:86
  14.5 4.8 %copy-start.12 = (f32[64]{0:T(128)S(1)}, f32[64]{0:T(128)}, u32[]{:S(2)}) copy-start(f32[64]{0:T(128)} %param.16) | copy-start | bytes 772
  14.5 4.8 %copy-start.13 = (f32[64]{0:T(128)S(1)}, f32[64]{0:T(128)}, u32[]{:S(2)}) copy-start(f32[64]{0:T(128)} %param.15) | copy-start | bytes 772
  17.1 5.3 %collective-permute-start.2 = (bf16[272,128]{1,0:T(8,128)(2,1)S(1)}, bf16[272,128]{1,0:T(8,128)(2,1)S(1)}, u32[]{:S(2)}, u32[]{:S(2)}) collective-permute-start(bf16[272,128]{1,0:T(8,128)(2,1)S(1)} %get-tuple-element.77), channel_id=1, source_target_pairs={{0,2},{4,6},{2,0},{6,4},{1,3},{5,7},{3,1},{7,5},{8,10},{12,14},{10... | collective-permute-start | bytes 208904 | tf_op jit(solution)/shard_map/ppermute | solution.py:86
  18.6 3.8 %collective-permute-start.3 = (bf16[272,128]{1,0:T(8,128)(2,1)S(1)}, bf16[272,128]{1,0:T(8,128)(2,1)S(1)}, u32[]{:S(2)}, u32[]{:S(2)}) collective-permute-start(bf16[272,128]{1,0:T(8,128)(2,1)S(1)} %get-tuple-element.78), channel_id=1, source_target_pairs={{2,4},{4,2},{3,5},{5,3},{10,12},{12,10},{11,13},{13,11},{18,20},{2... | collective-permute-start | bytes 208904 | tf_op jit(solution)/shard_map/ppermute | solution.py:86
  31.2 5.4 %collective-permute-start.4 = (bf16[256,256]{1,0:T(8,128)(2,1)S(1)}, bf16[256,256]{1,0:T(8,128)(2,1)S(1)}, u32[]{:S(2)}, u32[]{:S(2)}) collective-permute-start(bf16[256,256]{1,0:T(8,128)(2,1)S(1)} %get-tuple-element.81.first_ref), channel_id=1, source_target_pairs={{0,8},{16,24},{8,0},{24,16},{1,9},{17,25},{9,1},{25,17},{2,10},{18... | collective-permute-start | bytes 393224 | tf_op jit(solution)/shard_map/ppermute | solution.py:86
  31.3 5.3 %collective-permute-start.5 = (bf16[256,256]{1,0:T(8,128)(2,1)S(1)}, bf16[256,256]{1,0:T(8,128)(2,1)S(1)}, u32[]{:S(2)}, u32[]{:S(2)}) collective-permute-start(bf16[256,256]{1,0:T(8,128)(2,1)S(1)} %get-tuple-element.82.second_ref), channel_id=1, source_target_pairs={{8,16},{16,8},{9,17},{17,9},{10,18},{18,10},{11,19},{19,11},{12,20... | collective-permute-start | bytes 393224 | tf_op jit(solution)/shard_map/ppermute | solution.py:86
  37.2 7.3 %collective-permute-start.6 = (bf16[512,256]{1,0:T(8,128)(2,1)S(1)}, bf16[512,256]{1,0:T(8,128)(2,1)S(1)}, u32[]{:S(2)}, u32[]{:S(2)}) collective-permute-start(bf16[512,256]{1,0:T(8,128)(2,1)S(1)} %get-tuple-element.94), channel_id=1, source_target_pairs={{0,2},{4,6},{2,0},{6,4},{1,3},{5,7},{3,1},{7,5},{8,10},{12,14},{10... | collective-permute-start | bytes 786440 | tf_op jit(solution)/shard_map/ppermute | solution.py:86
  37.7 6.8 %collective-permute-start.7 = (bf16[512,256]{1,0:T(8,128)(2,1)S(1)}, bf16[512,256]{1,0:T(8,128)(2,1)S(1)}, u32[]{:S(2)}, u32[]{:S(2)}) collective-permute-start(bf16[512,256]{1,0:T(8,128)(2,1)S(1)} %get-tuple-element.95), channel_id=1, source_target_pairs={{2,4},{4,2},{3,5},{5,3},{10,12},{12,10},{11,13},{13,11},{18,20},{2... | collective-permute-start | bytes 786440 | tf_op jit(solution)/shard_map/ppermute | solution.py:86
  45.3 2.0 %collective-permute-start.8 = (bf16[2048,128]{1,0:T(8,128)(2,1)S(1)}, bf16[2048,128]{1,0:T(8,128)(2,1)S(1)}, u32[]{:S(2)}, u32[]{:S(2)}) collective-permute-start(bf16[2048,128]{1,0:T(8,128)(2,1)S(1)} %get-tuple-element.103), channel_id=1, source_target_pairs={{0,1},{1,0},{2,3},{3,2},{4,5},{5,4},{6,7},{7,6},{8,9},{9,8},{10,11... | collective-permute-start | bytes 1572872 | tf_op jit(solution)/shard_map/ppermute | solution.py:100
  45.4 1.9 %copy-start.1 = (f32[40,256]{1,0:T(8,128)S(1)}, f32[40,256]{1,0:T(8,128)}, u32[]{:S(2)}) copy-start(f32[40,256]{1,0:T(8,128)} %get-tuple-element.110.acts_ref) | copy-start | bytes 122884
  51.3 16.7 %all-to-all-start.1 = ((f32[32,8,128]{2,1,0:T(8,128)}), f32[32,8,128]{2,1,0:T(8,128)S(1)}, u32[]{:S(2)}, u32[]{:S(2)}) async-start(f32[32,8,128]{2,1,0:T(8,128)} %get-tuple-element.111), calls=%async_computation.1 | async-start | bytes 262144 | tf_op jit(solution)/shard_map/all_to_all | solution.py:105
  65.3 8.6 %copy-start.5 = (bf16[64,512]{1,0:T(8,128)(2,1)S(1)}, bf16[64,512]{1,0:T(8,128)(2,1)}, u32[]{:S(2)}) copy-start(bf16[64,512]{1,0:T(8,128)(2,1)} %rest_3_.1) | copy-start | bytes 196612
  68.1 5.9 %copy-start = (f32[32,8,128]{2,1,0:T(8,128)}, f32[32,8,128]{2,1,0:T(8,128)S(1)}, u32[]{:S(2)}) copy-start(f32[32,8,128]{2,1,0:T(8,128)S(1)} %all-to-all-done.1.stats_ref) | copy-start | bytes 393220
  71.0 11.2 %all-to-all-start.2 = ((f32[32,8,128]{2,1,0:T(8,128)}), f32[32,8,128]{2,1,0:T(8,128)S(1)}, u32[]{:S(2)}, u32[]{:S(2)}) async-start(f32[32,8,128]{2,1,0:T(8,128)} %get-tuple-element.123), calls=%async_computation.2 | async-start | bytes 262144 | tf_op jit(solution)/shard_map/all_to_all | solution.py:105
  78.0 0.6 copy-start.7
  87.0 0.7 copy-start.6
  87.0 3.3 %collective-permute-start.9 = (bf16[2304,128]{1,0:T(8,128)(2,1)}, bf16[2304,128]{1,0:T(8,128)(2,1)S(1)}, u32[]{:S(2)}, u32[]{:S(2)}) collective-permute-start(bf16[2304,128]{1,0:T(8,128)(2,1)} %get-tuple-element.133), channel_id=1, source_target_pairs={{0,1},{1,0},{2,3},{3,2},{4,5},{5,4},{6,7},{7,6},{8,9},{9,8},{10,11... | collective-permute-start | bytes 1769480 | tf_op jit(solution)/shard_map/ppermute | solution.py:100
  87.6 11.3 %all-to-all-start.3 = ((bf16[32,24,128]{2,1,0:T(8,128)(2,1)}), bf16[32,24,128]{2,1,0:T(8,128)(2,1)S(1)}, u32[]{:S(2)}, u32[]{:S(2)}) async-start(bf16[32,24,128]{2,1,0:T(8,128)(2,1)} %bitcast.30), calls=%async_computation.3 | async-start | bytes 393216 | tf_op jit(solution)/shard_map/all_to_all | solution.py:105
  96.7 6.8 %copy-start.8 = (bf16[4,64,128]{2,1,0:T(8,128)(2,1)S(1)}, bf16[4,64,128]{2,1,0:T(8,128)(2,1)}, u32[]{:S(2)}) copy-start(bf16[4,64,128]{2,1,0:T(8,128)(2,1)} %copy-done.7) | copy-start | bytes 196612
  99.9 24.1 %all-to-all-start.4 = ((bf16[32,88,128]{2,1,0:T(8,128)(2,1)}), bf16[32,88,128]{2,1,0:T(8,128)(2,1)S(1)}, u32[]{:S(2)}, u32[]{:S(2)}) async-start(bf16[32,88,128]{2,1,0:T(8,128)(2,1)} %shard_map.151), calls=%async_computation.4 | async-start | bytes 1441792 | tf_op jit(solution)/shard_map/all_to_all | solution.py:105
